TPU v7x, 256 devices: a whole 4x4x8 slice. The times are simulated.
256 devices in a mesh: ad: 32 (over x, z), tp: 8 (over y, core).
Axes of the slice: x: 4, y: 4, z: 8, core: 2. Of those that a mesh axis runs over, the one named last changes fastest.
Arguments:
- tokens: bfloat16 [49152, 8192], P('ad', 'tp'), may hold values from -6 to 6
- key_value_weight: bfloat16 [2, 8192, 1024], P(None, 'tp'), may hold values from -0.09375 to 0.09375
- adapter_down_weights: bfloat16 [128, 8192, 128], P('ad', 'tp'), may hold values from -0.0625 to 0.0625
- adapter_up_weights: bfloat16 [128, 2, 64, 1024], P('ad', None, None, 'tp'), may hold values from -0.75 to 0.75
- token_adapter_ident: int32 [49152, 1], P('ad'), may hold values from 0 to 127; in each aligned block of 1536 rows (0 to 1535, 1536 to 3071, ...) at most 18 rows name the same one
- adapter_storage_slot: int32 [128], replicated, may hold values from 0 to 127, each once
Outputs:
- projected: bfloat16 [49152, 2, 1024], P('ad', None, 'tp')
Inputs may be any that keep to these rules, and one draw needn't show every extreme that they name: `token_adapter_ident`: among the rows of one device no adapter id stands more than 18 times, and some id stands exactly 18 times. A permutation: adapter a is stored at position adapter_storage_slot[a] of adapter_down_weights and adapter_up_weights.
All inputs are finite; a program needn't handle non-finite values.
Results may differ from a plain program's by a relative error of at most 0.02.
Values may be sent and summed in bfloat16 or wider, within the bound.
No kernel may reach another device: no remote copies, remote signals or barrier semaphores. Data moves between devices by JAX's collectives and lax.ppermute only.
A program may use at most 128 MiB of HBM per device.

v0:
```python
import jax
import jax.numpy as jnp
from jax import lax
from jax.sharding import PartitionSpec as P


def return_rows(payload, owner_count, capacity):
    resident_count = payload.shape[0]
    column_count = payload.shape[3]
    shaped = payload.reshape(resident_count, owner_count, capacity, 2 * column_count)
    returned = lax.all_to_all(shaped, "ad", split_axis=1, concat_axis=1, tiled=True)
    return returned.reshape(resident_count * owner_count * capacity, 2, column_count)


def body(
    tokens,
    key_value_weight,
    adapter_down_weights,
    adapter_up_weights,
    token_adapter_ident,
    adapter_storage_slot,
):
    owner_count = lax.axis_size("ad")
    resident_count = adapter_down_weights.shape[0]
    adapter_count = adapter_storage_slot.shape[0]
    tok_rows = tokens.shape[0]
    feature_count = tokens.shape[1]
    capacity = 3 * tok_rows // (2 * adapter_count)
    adapter_ids = token_adapter_ident[:, 0]
    catalog = jnp.arange(adapter_count, dtype=jnp.int32)
    placed = jnp.sum(
        jnp.where(adapter_ids[:, None] == catalog[None, :], adapter_storage_slot[None, :], 0),
        axis=1,
    )
    position = jnp.arange(tok_rows, dtype=jnp.int32)
    earlier = (adapter_ids[:, None] == adapter_ids[None, :]) & (
        position[None, :] < position[:, None]
    )
    ordinal = jnp.sum(earlier.astype(jnp.int32), axis=1)
    slot_index = placed * capacity + ordinal
    outgoing = (
        jnp.zeros((adapter_count * capacity, feature_count), tokens.dtype)
        .at[slot_index]
        .set(tokens)
    )
    outgoing = outgoing.reshape(owner_count, resident_count, capacity, feature_count)
    received_rows = lax.all_to_all(outgoing, "ad", split_axis=0, concat_axis=2, tiled=True)[0]
    reduced_rows = jnp.einsum(
        "ouj,ojv->ouv", received_rows, adapter_down_weights, preferred_element_type=jnp.float32
    )
    shrunk = lax.psum(reduced_rows.astype(jnp.bfloat16), "tp")
    rank_extent = adapter_up_weights.shape[2]
    matched_rows = shrunk.reshape(resident_count, shrunk.shape[1], 2, rank_extent)
    lowrank_delta = jnp.einsum(
        "zwum,zumh->zwuh", matched_rows, adapter_up_weights, preferred_element_type=jnp.float32
    ).astype(jnp.bfloat16)
    home_index = (
        placed % resident_count * owner_count + placed // resident_count
    ) * capacity + ordinal
    partial_value = jnp.einsum(
        "tf,cfk->tck", tokens, key_value_weight, preferred_element_type=jnp.float32
    )
    base_out = lax.psum_scatter(
        partial_value.astype(jnp.bfloat16), "tp", scatter_dimension=2, tiled=True
    ).astype(jnp.float32)
    returned = return_rows(lowrank_delta, owner_count, capacity)
    picked = returned[home_index]
    return (base_out + picked.astype(jnp.float32)).astype(jnp.bfloat16)


def solution(mesh):
    return jax.shard_map(
        body,
        mesh=mesh,
        in_specs=(
            P("ad", "tp"),
            P(None, "tp", None),
            P("ad", "tp", None),
            P("ad", None, None, "tp"),
            P("ad", None),
            P(),
        ),
        out_specs=P("ad", None, "tp"),
        check_vma=False,
    )
```

profile of v0, /device:TPU:64, one launch (start us, length us, event | category | flops | bytes accessed | tf_op | source)
XLA Modules:
  0.0 287.8 jit_solution(2440930863436351990)
XLA Ops:
  6.5 0.8 reduce
  7.3 2.7 convert_reduce_fusion
  10.0 1.2 select_reduce_fusion
  11.3 11.2 %scatter_custom_fusion = bf16[2304,1024]{1,0:T(8,128)(2,1)} fusion(s32[1536]{0:T(1024)S(1)} %get-tuple-element.6, bf16[1536,1024]{1,0:T(8,128)(2,1)} %param.6, bf16[]{:T(256)} %constant.28.clone.1), kind=kCustom, calls=%fused_computation.9 | custom fusion | bytes 4719104 | tf_op jit(solution)/shard_map/scatter | solution.py:44
  22.5 7.6 %reshape.131 = bf16[32,4,18,1024]{3,2,1,0:T(8,128)(2,1)} reshape(bf16[2304,1024]{1,0:T(8,128)(2,1)} %scatter_custom_fusion) | data formatting | bytes 9437184 | tf_op jit(solution)/shard_map/reshape | solution.py:46
  30.0 7.2 %copy.28 = bf16[32,4,18,1024]{3,1,2,0:T(4,128)(2,1)S(1)} copy(bf16[32,4,18,1024]{3,2,1,0:T(8,128)(2,1)} %reshape.131) | data formatting | bytes 9437184 | tf_op jit(solution)/shard_map/reshape | solution.py:46
  37.2 116.9 %all_to_all.20 = bf16[32,4,18,1024]{3,1,2,0:T(4,128)(2,1)S(1)} all-to-all(bf16[32,4,18,1024]{3,1,2,0:T(4,128)(2,1)S(1)} %copy.28), channel_id=1, replica_groups=mesh['ad'=32,'tp'=8] {'ad'}, dimensions={0} | all-to-all | bytes 9437184 | tf_op jit(solution)/shard_map/all_to_all | solution.py:47
  154.1 1.5 fusion.7
  155.6 1.1 copy.30
  156.8 11.2 %convolution_convert_fusion = bf16[1536,2,1024]{2,0,1:T(8,128)(2,1)} fusion(bf16[2,1024,1024]{2,1,0:T(8,128)(2,1)} %param.7, bf16[1536,1024]{1,0:T(8,128)(2,1)} %param.6), kind=kOutput, calls=%fused_computation.5 | convolution fusion | flops 6445596672 | bytes 13631488 | tf_op jit(solution)/shard_map/tf,cfk->tck/dot_general | solution.py:60
  168.0 16.5 %copy.35 = bf16[1536,2,1024]{0,1,2:T(2,128)(2,1)} copy(bf16[1536,2,1024]{2,0,1:T(8,128)(2,1)} %convolution_convert_fusion) | data formatting | bytes 12582912
  184.5 7.1 %copy.37 = bf16[128,8,2,1536]{3,1,2,0:T(8,128)(2,1)} copy(bf16[128,8,2,1536]{3,2,1,0:T(2,128)(2,1)} %bitcast.23) | data formatting | bytes 12582912
  191.6 29.3 %all-reduce.2.cloned.1.call-done = bf16[4,576,2,64]{1,3,2,0:T(8,128)(2,1)} async-done(((bf16[4,576,2,64]{1,3,2,0:T(8,128)(2,1)}), bf16[4,576,2,64]{1,3,2,0:T(8,128)(2,1)}) %all-reduce.2.cloned.1.call-update) | async-done | bytes 589840 | tf_op jit(solution)/shard_map/psum | solution.py:51
  220.8 1.6 fusion.6
  222.5 1.2 copy.31
  223.7 1.6 reshape.133
  225.4 10.0 %all-to-all-start.1 = ((bf16[4,32,18,256]{3,0,2,1:T(4,128)(2,1)}), bf16[4,32,18,256]{3,0,2,1:T(4,128)(2,1)}, u32[]{:S(2)}, u32[]{:S(2)}) async-start(bf16[4,32,18,256]{3,0,2,1:T(4,128)(2,1)} %reshape.133), calls=%async_computation.1 | async-start | bytes 2359296 | tf_op jit(solution)/shard_map/all_to_all | solution.py:11
  235.4 27.6 %all-to-all-done.1 = bf16[4,32,18,256]{3,0,2,1:T(4,128)(2,1)} async-done(((bf16[4,32,18,256]{3,0,2,1:T(4,128)(2,1)}), bf16[4,32,18,256]{3,0,2,1:T(4,128)(2,1)}, u32[]{:S(2)}, u32[]{:S(2)}) %all-to-all-start.1) | async-done | bytes 1179680 | tf_op jit(solution)/shard_map/all_to_all | solution.py:11
  263.0 1.5 copy.32
  264.5 1.4 reshape.134
  265.9 4.3 %gather_fusion = bf16[1536,2,128]{2,1,0:T(2,128)(2,1)S(1)} fusion(bf16[2304,2,128]{2,1,0:T(2,128)(2,1)} %reshape.134, s32[2048]{0:T(1024)S(1)} %pad_clamp_fusion), kind=kCustom, calls=%fused_computation | custom fusion | bytes 1579008 | tf_op jit(solution)/shard_map/gather | solution.py:67
  270.2 2.6 reshape.153
  272.8 0.8 copy.36
  273.7 7.3 %copy.34 = bf16[1536,2,128]{2,1,0:T(2,128)(2,1)} copy(bf16[1536,2,128]{2,0,1:T(8,128)(2,1)S(1)} %add_convert_fusion) | data formatting | bytes 1572864 | tf_op jit(solution)/shard_map/convert_element_type | solution.py:68
  (12 shorter events, 0.4 us)
Async XLA Ops:
  6.5 147.6 %copy-start = (bf16[4,1024,128]{2,1,0:T(8,128)(2,1)S(1)}, bf16[4,1024,128]{2,1,0:T(8,128)(2,1)}, u32[]{:S(2)}) copy-start(bf16[4,1024,128]{2,1,0:T(8,128)(2,1)} %param.8) | copy-start | bytes 3145732
  6.5 214.3 %all-reduce.2.cloned.1.call-start = ((), (), s32[]{:S(2)}) async-start(), calls=%async_computation.3 | async-start | bytes 1310720 | tf_op jit(solution)/shard_map/psum | solution.py:51
  156.7 113.5 %reduce-scatter.4.cloned.1.call-start = ((), (), s32[]{:S(2)}) async-start(), calls=%async_computation.4 | async-start | bytes 7077888
  191.5 29.3 %copy-start.1 = (bf16[4,2,64,128]{3,2,1,0:T(8,128)(2,1)S(1)}, bf16[4,2,64,128]{3,2,1,0:T(8,128)(2,1)}, u32[]{:S(2)}) copy-start(bf16[4,2,64,128]{3,2,1,0:T(8,128)(2,1)} %param.9) | copy-start | bytes 393220
  225.4 37.6 %all-to-all-start.1 = ((bf16[4,32,18,256]{3,0,2,1:T(4,128)(2,1)}), bf16[4,32,18,256]{3,0,2,1:T(4,128)(2,1)}, u32[]{:S(2)}, u32[]{:S(2)}) async-start(bf16[4,32,18,256]{3,0,2,1:T(4,128)(2,1)} %reshape.133), calls=%async_computation.1 | async-start | bytes 2359296 | tf_op jit(solution)/shard_map/all_to_all | solution.py:11
Sparse Core Ops, SparseCore 0:
  156.8 63.9 all-reduce.1
  223.4 44.7 reduce-scatter.3
where the time goes:
time: 291 us; the launch traced here: 288 us
  blocking collectives  117 us (40%)
  local copies, waits for them, and re-layouts  71.2 us (24%)
  waiting for transfers between devices  56.9 us (20%)
  matrix products  14.4 us (5%)
  between operations  13.5 us (5%)
  starting transfers between devices  10.1 us (3%)
  other arithmetic  4.88 us (2%)
    all_to_all x1, blocking collectives, body(): lax.all_to_all(outgoing, 'ad', split_axis=0, concat_axis=2, tiled=True)[0]  117 us
    psum x1, waiting for transfers between devices, body(): shrunk = lax.psum(reduced_rows.astype(jnp.bfloat16), 'tp')  29.3 us
    all_to_all x1, waiting for transfers between devices, return_rows(): lax.all_to_all(shaped, 'ad', split_axis=1, concat_axis=1, tiled=True)  27.6 us
    unnamed x8, local copies, waits for them, and re-layouts  26.9 us
    reshape x2, local copies, waits for them, and re-layouts, body(): outgoing.reshape(owner_count, resident_count, capacity, feature_count)  14.8 us
    dot_general x1, matrix products, body(): jnp.einsum('tf,cfk->tck', tokens, key_value_weight, preferred_element_typ...  11.2 us
    scatter x1, local copies, waits for them, and re-layouts, body(): outgoing = jnp.zeros((adapter_count * capacity, feature_count), tokens.dt...  11.2 us
    all_to_all x1, starting transfers between devices, return_rows(): lax.all_to_all(shaped, 'ad', split_axis=1, concat_axis=1, tiled=True)  10 us
  transfers between devices with their start and end apart: 3, of which 2 were waited for; matrix products, arithmetic and copies ran while one was open for 16% of the time, Pallas kernels for 0%

commit v1 on v0

v1 whole, which is shorter than its diff:
```python
import functools

import jax
import jax.numpy as jnp
from jax import lax
from jax.experimental import pallas as pl
from jax.experimental.pallas import tpu as pltpu
from jax.sharding import PartitionSpec as P

F32 = jnp.float32
BF16 = jnp.bfloat16
I32 = jnp.int32

NX, NZ = 4, 8
NY = 4
LOCAL = 4
CAP = 18
BLOCK = LOCAL * CAP
WIDE = 80

ORDER = (0, 7, 1, 6, 2, 5, 3, 4)
CHUNKS = ((0, 368, (0, 7, 1, 6, 2)), (368, 144, (5, 3)), (512, 80, (4,)))
ROWS = 592
COST = {
    "route": 3, "pack": 11, "base": 11, "gather": 7, "finish": 6,
    "shrink": (20, 4, 40), "expand": (20, 3, 30),
}
VMEM = 56 * 1024 * 1024


def iota(shape, dim):
    return lax.broadcasted_iota(I32, shape, dim)


def params(*semantics):
    if semantics:
        return pltpu.CompilerParams(vmem_limit_bytes=VMEM, dimension_semantics=semantics)
    return pltpu.CompilerParams(vmem_limit_bytes=VMEM)


def cost(micros):
    return pl.CostEstimate(
        flops=int(micros * 1.1e9), bytes_accessed=1000, transcendentals=0
    )


def whole():
    return pl.BlockSpec(memory_space=pltpu.VMEM)


def scalars():
    return pl.BlockSpec(memory_space=pltpu.SMEM)


def route_kernel(place_ref, ids_ref, store_ref, row_ref, col_ref):
    x, z = place_ref[0], place_ref[1]
    count = ids_ref.shape[1]
    ids = jnp.broadcast_to(ids_ref[...], (128, count))
    ids_down = ids.T
    store = jnp.broadcast_to(store_ref[...], (128, 128)).T
    for j in range(count // 128):
        mine = ids[:, j * 128 : (j + 1) * 128]
        placed = jnp.sum(
            jnp.where(mine == iota((128, 128), 0), store, 0), axis=0, keepdims=True
        )
        seen = (j + 1) * 128
        same = (ids_down[:seen] == mine[:1]) & (
            iota((seen, 128), 0) < iota((seen, 128), 1) + j * 128
        )
        ordinal = jnp.sum(same.astype(I32), axis=0, keepdims=True)
        owner = placed >> 2
        east = ((owner >> 3) - x) & 3
        north = ((owner & 7) - z) & 7
        start = jnp.zeros_like(owner)
        for first, _, blocks in CHUNKS:
            for k, offset in enumerate(blocks):
                start = jnp.where(north == offset, first + k * BLOCK, start)
        row_ref[:, j * 128 : (j + 1) * 128] = (
            east * ROWS + start + (placed & 3) * CAP + ordinal
        )
    col_ref[...] = jnp.broadcast_to(row_ref[...], (128, count)).T


def route(place, ids, store):
    count = ids.shape[1]
    return pl.pallas_call(
        route_kernel,
        out_shape=(
            jax.ShapeDtypeStruct((1, count), I32),
            jax.ShapeDtypeStruct((count, 128), I32),
        ),
        in_specs=[scalars(), whole(), whole()],
        out_specs=(whole(), whole()),
        compiler_params=params(),
        cost_estimate=cost(COST['route']),
        name="route",
    )(place, ids, store)


def pack_kernel(row_ref, tok_ref, *refs):
    outs, hot = refs[:NX], refs[NX]

    @pl.when(pl.program_id(0) == 0)
    def _():
        count = row_ref.shape[1]
        rows = row_ref[...]
        for e in range(NX):
            hot[e] = (rows == iota((ROWS, count), 0) + e * ROWS).astype(BF16)

    for e in range(NX):
        outs[e][...] = jnp.dot(
            hot[e], tok_ref[...], preferred_element_type=F32
        ).astype(BF16)


def pack(row, tokens):
    count, width = tokens.shape
    step = 256
    return pl.pallas_call(
        pack_kernel,
        grid=(width // step,),
        out_shape=[jax.ShapeDtypeStruct((ROWS, width), BF16)] * NX,
        in_specs=[
            pl.BlockSpec((1, count), lambda i: (0, 0)),
            pl.BlockSpec((count, step), lambda i: (0, i)),
        ],
        out_specs=[pl.BlockSpec((ROWS, step), lambda i: (0, i))] * NX,
        scratch_shapes=[pltpu.VMEM((NX, ROWS, count), BF16)],
        compiler_params=params("arbitrary"),
        cost_estimate=cost(COST['pack']),
        name="pack",
    )(row, tokens)


def base_kernel(tok_ref, w_ref, _, out_ref):
    parts = out_ref.shape[0]
    for c in range(2):
        y = jnp.dot(tok_ref[...], w_ref[c], preferred_element_type=F32).astype(BF16)
        for p in range(parts):
            out_ref[p, :, c * 128 : (c + 1) * 128] = y[:, p * 128 : (p + 1) * 128]


def base(tokens, weight, parts, earlier):
    count, width = tokens.shape
    out_width = weight.shape[2]
    step = 256
    return pl.pallas_call(
        base_kernel,
        grid=(count // step,),
        out_shape=jax.ShapeDtypeStruct((parts, count, 256), BF16),
        in_specs=[
            pl.BlockSpec((step, width), lambda i: (i, 0)),
            pl.BlockSpec(weight.shape, lambda i: (0, 0, 0)),
            pl.BlockSpec(memory_space=pl.ANY),
        ],
        out_specs=pl.BlockSpec((parts, step, 256), lambda i: (0, i, 0)),
        compiler_params=params("arbitrary"),
        cost_estimate=cost(COST['base']),
        name="base",
    )(tokens, weight, earlier)


def spans(blocks):
    for k in range(len(blocks)):
        low = k * BLOCK // 16 * 16
        yield k, low


def adapter_of(k, low):
    row = iota((WIDE, 1), 0) + (low - k * BLOCK)
    which = jnp.full((WIDE, 1), -1, I32)
    for a in range(LOCAL):
        which = jnp.where((row >= a * CAP) & (row < (a + 1) * CAP), a, which)
    return jnp.concatenate([which] * NX, axis=0)


def shrink_kernel(blocks, pieces, *refs):
    xs, ws = refs[:NX], refs[NX : NX + len(pieces)]
    out_ref, total = refs[-2], refs[-1]
    total[...] = jnp.zeros_like(total)
    for k, low in spans(blocks):
        panels = [
            w[a] for w, (block, n) in zip(ws, pieces, strict=True) if block == k for a in range(n)
        ]
        rows = jnp.concatenate([x[low : low + WIDE, :] for x in xs], axis=0)
        y = jnp.dot(rows, jnp.concatenate(panels, axis=1), preferred_element_type=F32)
        which = adapter_of(k, low)
        kept = jnp.zeros((NX * WIDE, 128), F32)
        for a in range(LOCAL):
            kept = kept + jnp.where(which == a, y[:, a * 128 : (a + 1) * 128], 0.0)
        for e in range(NX):
            total[e, low : low + WIDE, :] += kept[e * WIDE : (e + 1) * WIDE]
    out_ref[...] = total[...].astype(BF16)


def shrink(chunk, xs, panels):
    first, size, blocks = chunk
    pieces = tuple((k, w.shape[0]) for k, w in panels)
    width = xs[0].shape[1]
    return pl.pallas_call(
        functools.partial(shrink_kernel, blocks, pieces),
        grid=(1,),
        out_shape=jax.ShapeDtypeStruct((NX, size, 128), BF16),
        in_specs=[
            pl.BlockSpec((pl.Element(size), pl.Element(width)), lambda i: (first, 0))
        ] * NX
        + [pl.BlockSpec(w.shape, lambda i: (0, 0, 0)) for _, w in panels],
        out_specs=pl.BlockSpec((NX, size, 128), lambda i: (0, 0, 0)),
        scratch_shapes=[pltpu.VMEM((NX, size, 128), F32)],
        compiler_params=params("arbitrary"),
        cost_estimate=cost(COST['shrink'][CHUNKS.index(chunk)]),
        name="shrink",
    )(*xs, *[w for _, w in panels])


def expand_kernel(blocks, place_ref, *refs):
    parts, up_ref, outs = refs[:NY], refs[NY], refs[NY + 1 : NY + 1 + NX]
    wide_up, total = refs[-2], refs[-1]
    z = place_ref[1]
    shrunk = parts[0][...].astype(F32)
    for part in parts[1:]:
        shrunk = shrunk + part[...].astype(F32)
    shrunk = shrunk.astype(BF16)
    wide_up[...] = jnp.zeros_like(wide_up)
    total[...] = jnp.zeros_like(total)
    for k, low in spans(blocks):
        owner = ((z + blocks[k]) & (NZ - 1)) * LOCAL
        for a in range(LOCAL):
            for c in range(2):
                wide_up[a * 128 + c * 64 : a * 128 + c * 64 + 64, c * 128 : (c + 1) * 128] = (
                    up_ref[owner + a, c]
                )
        rows = jnp.concatenate([shrunk[e, low : low + WIDE] for e in range(NX)], axis=0)
        which = adapter_of(k, low)
        lhs = jnp.concatenate(
            [jnp.where(which == a, rows, jnp.zeros_like(rows)) for a in range(LOCAL)], axis=1
        )
        y = jnp.dot(lhs, wide_up[...], preferred_element_type=F32)
        for e in range(NX):
            total[e, low : low + WIDE, :] += y[e * WIDE : (e + 1) * WIDE]
    for e in range(NX):
        outs[e][...] = total[e].astype(BF16)


def expand(chunk, place, parts, up):
    _, size, blocks = chunk
    return pl.pallas_call(
        functools.partial(expand_kernel, blocks),
        out_shape=[jax.ShapeDtypeStruct((size, 256), BF16)] * NX,
        in_specs=[scalars()] + [whole()] * (NY + 1),
        out_specs=[whole()] * NX,
        scratch_shapes=[pltpu.VMEM((LOCAL * 128, 256), BF16), pltpu.VMEM((NX, size, 256), F32)],
        compiler_params=params(),
        cost_estimate=cost(COST['expand'][CHUNKS.index(chunk)]),
        name="expand",
    )(place, *parts, up)


def picked(slot, chunk, deltas):
    first, size, _ = chunk
    total = jnp.zeros((slot.shape[0], 256), F32)
    for e in range(NX):
        hot = (slot == iota((slot.shape[0], size), 1) + (e * ROWS + first)).astype(BF16)
        total = total + jnp.dot(hot, deltas[e][...], preferred_element_type=F32)
    return total


def gather_kernel(chunks, col_ref, base_ref, *refs):
    slot = col_ref[:, :1]
    total = base_ref[...].astype(F32)
    for n, chunk in enumerate(chunks):
        total = total + picked(slot, chunk, refs[n * NX : (n + 1) * NX])
    refs[-1][...] = total


def gather(chunks, col, summed, deltas):
    count = col.shape[0]
    step = 256
    return pl.pallas_call(
        functools.partial(gather_kernel, chunks),
        grid=(count // step,),
        out_shape=jax.ShapeDtypeStruct((count, 256), F32),
        in_specs=[
            pl.BlockSpec((step, 128), lambda i: (i, 0)),
            pl.BlockSpec((step, 256), lambda i: (i, 0)),
        ]
        + [pl.BlockSpec(d.shape, lambda i: (0, 0)) for d in deltas],
        out_specs=pl.BlockSpec((step, 256), lambda i: (i, 0)),
        compiler_params=params("arbitrary"),
        cost_estimate=cost(COST['gather']),
        name="gather",
    )(col, summed, *deltas)


def finish_kernel(chunk, col_ref, total_ref, *refs):
    out_ref, both = refs[-2], refs[-1]
    rows = col_ref.shape[0]
    total = total_ref[...] + picked(col_ref[:, :1], chunk, refs[:NX])
    both[pl.ds(0, rows, stride=2), :] = total[:, :128]
    both[pl.ds(1, rows, stride=2), :] = total[:, 128:]
    out_ref[...] = both[...].astype(BF16)


def finish(chunk, col, total, deltas):
    count = col.shape[0]
    step = 256
    return pl.pallas_call(
        functools.partial(finish_kernel, chunk),
        grid=(count // step,),
        out_shape=jax.ShapeDtypeStruct((2 * count, 128), BF16),
        in_specs=[
            pl.BlockSpec((step, 128), lambda i: (i, 0)),
            pl.BlockSpec((step, 256), lambda i: (i, 0)),
        ]
        + [pl.BlockSpec(d.shape, lambda i: (0, 0)) for d in deltas],
        out_specs=pl.BlockSpec((2 * step, 128), lambda i: (i, 0)),
        scratch_shapes=[pltpu.VMEM((2 * step, 128), F32)],
        compiler_params=params("arbitrary"),
        cost_estimate=cost(COST['finish']),
        name="finish",
    )(col, total, *deltas)


def along_z(array, d):
    pairs = [(x * NZ + z, x * NZ + (z + d) % NZ) for x in range(NX) for z in range(NZ)]
    return lax.ppermute(array, "ad", pairs)


def along_x(array, d):
    pairs = [(x * NZ + z, (x + d) % NX * NZ + z) for x in range(NX) for z in range(NZ)]
    return lax.ppermute(array, "ad", pairs)


def along_y(array, d):
    pairs = [(y * 2 + c, (y + d) % NY * 2 + c) for y in range(NY) for c in range(2)]
    return lax.ppermute(array, "tp", pairs)


def other_core(array):
    return lax.ppermute(array, "tp", [(i, i ^ 1) for i in range(2 * NY)])


def adapter_rows(chunk, place, xs, panels, up):
    partial = shrink(chunk, xs, panels)
    chip = (partial.astype(F32) + other_core(partial).astype(F32)).astype(BF16)
    parts = [chip] + [along_y(chip, d) for d in (2, 1, 3)]
    deltas = expand(chunk, place, parts, up)
    return [deltas[0]] + [along_x(deltas[e], -e) for e in (1, 2, 3)]


def after(value, *others):
    return lax.optimization_barrier((value, *others))[0]


def body(tokens, weight, down, up, ident, store):
    index = lax.axis_index("ad")
    place = jnp.stack([index >> 3, index & 7]).astype(I32)
    groups = [[x * NZ + z for z in range(NZ)] for x in range(NX)]

    cw1, ccw1 = along_z(down, 1), along_z(down, -1)
    row, col = route(place, ident.reshape(1, -1), store.reshape(1, -1))
    packed = pack(row, tokens)
    xs = [packed[0]] + [along_x(packed[e], e) for e in (1, 2, 3)]
    ups = lax.all_gather(up, "ad", axis_index_groups=groups, tiled=True)

    partial_base = base(tokens, weight, lax.axis_size("tp"), packed[1])
    summed = lax.psum_scatter(partial_base, "tp", scatter_dimension=0, tiled=True)[0]
    cw2, ccw2 = along_z(cw1, 1), along_z(ccw1, -1)
    cw3, ccw3 = along_z(cw2, 1), along_z(ccw2, -1)
    last = (along_z(cw3[:2], 1), along_z(ccw3[2:], -1))

    a = adapter_rows(
        CHUNKS[0], place, xs, [(0, down), (1, cw1), (2, ccw1), (3, cw2), (4, ccw2)], ups
    )
    b = adapter_rows(CHUNKS[1], place, xs, [(0, cw3), (1, ccw3)], ups)
    c = adapter_rows(CHUNKS[2], place, xs, [(0, last[0]), (0, last[1])], ups)
    total = gather(CHUNKS[:2], col, summed, a + b)
    out = finish(CHUNKS[2], col, total, c)
    return out.reshape(tokens.shape[0], 2, 128)


def solution(mesh):
    return jax.shard_map(
        body,
        mesh=mesh,
        in_specs=(
            P("ad", "tp"),
            P(None, "tp", None),
            P("ad", "tp", None),
            P("ad", None, None, "tp"),
            P("ad", None),
            P(),
        ),
        out_specs=P("ad", None, "tp"),
        check_vma=False,
    )
```

time: 291 us -> 183 us (0.63)
  blocking collectives: 117 us -> 0 us
  local copies, waits for them, and re-layouts: 71.2 us -> 1.97 us
  Pallas kernels: 0 us -> 58.9 us
  starting transfers between devices: 10.1 us -> 49.1 us
  matrix products: 14.4 us -> 0 us
  waiting for transfers between devices: 56.9 us -> 52.3 us
    all_to_all x1 -> x0, blocking collectives: 117 us -> none  [body(): lax.all_to_all(outgoing, 'ad', split_axis=0, concat_axis=2, tiled=True)[0]]
    pallas_call x0 -> x11, Pallas kernels: none -> 58.9 us  [the longest x3 12.2 us: shrink(): pl.pallas_call(functools.partial(shrink_kernel, blocks, pieces), grid=(1,...]
    ppermute x0 -> x32, waiting for transfers between devices: none -> 52.2 us  [the longest x8 20.8 us: along_z(): return lax.ppermute(array, 'ad', pairs)]
    ppermute x0 -> x32, starting transfers between devices: none -> 49.1 us  [the longest x9 18.5 us: along_y(): return lax.ppermute(array, 'tp', pairs)]
    psum x1 -> x0, waiting for transfers between devices: 29.3 us -> none  [body(): shrunk = lax.psum(reduced_rows.astype(jnp.bfloat16), 'tp')]
    all_to_all x1 -> x0, waiting for transfers between devices: 27.6 us -> none  [return_rows(): lax.all_to_all(shaped, 'ad', split_axis=1, concat_axis=1, tiled=True)]
    unnamed x8 -> x50, local copies, waits for them, and re-layouts: 26.9 us -> 1.9 us
    reshape x4 -> x0, local copies, waits for them, and re-layouts: 17.8 us -> none  [the longest x2 14.8 us: body(): outgoing.reshape(owner_count, resident_count, capacity, feature_count)]
  transfers between devices with their start and end apart: 3 -> 34, of which waited for: 2 -> 9; matrix products, arithmetic and copies ran while one was open for 16% -> 2% of each run, Pallas kernels for 0% -> 30%
where the time goes in v1:
time: 183 us; the launch traced here: 180 us
  Pallas kernels  58.9 us (32%)
  waiting for transfers between devices  52.3 us (29%)
  starting transfers between devices  49.1 us (27%)
  between operations  15.1 us (8%)
  other arithmetic  2.63 us (1%)
  local copies, waits for them, and re-layouts  1.97 us (1%)
    ppermute x8, waiting for transfers between devices, along_z(): return lax.ppermute(array, 'ad', pairs)  20.8 us
    ppermute x9, starting transfers between devices, along_y(): return lax.ppermute(array, 'tp', pairs)  18.5 us
    ppermute x9, waiting for transfers between devices, along_y(): return lax.ppermute(array, 'tp', pairs)  18.2 us
    ppermute x12, starting transfers between devices, along_x(): return lax.ppermute(array, 'ad', pairs)  17.7 us
    ppermute x8, starting transfers between devices, along_z(): return lax.ppermute(array, 'ad', pairs)  12.4 us
    pallas_call x3, Pallas kernels, shrink(): pl.pallas_call(functools.partial(shrink_kernel, blocks, pieces), grid=(1,...  12.2 us
    pallas_call x1, Pallas kernels, base(): pl.pallas_call(base_kernel, grid=(count // step,), out_shape=jax.ShapeDty...  11.7 us
    pallas_call x1, Pallas kernels, pack(): pl.pallas_call(pack_kernel, grid=(width // step,), out_shape=[jax.ShapeDt...  11.5 us
  transfers between devices with their start and end apart: 34, of which 9 were waited for; matrix products, arithmetic and copies ran while one was open for 2% of the time, Pallas kernels for 30%

profile of v1, /device:TPU:64, one launch (start us, length us, event | category | flops | bytes accessed | tf_op | source)
XLA Modules:
  0.0 180.0 jit_solution(9979040004977011011)
XLA Ops:
  10.1 2.6 %route.1 = (s32[1,1536]{1,0:T(1,128)}, s32[1536,128]{1,0:T(8,128)}) custom-call(s32[2]{0:T(128)} %pad_add_fusion.place_ref, s32[1,1536]{1,0:T(1,128)} %bitcast.7, s32[1,128]{1,0:T(1,128)} %bitcast.8), custom_call_target="tpu_custom_call" | custom-call | flops 3300000000 | bytes 1000 | tf_op jit(solution)/shard_map/route/pallas_call | solution.py:86
  12.7 11.5 %pack.1 = (bf16[592,1024]{1,0:T(8,128)(2,1)}, bf16[592,1024]{1,0:T(8,128)(2,1)}, bf16[592,1024]{1,0:T(8,128)(2,1)}, bf16[592,1024]{1,0:T(8,128)(2,1)}) custom-call(s32[1,1536]{1,0:T(1,128)} %get-tuple-element.24.row_ref, bf16[1536,1024]{1,0:T(8,128)(2,1)} %tok_ref.3), custom_call_target="tpu_custom_call" | custom-call | flops 12099999744 | bytes 1000 | tf_op jit(solution)/shard_map/pack/pallas_call | solution.py:119
  25.7 2.7 %collective-permute-start.1 = (bf16[592,1024]{1,0:T(8,128)(2,1)}, bf16[592,1024]{1,0:T(8,128)(2,1)}, u32[]{:S(2)}, u32[]{:S(2)}) collective-permute-start(bf16[592,1024]{1,0:T(8,128)(2,1)} %get-tuple-element.27), channel_id=1, source_target_pairs={{0,128},{8,136},{16,144},{24,152},{32,160},{40,168},{48,176},{56,1... | collective-permute-start | bytes 3637256 | tf_op jit(solution)/shard_map/ppermute | solution.py:331
  29.9 7.2 %collective-permute-done.3.refs_5_ = bf16[4,1024,128]{2,1,0:T(8,128)(2,1)S(1)} collective-permute-done((bf16[4,1024,128]{2,1,0:T(8,128)(2,1)}, bf16[4,1024,128]{2,1,0:T(8,128)(2,1)S(1)}, u32[]{:S(2)}, u32[]{:S(2)}) %collective-permute-start.3) | collective-permute-done | bytes 1048608 | tf_op jit(solution)/shard_map/ppermute | solution.py:326
  37.0 4.5 %collective-permute-start.5 = (bf16[4,1024,128]{2,1,0:T(8,128)(2,1)S(1)}, bf16[4,1024,128]{2,1,0:T(8,128)(2,1)}, u32[]{:S(2)}, u32[]{:S(2)}) collective-permute-start(bf16[4,1024,128]{2,1,0:T(8,128)(2,1)S(1)} %collective-permute-done.3.refs_5_), channel_id=1, source_target_pairs={{0,8},{8,16},{16,24},{24,32},{32,40},{40,48},{48,56},{56,0},{64,72... | collective-permute-start | bytes 3145736 | tf_op jit(solution)/shard_map/ppermute | solution.py:326
  41.5 11.7 %base.1 = bf16[8,1536,256]{2,1,0:T(8,128)(2,1)} custom-call(bf16[1536,1024]{1,0:T(8,128)(2,1)} %tok_ref.3, bf16[2,1024,1024]{2,1,0:T(8,128)(2,1)} %w_ref.1, bf16[592,1024]{1,0:T(8,128)(2,1)} %get-tuple-element.25._), custom_call_target="tpu_custom_call" | custom-call | flops 12099999744 | bytes 1000 | tf_op jit(solution)/shard_map/base/pallas_call | solution.py:147
  53.2 12.5 %collective-permute-done.5.refs_7_ = bf16[4,1024,128]{2,1,0:T(8,128)(2,1)} collective-permute-done((bf16[4,1024,128]{2,1,0:T(8,128)(2,1)S(1)}, bf16[4,1024,128]{2,1,0:T(8,128)(2,1)}, u32[]{:S(2)}, u32[]{:S(2)}) %collective-permute-start.5) | collective-permute-done | bytes 1048608 | tf_op jit(solution)/shard_map/ppermute | solution.py:326
  69.5 11.3 %collective-permute-done.1.refs_2_ = bf16[592,1024]{1,0:T(8,128)(2,1)} collective-permute-done((bf16[592,1024]{1,0:T(8,128)(2,1)}, bf16[592,1024]{1,0:T(8,128)(2,1)}, u32[]{:S(2)}, u32[]{:S(2)}) %collective-permute-start.1) | collective-permute-done | bytes 1212448 | tf_op jit(solution)/shard_map/ppermute | solution.py:331
  80.7 6.1 %shrink.3 = bf16[4,368,128]{2,1,0:T(8,128)(2,1)} custom-call(bf16[592,1024]{1,0:T(8,128)(2,1)} %get-tuple-element.26.refs_0_, bf16[592,1024]{1,0:T(8,128)(2,1)} %copy-done.6, bf16[592,1024]{1,0:T(8,128)(2,1)} %collective-permute-done.1.refs_2_, bf16[592,1024]{1,0:T(8,128)(2,1)} %collective-permute-done.2.refs_3_, bf16[4,1024,128]{2,1,0:T(8,128)(2,1)} %refs_4_.1, ...), custom_call_target="tpu_custom_call" | custom-call | flops 22000001024 | bytes 1000 | tf_op jit(solution)/shard_map/shrink/pallas_call | solution.py:200
  89.9 3.3 %collective-permute-start.8 = (bf16[4,368,128]{2,1,0:T(8,128)(2,1)S(1)}, bf16[4,368,128]{2,1,0:T(8,128)(2,1)}, u32[]{:S(2)}, u32[]{:S(2)}) collective-permute-start(bf16[4,368,128]{2,1,0:T(8,128)(2,1)S(1)} %add_convert_fusion.refs_0_), channel_id=1, source_target_pairs={{0,4},{1,5},{2,6},{3,7},{4,0},{5,1},{6,2},{7,3},{8,12},{9,13},{10,... | collective-permute-start | bytes 1130504 | tf_op jit(solution)/shard_map/ppermute | solution.py:336
  96.5 3.2 %collective-permute-start.23 = (bf16[2,1024,128]{2,1,0:T(8,128)(2,1)S(1)}, bf16[2,1024,128]{2,1,0:T(8,128)(2,1)}, u32[]{:S(2)}, u32[]{:S(2)}) collective-permute-start(bf16[2,1024,128]{2,1,0:T(8,128)(2,1)S(1)} %slice.8), channel_id=1, source_target_pairs={{0,8},{8,16},{16,24},{24,32},{32,40},{40,48},{48,56},{56,0},{64,72... | collective-permute-start | bytes 1572872 | tf_op jit(solution)/shard_map/ppermute | solution.py:326
  99.9 7.3 %collective-permute-done.8.refs_1_ = bf16[4,368,128]{2,1,0:T(8,128)(2,1)} collective-permute-done((bf16[4,368,128]{2,1,0:T(8,128)(2,1)S(1)}, bf16[4,368,128]{2,1,0:T(8,128)(2,1)}, u32[]{:S(2)}, u32[]{:S(2)}) %collective-permute-start.8) | collective-permute-done | bytes 376864 | tf_op jit(solution)/shard_map/ppermute | solution.py:336
  107.2 8.6 %collective-permute-done.9.refs_2_ = bf16[4,368,128]{2,1,0:T(8,128)(2,1)} collective-permute-done((bf16[4,368,128]{2,1,0:T(8,128)(2,1)S(1)}, bf16[4,368,128]{2,1,0:T(8,128)(2,1)}, u32[]{:S(2)}, u32[]{:S(2)}) %collective-permute-start.9) | collective-permute-done | bytes 376864 | tf_op jit(solution)/shard_map/ppermute | solution.py:336
  116.7 3.3 %expand.3 = (bf16[368,256]{1,0:T(8,128)(2,1)}, bf16[368,256]{1,0:T(8,128)(2,1)}, bf16[368,256]{1,0:T(8,128)(2,1)}, bf16[368,256]{1,0:T(8,128)(2,1)}) custom-call(s32[2]{0:T(128)} %pad_add_fusion.place_ref, bf16[4,368,128]{2,1,0:T(8,128)(2,1)} %copy-done, bf16[4,368,128]{2,1,0:T(8,128)(2,1)} %collective-permute-done.8.refs_1_, ...), custom_call_target="tpu_custom_call" | custom-call | flops 22000001024 | bytes 1000 | tf_op jit(solution)/shard_map/expand/pallas_call | solution.py:247
  120.0 2.8 %collective-permute-start.11 = (bf16[368,256]{1,0:T(8,128)(2,1)}, bf16[368,256]{1,0:T(8,128)(2,1)S(1)}, u32[]{:S(2)}, u32[]{:S(2)}) collective-permute-start(bf16[368,256]{1,0:T(8,128)(2,1)} %get-tuple-element.30), channel_id=1, source_target_pairs={{0,192},{8,200},{16,208},{24,216},{32,224},{40,232},{48,240},{56,2... | collective-permute-start | bytes 565256 | tf_op jit(solution)/shard_map/ppermute | solution.py:331
  123.6 3.4 %shrink.4 = bf16[4,144,128]{2,1,0:T(8,128)(2,1)} custom-call(bf16[592,1024]{1,0:T(8,128)(2,1)} %get-tuple-element.26.refs_0_, bf16[592,1024]{1,0:T(8,128)(2,1)} %copy-done.6, bf16[592,1024]{1,0:T(8,128)(2,1)} %collective-permute-done.1.refs_2_, bf16[592,1024]{1,0:T(8,128)(2,1)} %collective-permute-done.2.refs_3_, bf16[4,1024,128]{2,1,0:T(8,128)(2,1)} %copy-done.1, ...), custom_call_target="tpu_custom_call" | custom-call | flops 4400000000 | bytes 1000 | tf_op jit(solution)/shard_map/shrink/pallas_call | solution.py:200
  127.0 2.7 %shrink.5 = bf16[4,80,128]{2,1,0:T(8,128)(2,1)} custom-call(bf16[592,1024]{1,0:T(8,128)(2,1)} %get-tuple-element.26.refs_0_, bf16[592,1024]{1,0:T(8,128)(2,1)} %copy-done.6, bf16[592,1024]{1,0:T(8,128)(2,1)} %collective-permute-done.1.refs_2_, bf16[592,1024]{1,0:T(8,128)(2,1)} %collective-permute-done.2.refs_3_, ...), custom_call_target="tpu_custom_call" | custom-call | flops 44000002048 | bytes 1000 | tf_op jit(solution)/shard_map/shrink/pallas_call | solution.py:200
  130.2 2.8 %collective-permute-start.17 = (bf16[4,144,128]{2,1,0:T(8,128)(2,1)S(1)}, bf16[4,144,128]{2,1,0:T(8,128)(2,1)S(1)}, u32[]{:S(2)}, u32[]{:S(2)}) collective-permute-start(bf16[4,144,128]{2,1,0:T(8,128)(2,1)S(1)} %add_convert_fusion.1.refs_0_), channel_id=1, source_target_pairs={{0,4},{1,5},{2,6},{3,7},{4,0},{5,1},{6,2},{7,3},{8,12},{9,13},{10,... | collective-permute-start | bytes 442376 | tf_op jit(solution)/shard_map/ppermute | solution.py:336
  133.1 3.1 %collective-permute-start.19 = (bf16[4,144,128]{2,1,0:T(8,128)(2,1)S(1)}, bf16[4,144,128]{2,1,0:T(8,128)(2,1)S(1)}, u32[]{:S(2)}, u32[]{:S(2)}) collective-permute-start(bf16[4,144,128]{2,1,0:T(8,128)(2,1)S(1)} %add_convert_fusion.1.refs_0_), channel_id=1, source_target_pairs={{0,6},{1,7},{2,0},{3,1},{4,2},{5,3},{6,4},{7,5},{8,14},{9,15},{10,... | collective-permute-start | bytes 442376 | tf_op jit(solution)/shard_map/ppermute | solution.py:336
  138.5 2.7 %collective-permute-start.26 = (bf16[4,80,128]{2,1,0:T(8,128)(2,1)S(1)}, bf16[4,80,128]{2,1,0:T(8,128)(2,1)S(1)}, u32[]{:S(2)}, u32[]{:S(2)}) collective-permute-start(bf16[4,80,128]{2,1,0:T(8,128)(2,1)S(1)} %add_convert_fusion.2.refs_0_), channel_id=1, source_target_pairs={{0,4},{1,5},{2,6},{3,7},{4,0},{5,1},{6,2},{7,3},{8,12},{9,13},{10,... | collective-permute-start | bytes 245768 | tf_op jit(solution)/shard_map/ppermute | solution.py:336
  144.5 2.6 %expand.4 = (bf16[144,256]{1,0:T(8,128)(2,1)}, bf16[144,256]{1,0:T(8,128)(2,1)}, bf16[144,256]{1,0:T(8,128)(2,1)}, bf16[144,256]{1,0:T(8,128)(2,1)}) custom-call(s32[2]{0:T(128)} %pad_add_fusion.place_ref, bf16[4,144,128]{2,1,0:T(8,128)(2,1)} %copy-done.3, bf16[4,144,128]{2,1,0:T(8,128)(2,1)} %copy-done.13, bf16[4,144,128]{2,1,0:T(8,128)(2,1)} %copy-done.14, ...), custom_call_target="tpu_custom_call" | custom-call | flops 3300000000 | bytes 1000 | tf_op jit(solution)/shard_map/expand/pallas_call | solution.py:247
  155.0 2.7 %collective-permute-start.29 = (bf16[80,256]{1,0:T(8,128)(2,1)}, bf16[80,256]{1,0:T(8,128)(2,1)S(1)}, u32[]{:S(2)}, u32[]{:S(2)}) collective-permute-start(bf16[80,256]{1,0:T(8,128)(2,1)} %get-tuple-element.38), channel_id=1, source_target_pairs={{0,192},{8,200},{16,208},{24,216},{32,224},{40,232},{48,240},{56,2... | collective-permute-start | bytes 122888 | tf_op jit(solution)/shard_map/ppermute | solution.py:331
  159.3 6.9 %gather.1.total_ref = f32[1536,256]{1,0:T(8,128)} custom-call(s32[1536,128]{1,0:T(8,128)} %get-tuple-element.23.col_ref, bf16[1536,256]{1,0:T(8,128)(2,1)} %bitcast.6, bf16[368,256]{1,0:T(8,128)(2,1)} %get-tuple-element.29.refs_0_, bf16[368,256]{1,0:T(8,128)(2,1)} %copy-done.9, bf16[368,256]{1,0:T(8,128)(2,1)} %copy-done.10, bf16[368,256]{1,0:T(8,128)(2,1)} %copy-done.12, ...), custom_call_target="tpu_custom_call" | custom-call | flops 7699999744 | bytes 1000 | tf_op jit(solution)/shard_map/gather/pallas_call | solution.py:279
  166.9 5.7 %finish.1 = bf16[3072,128]{1,0:T(8,128)(2,1)} custom-call(s32[1536,128]{1,0:T(8,128)} %get-tuple-element.23.col_ref, f32[1536,256]{1,0:T(8,128)} %gather.1.total_ref, bf16[80,256]{1,0:T(8,128)(2,1)} %get-tuple-element.37.refs_0_, bf16[80,256]{1,0:T(8,128)(2,1)} %copy-done.22, bf16[80,256]{1,0:T(8,128)(2,1)} %copy-done.23, bf16[80,256]{1,0:T(8,128)(2,1)} %copy-done.24), custom_call_target="tpu_custom_call" | custom-call | flops 6600000000 | bytes 1000 | tf_op jit(solution)/shard_map/finish/pallas_call | solution.py:307
  (113 shorter events, 33.8 us)
Async XLA Ops:
  7.4 92.5 %all-gather.2.cloned.1.call-start = ((), (), s32[]{:S(2)}) async-start(), calls=%async_computation.2 | async-start | bytes 1179648 | tf_op jit(solution)/shard_map/all_gather | solution.py:364
  7.4 29.6 %collective-permute-start.3 = (bf16[4,1024,128]{2,1,0:T(8,128)(2,1)}, bf16[4,1024,128]{2,1,0:T(8,128)(2,1)S(1)}, u32[]{:S(2)}, u32[]{:S(2)}) collective-permute-start(bf16[4,1024,128]{2,1,0:T(8,128)(2,1)} %refs_4_.1), channel_id=1, source_target_pairs={{0,8},{8,16},{16,24},{24,32},{32,40},{40,48},{48,56},{56,0},{64,72... | collective-permute-start | bytes 3145736 | tf_op jit(solution)/shard_map/ppermute | solution.py:326
  9.3 32.2 %collective-permute-start.4 = (bf16[4,1024,128]{2,1,0:T(8,128)(2,1)}, bf16[4,1024,128]{2,1,0:T(8,128)(2,1)S(1)}, u32[]{:S(2)}, u32[]{:S(2)}) collective-permute-start(bf16[4,1024,128]{2,1,0:T(8,128)(2,1)} %refs_4_.1), channel_id=1, source_target_pairs={{0,56},{8,0},{16,8},{24,16},{32,24},{40,32},{48,40},{56,48},{64,12... | collective-permute-start | bytes 3145736 | tf_op jit(solution)/shard_map/ppermute | solution.py:326
  9.4 149.3 %reduce-scatter.2.cloned.1.call-start = ((), (), s32[]{:S(2)}) async-start(), calls=%async_computation.1 | async-start | bytes 7077888 | tf_op jit(solution)/shard_map/reduce_scatter | solution.py:367
  24.2 45.2 %collective-permute-start = (bf16[592,1024]{1,0:T(8,128)(2,1)}, bf16[592,1024]{1,0:T(8,128)(2,1)S(1)}, u32[]{:S(2)}, u32[]{:S(2)}) collective-permute-start(bf16[592,1024]{1,0:T(8,128)(2,1)} %get-tuple-element.25._), channel_id=1, source_target_pairs={{0,64},{8,72},{16,80},{24,88},{32,96},{40,104},{48,112},{56,120},{... | collective-permute-start | bytes 3637256 | tf_op jit(solution)/shard_map/ppermute | solution.py:331
  25.7 55.0 %collective-permute-start.1 = (bf16[592,1024]{1,0:T(8,128)(2,1)}, bf16[592,1024]{1,0:T(8,128)(2,1)}, u32[]{:S(2)}, u32[]{:S(2)}) collective-permute-start(bf16[592,1024]{1,0:T(8,128)(2,1)} %get-tuple-element.27), channel_id=1, source_target_pairs={{0,128},{8,136},{16,144},{24,152},{32,160},{40,168},{48,176},{56,1... | collective-permute-start | bytes 3637256 | tf_op jit(solution)/shard_map/ppermute | solution.py:331
  28.4 52.3 %collective-permute-start.2 = (bf16[592,1024]{1,0:T(8,128)(2,1)}, bf16[592,1024]{1,0:T(8,128)(2,1)}, u32[]{:S(2)}, u32[]{:S(2)}) collective-permute-start(bf16[592,1024]{1,0:T(8,128)(2,1)} %get-tuple-element.28), channel_id=1, source_target_pairs={{0,192},{8,200},{16,208},{24,216},{32,224},{40,232},{48,240},{56,2... | collective-permute-start | bytes 3637256 | tf_op jit(solution)/shard_map/ppermute | solution.py:331
  37.0 28.7 %collective-permute-start.5 = (bf16[4,1024,128]{2,1,0:T(8,128)(2,1)S(1)}, bf16[4,1024,128]{2,1,0:T(8,128)(2,1)}, u32[]{:S(2)}, u32[]{:S(2)}) collective-permute-start(bf16[4,1024,128]{2,1,0:T(8,128)(2,1)S(1)} %collective-permute-done.3.refs_5_), channel_id=1, source_target_pairs={{0,8},{8,16},{16,24},{24,32},{32,40},{40,48},{48,56},{56,0},{64,72... | collective-permute-start | bytes 3145736 | tf_op jit(solution)/shard_map/ppermute | solution.py:326
  41.5 28.0 %collective-permute-start.6 = (bf16[4,1024,128]{2,1,0:T(8,128)(2,1)S(1)}, bf16[4,1024,128]{2,1,0:T(8,128)(2,1)}, u32[]{:S(2)}, u32[]{:S(2)}) collective-permute-start(bf16[4,1024,128]{2,1,0:T(8,128)(2,1)S(1)} %collective-permute-done.4.refs_6_), channel_id=1, source_target_pairs={{0,56},{8,0},{16,8},{24,16},{32,24},{40,32},{48,40},{56,48},{64,12... | collective-permute-start | bytes 3145736 | tf_op jit(solution)/shard_map/ppermute | solution.py:326
  65.7 30.7 %collective-permute-start.14 = (bf16[4,1024,128]{2,1,0:T(8,128)(2,1)}, bf16[4,1024,128]{2,1,0:T(8,128)(2,1)S(1)}, u32[]{:S(2)}, u32[]{:S(2)}) collective-permute-start(bf16[4,1024,128]{2,1,0:T(8,128)(2,1)} %collective-permute-done.5.refs_7_), channel_id=1, source_target_pairs={{0,8},{8,16},{16,24},{24,32},{32,40},{40,48},{48,56},{56,0},{64,72... | collective-permute-start | bytes 3145736 | tf_op jit(solution)/shard_map/ppermute | solution.py:326
  69.4 30.2 %collective-permute-start.15 = (bf16[4,1024,128]{2,1,0:T(8,128)(2,1)}, bf16[4,1024,128]{2,1,0:T(8,128)(2,1)S(1)}, u32[]{:S(2)}, u32[]{:S(2)}) collective-permute-start(bf16[4,1024,128]{2,1,0:T(8,128)(2,1)} %collective-permute-done.6.refs_8_), channel_id=1, source_target_pairs={{0,56},{8,0},{16,8},{24,16},{32,24},{40,32},{48,40},{56,48},{64,12... | collective-permute-start | bytes 3145736 | tf_op jit(solution)/shard_map/ppermute | solution.py:326
  89.9 17.3 %collective-permute-start.8 = (bf16[4,368,128]{2,1,0:T(8,128)(2,1)S(1)}, bf16[4,368,128]{2,1,0:T(8,128)(2,1)}, u32[]{:S(2)}, u32[]{:S(2)}) collective-permute-start(bf16[4,368,128]{2,1,0:T(8,128)(2,1)S(1)} %add_convert_fusion.refs_0_), channel_id=1, source_target_pairs={{0,4},{1,5},{2,6},{3,7},{4,0},{5,1},{6,2},{7,3},{8,12},{9,13},{10,... | collective-permute-start | bytes 1130504 | tf_op jit(solution)/shard_map/ppermute | solution.py:336
  93.2 22.6 %collective-permute-start.9 = (bf16[4,368,128]{2,1,0:T(8,128)(2,1)S(1)}, bf16[4,368,128]{2,1,0:T(8,128)(2,1)}, u32[]{:S(2)}, u32[]{:S(2)}) collective-permute-start(bf16[4,368,128]{2,1,0:T(8,128)(2,1)S(1)} %add_convert_fusion.refs_0_), channel_id=1, source_target_pairs={{0,2},{1,3},{2,4},{3,5},{4,6},{5,7},{6,0},{7,1},{8,10},{9,11},{10,... | collective-permute-start | bytes 1130504 | tf_op jit(solution)/shard_map/ppermute | solution.py:336
  93.8 22.8 %collective-permute-start.10 = (bf16[4,368,128]{2,1,0:T(8,128)(2,1)S(1)}, bf16[4,368,128]{2,1,0:T(8,128)(2,1)}, u32[]{:S(2)}, u32[]{:S(2)}) collective-permute-start(bf16[4,368,128]{2,1,0:T(8,128)(2,1)S(1)} %add_convert_fusion.refs_0_), channel_id=1, source_target_pairs={{0,6},{1,7},{2,0},{3,1},{4,2},{5,3},{6,4},{7,5},{8,14},{9,15},{10,... | collective-permute-start | bytes 1130504 | tf_op jit(solution)/shard_map/ppermute | solution.py:336
  96.5 30.5 %collective-permute-start.23 = (bf16[2,1024,128]{2,1,0:T(8,128)(2,1)S(1)}, bf16[2,1024,128]{2,1,0:T(8,128)(2,1)}, u32[]{:S(2)}, u32[]{:S(2)}) collective-permute-start(bf16[2,1024,128]{2,1,0:T(8,128)(2,1)S(1)} %slice.8), channel_id=1, source_target_pairs={{0,8},{8,16},{16,24},{24,32},{32,40},{40,48},{48,56},{56,0},{64,72... | collective-permute-start | bytes 1572872 | tf_op jit(solution)/shard_map/ppermute | solution.py:326
  99.7 27.3 %collective-permute-start.24 = (bf16[2,1024,128]{2,1,0:T(8,128)(2,1)S(1)}, bf16[2,1024,128]{2,1,0:T(8,128)(2,1)}, u32[]{:S(2)}, u32[]{:S(2)}) collective-permute-start(bf16[2,1024,128]{2,1,0:T(8,128)(2,1)S(1)} %slice.9), channel_id=1, source_target_pairs={{0,56},{8,0},{16,8},{24,16},{32,24},{40,32},{48,40},{56,48},{64,12... | collective-permute-start | bytes 1572872 | tf_op jit(solution)/shard_map/ppermute | solution.py:326
  120.0 27.2 %collective-permute-start.11 = (bf16[368,256]{1,0:T(8,128)(2,1)}, bf16[368,256]{1,0:T(8,128)(2,1)S(1)}, u32[]{:S(2)}, u32[]{:S(2)}) collective-permute-start(bf16[368,256]{1,0:T(8,128)(2,1)} %get-tuple-element.30), channel_id=1, source_target_pairs={{0,192},{8,200},{16,208},{24,216},{32,224},{40,232},{48,240},{56,2... | collective-permute-start | bytes 565256 | tf_op jit(solution)/shard_map/ppermute | solution.py:331
  122.7 32.2 %collective-permute-start.12 = (bf16[368,256]{1,0:T(8,128)(2,1)}, bf16[368,256]{1,0:T(8,128)(2,1)S(1)}, u32[]{:S(2)}, u32[]{:S(2)}) collective-permute-start(bf16[368,256]{1,0:T(8,128)(2,1)} %get-tuple-element.31), channel_id=1, source_target_pairs={{0,128},{8,136},{16,144},{24,152},{32,160},{40,168},{48,176},{56,1... | collective-permute-start | bytes 565256 | tf_op jit(solution)/shard_map/ppermute | solution.py:331
  138.5 9.6 %collective-permute-start.26 = (bf16[4,80,128]{2,1,0:T(8,128)(2,1)S(1)}, bf16[4,80,128]{2,1,0:T(8,128)(2,1)S(1)}, u32[]{:S(2)}, u32[]{:S(2)}) collective-permute-start(bf16[4,80,128]{2,1,0:T(8,128)(2,1)S(1)} %add_convert_fusion.2.refs_0_), channel_id=1, source_target_pairs={{0,4},{1,5},{2,6},{3,7},{4,0},{5,1},{6,2},{7,3},{8,12},{9,13},{10,... | collective-permute-start | bytes 245768 | tf_op jit(solution)/shard_map/ppermute | solution.py:336
  141.2 9.2 %collective-permute-start.27 = (bf16[4,80,128]{2,1,0:T(8,128)(2,1)S(1)}, bf16[4,80,128]{2,1,0:T(8,128)(2,1)S(1)}, u32[]{:S(2)}, u32[]{:S(2)}) collective-permute-start(bf16[4,80,128]{2,1,0:T(8,128)(2,1)S(1)} %add_convert_fusion.2.refs_0_), channel_id=1, source_target_pairs={{0,2},{1,3},{2,4},{3,5},{4,6},{5,7},{6,0},{7,1},{8,10},{9,11},{10,... | collective-permute-start | bytes 245768 | tf_op jit(solution)/shard_map/ppermute | solution.py:336
  142.0 10.0 %collective-permute-start.28 = (bf16[4,80,128]{2,1,0:T(8,128)(2,1)S(1)}, bf16[4,80,128]{2,1,0:T(8,128)(2,1)S(1)}, u32[]{:S(2)}, u32[]{:S(2)}) collective-permute-start(bf16[4,80,128]{2,1,0:T(8,128)(2,1)S(1)} %add_convert_fusion.2.refs_0_), channel_id=1, source_target_pairs={{0,6},{1,7},{2,0},{3,1},{4,2},{5,3},{6,4},{7,5},{8,14},{9,15},{10,... | collective-permute-start | bytes 245768 | tf_op jit(solution)/shard_map/ppermute | solution.py:336
  147.2 10.5 %collective-permute-start.13 = (bf16[368,256]{1,0:T(8,128)(2,1)S(1)}, bf16[368,256]{1,0:T(8,128)(2,1)S(1)}, u32[]{:S(2)}, u32[]{:S(2)}) collective-permute-start(bf16[368,256]{1,0:T(8,128)(2,1)S(1)} %copy-done.11), channel_id=1, source_target_pairs={{0,64},{8,72},{16,80},{24,88},{32,96},{40,104},{48,112},{56,120},{... | collective-permute-start | bytes 565256 | tf_op jit(solution)/shard_map/ppermute | solution.py:331
  148.1 10.4 %collective-permute-start.20 = (bf16[144,256]{1,0:T(8,128)(2,1)}, bf16[144,256]{1,0:T(8,128)(2,1)S(1)}, u32[]{:S(2)}, u32[]{:S(2)}) collective-permute-start(bf16[144,256]{1,0:T(8,128)(2,1)} %get-tuple-element.34), channel_id=1, source_target_pairs={{0,192},{8,200},{16,208},{24,216},{32,224},{40,232},{48,240},{56,2... | collective-permute-start | bytes 221192 | tf_op jit(solution)/shard_map/ppermute | solution.py:331
  155.0 11.2 %collective-permute-start.29 = (bf16[80,256]{1,0:T(8,128)(2,1)}, bf16[80,256]{1,0:T(8,128)(2,1)S(1)}, u32[]{:S(2)}, u32[]{:S(2)}) collective-permute-start(bf16[80,256]{1,0:T(8,128)(2,1)} %get-tuple-element.38), channel_id=1, source_target_pairs={{0,192},{8,200},{16,208},{24,216},{32,224},{40,232},{48,240},{56,2... | collective-permute-start | bytes 122888 | tf_op jit(solution)/shard_map/ppermute | solution.py:331
  (35 other events, 246.4 us)
Sparse Core Ops, SparseCore 0:
  10.0 43.0 all-gather.1
Sparse Core Ops, SparseCore 1:
  53.3 65.2 reduce-scatter.1

commit v2 on v1

v2 whole, which is shorter than its diff:
```python
import functools

import jax
import jax.numpy as jnp
from jax import lax
from jax.experimental import pallas as pl
from jax.experimental.pallas import tpu as pltpu
from jax.sharding import PartitionSpec as P

F32 = jnp.float32
BF16 = jnp.bfloat16
I32 = jnp.int32

NX, NZ = 4, 8
NY = 4
LOCAL = 4
CAP = 18
BLOCK = LOCAL * CAP
WIDE = 80

NEAR = (0, 7, 1, 6, 2)
FAR = (5, 3)
OPPOSITE = 4
NEAR_ROWS = 368
FAR_ROWS = 144
ROWS = 592
LATE_ROWS = ROWS - NEAR_ROWS
START = {offset: k * BLOCK for k, offset in enumerate(NEAR)}
START.update({offset: NEAR_ROWS + k * BLOCK for k, offset in enumerate(FAR)})
START[OPPOSITE] = NEAR_ROWS + FAR_ROWS

MIB = 1024 * 1024
VMEM = 56 * MIB
COST = {
    "route": 3, "pack": 3, "base": 11, "carve": 1, "shrink_near": 1, "expand_near": 1,
    "shrink_far": 120, "shrink_late": 3, "expand_late": 30, "gather": 5, "finish": 5,
}
VMEM = 56 * 1024 * 1024


def iota(shape, dim):
    return lax.broadcasted_iota(I32, shape, dim)


def params(*semantics, limit=VMEM):
    if semantics:
        return pltpu.CompilerParams(vmem_limit_bytes=limit, dimension_semantics=semantics)
    return pltpu.CompilerParams(vmem_limit_bytes=limit)


def cost(micros):
    return pl.CostEstimate(
        flops=int(micros * 1.1e9), bytes_accessed=1000, transcendentals=0
    )


def whole():
    return pl.BlockSpec(memory_space=pltpu.VMEM)


def scalars():
    return pl.BlockSpec(memory_space=pltpu.SMEM)


def route_kernel(place_ref, ids_ref, store_ref, row_ref, col_ref):
    x, z = place_ref[0], place_ref[1]
    count = ids_ref.shape[1]
    ids = jnp.broadcast_to(ids_ref[...], (128, count))
    ids_down = ids.T
    store = jnp.broadcast_to(store_ref[...], (128, 128)).T
    for j in range(count // 128):
        mine = ids[:, j * 128 : (j + 1) * 128]
        placed = jnp.sum(
            jnp.where(mine == iota((128, 128), 0), store, 0), axis=0, keepdims=True
        )
        seen = (j + 1) * 128
        same = (ids_down[:seen] == mine[:1]) & (
            iota((seen, 128), 0) < iota((seen, 128), 1) + j * 128
        )
        ordinal = jnp.sum(same.astype(I32), axis=0, keepdims=True)
        owner = placed >> 2
        east = ((owner >> 3) - x) & 3
        north = ((owner & 7) - z) & 7
        start = jnp.zeros_like(owner)
        for offset, first in START.items():
            start = jnp.where(north == offset, first, start)
        row_ref[:, j * 128 : (j + 1) * 128] = (
            east * ROWS + start + (placed & 3) * CAP + ordinal
        )
    col_ref[...] = jnp.broadcast_to(row_ref[...], (128, count)).T


def route(place, ids, store):
    count = ids.shape[1]
    return pl.pallas_call(
        route_kernel,
        out_shape=(
            jax.ShapeDtypeStruct((1, count), I32),
            jax.ShapeDtypeStruct((count, 128), I32),
        ),
        in_specs=[scalars(), whole(), whole()],
        out_specs=(whole(), whole()),
        compiler_params=params(),
        cost_estimate=cost(COST['route']),
        name="route",
    )(place, ids, store)


def pack_kernel(e, row_ref, tok_ref, out_ref):
    hot = row_ref[...] == iota((ROWS, row_ref.shape[1]), 0) + e * ROWS
    out_ref[...] = jnp.dot(
        hot.astype(BF16), tok_ref[...], preferred_element_type=F32
    ).astype(BF16)


def pack(e, row, tokens):
    return pl.pallas_call(
        functools.partial(pack_kernel, e),
        out_shape=jax.ShapeDtypeStruct((ROWS, tokens.shape[1]), BF16),
        in_specs=[whole()] * 2,
        out_specs=whole(),
        compiler_params=params(limit=24 * MIB),
        cost_estimate=cost(COST["pack"]),
        name="pack",
    )(row, tokens)


def base_kernel(tok_ref, w_ref, *refs):
    out_ref = refs[-1]
    for p in range(out_ref.shape[0]):
        columns = slice(p * 128, (p + 1) * 128)
        both = jnp.concatenate([w_ref[0, :, columns], w_ref[1, :, columns]], axis=1)
        out_ref[p] = jnp.dot(tok_ref[...], both, preferred_element_type=F32).astype(BF16)


def base(tokens, weight, parts, *earlier):
    count, width = tokens.shape
    step = 2
    return pl.pallas_call(
        base_kernel,
        grid=(parts // step,),
        out_shape=jax.ShapeDtypeStruct((parts, count, 256), BF16),
        in_specs=[
            pl.BlockSpec((count, width), lambda i: (0, 0)),
            pl.BlockSpec((2, width, step * 128), lambda i: (0, 0, i)),
        ]
        + [pl.BlockSpec(memory_space=pl.ANY)] * len(earlier),
        out_specs=pl.BlockSpec((step, count, 256), lambda i: (i, 0, 0)),
        compiler_params=params("arbitrary"),
        cost_estimate=cost(COST["base"]),
        name="base",
    )(tokens, weight, *earlier)


def adapter_of(skip, copies):
    row = iota((WIDE, 1), 0) - skip
    which = jnp.full((WIDE, 1), -1, I32)
    for a in range(LOCAL):
        which = jnp.where((row >= a * CAP) & (row < (a + 1) * CAP), a, which)
    return jnp.concatenate([which] * copies, axis=0)


def spans(blocks):
    return [(k, k * BLOCK // 16 * 16, k * BLOCK % 16) for k in range(len(blocks))]


def shrunk_rows(rows, panel, skip, copies):
    y = jnp.dot(
        rows,
        jnp.concatenate([panel[a] for a in range(LOCAL)], axis=1),
        preferred_element_type=F32,
    )
    which = adapter_of(skip, copies)
    kept = jnp.zeros((copies * WIDE, 128), F32)
    for a in range(LOCAL):
        kept = kept + jnp.where(which == a, y[:, a * 128 : (a + 1) * 128], 0.0)
    return kept


def shrink_blocks(xs, panels, blocks, total):
    for k, low, skip in spans(blocks):
        rows = jnp.concatenate([x[low : low + WIDE, :] for x in xs], axis=0)
        kept = shrunk_rows(rows, panels[k], skip, NX)
        for e in range(NX):
            total[e, low : low + WIDE, :] += kept[e * WIDE : (e + 1) * WIDE]


def shrink_near_kernel(place_ref, *refs):
    xs, panels = refs[:NX], refs[NX : NX + len(NEAR)]
    keep_ref, send_ref, total = refs[NX + len(NEAR) + 1 :]
    total[...] = jnp.zeros_like(total)
    shrink_blocks(xs, panels, NEAR, total)
    core = place_ref[2]
    keep_ref[...] = total[pl.ds(core * 2, 2)].astype(BF16)
    send_ref[...] = total[pl.ds(2 - core * 2, 2)].astype(BF16)


def shrink_near(place, xs, panels, earlier):
    width = xs[0].shape[1]
    half = jax.ShapeDtypeStruct((2, NEAR_ROWS, 128), BF16)
    return pl.pallas_call(
        shrink_near_kernel,
        grid=(1,),
        out_shape=(half, half),
        in_specs=[scalars()]
        + [pl.BlockSpec((pl.Element(NEAR_ROWS), pl.Element(width)), lambda i: (0, 0))] * NX
        + [pl.BlockSpec(w.shape, lambda i: (0, 0, 0)) for w in panels]
        + [pl.BlockSpec(memory_space=pl.ANY)],
        out_specs=(pl.BlockSpec(half.shape, lambda i: (0, 0, 0)),) * 2,
        scratch_shapes=[pltpu.VMEM((NX, NEAR_ROWS, 128), F32)],
        compiler_params=params("arbitrary", limit=32 * MIB),
        cost_estimate=cost(COST["shrink_near"]),
        name="shrink_near",
    )(place, *xs, *panels, earlier)


def carve_kernel(*refs):
    xs, outs = refs[:NX], refs[NX:]
    for e in range(NX):
        outs[e // 2][e % 2] = xs[e][...]


def carve(xs):
    width = xs[0].shape[1]
    first = NEAR_ROWS + FAR_ROWS
    pair = jax.ShapeDtypeStruct((2, WIDE, width), BF16)
    return pl.pallas_call(
        carve_kernel,
        grid=(1,),
        out_shape=(pair, pair),
        in_specs=[pl.BlockSpec((pl.Element(WIDE), pl.Element(width)), lambda i: (first, 0))] * NX,
        out_specs=(pl.BlockSpec(pair.shape, lambda i: (0, 0, 0)),) * 2,
        compiler_params=params("arbitrary", limit=8 * MIB),
        cost_estimate=cost(COST["carve"]),
        name="carve",
    )(*xs)


def shrink_far_kernel(*refs):
    xs, panels = refs[:NX], refs[NX : NX + 2]
    out_ref, total = refs[NX + 4 :]
    total[...] = jnp.zeros_like(total)
    shrink_blocks(xs, panels, FAR, total)
    out_ref[...] = total[...].astype(BF16)


def shrink_far(xs, panels, *earlier):
    width = xs[0].shape[1]
    return pl.pallas_call(
        shrink_far_kernel,
        grid=(1,),
        out_shape=jax.ShapeDtypeStruct((NX, FAR_ROWS, 128), BF16),
        in_specs=[
            pl.BlockSpec((pl.Element(FAR_ROWS), pl.Element(width)), lambda i: (NEAR_ROWS, 0))
        ]
        * NX
        + [pl.BlockSpec(w.shape, lambda i: (0, 0, 0)) for w in panels]
        + [pl.BlockSpec(memory_space=pl.ANY)] * len(earlier),
        out_specs=pl.BlockSpec((NX, FAR_ROWS, 128), lambda i: (0, 0, 0)),
        scratch_shapes=[pltpu.VMEM((NX, FAR_ROWS, 128), F32)],
        compiler_params=params("arbitrary", limit=16 * MIB),
        cost_estimate=cost(COST["shrink_far"]),
        name="shrink_far",
    )(*xs, *panels, *earlier)


def shrink_late_kernel(far_ref, from_low, from_high, low_ref, high_ref, _, out_ref):
    out_ref[:, :FAR_ROWS, :] = far_ref[...]
    for guest, panel, first in ((from_low, high_ref, 0), (from_high, low_ref, 2)):
        kept = shrunk_rows(jnp.concatenate([guest[0], guest[1]], axis=0), panel, 0, 2)
        for e in range(2):
            out_ref[first + e, FAR_ROWS:, :] = kept[e * WIDE : (e + 1) * WIDE].astype(BF16)


def shrink_late(far, guests, panels, earlier):
    return pl.pallas_call(
        shrink_late_kernel,
        out_shape=jax.ShapeDtypeStruct((NX, LATE_ROWS, 128), BF16),
        in_specs=[whole()] * 5 + [pl.BlockSpec(memory_space=pl.ANY)],
        out_specs=whole(),
        compiler_params=params(limit=16 * MIB),
        cost_estimate=cost(COST["shrink_late"]),
        name="shrink_late",
    )(far, *guests, *panels, earlier)


def widen(up_ref, owner, wide_up):
    for a in range(LOCAL):
        for c in range(2):
            wide_up[a * 128 + c * 64 : a * 128 + c * 64 + 64, c * 128 : (c + 1) * 128] = up_ref[
                owner * LOCAL + a, c
            ]


def expanded_rows(rows, wide_up, skip, copies):
    which = adapter_of(skip, copies)
    lhs = jnp.concatenate(
        [jnp.where(which == a, rows, jnp.zeros_like(rows)) for a in range(LOCAL)], axis=1
    )
    return jnp.dot(lhs, wide_up[...], preferred_element_type=F32)


def expand_near_kernel(place_ref, mine_ref, other_ref, up_ref, _, *refs):
    outs, wide_up, total, shrunk = refs[:NX], refs[NX], refs[NX + 1], refs[NX + 2]
    z, core = place_ref[1], place_ref[2]
    shrunk[pl.ds(core * 2, 2)] = mine_ref[...]
    shrunk[pl.ds(2 - core * 2, 2)] = other_ref[...]
    wide_up[...] = jnp.zeros_like(wide_up)
    total[...] = jnp.zeros_like(total)
    for k, low, skip in spans(NEAR):
        widen(up_ref, (z + NEAR[k]) & (NZ - 1), wide_up)
        rows = jnp.concatenate([shrunk[e, low : low + WIDE] for e in range(NX)], axis=0)
        y = expanded_rows(rows, wide_up, skip, NX)
        for e in range(NX):
            total[e, low : low + WIDE, :] += y[e * WIDE : (e + 1) * WIDE]
    for e in range(NX):
        outs[e][...] = total[e].astype(BF16)


def expand_near(place, mine, other, up, earlier):
    return pl.pallas_call(
        expand_near_kernel,
        out_shape=[jax.ShapeDtypeStruct((NEAR_ROWS, 256), BF16)] * NX,
        in_specs=[scalars()] + [whole()] * 3 + [pl.BlockSpec(memory_space=pl.ANY)],
        out_specs=[whole()] * NX,
        scratch_shapes=[
            pltpu.VMEM((LOCAL * 128, 256), BF16),
            pltpu.VMEM((NX, NEAR_ROWS, 256), F32),
            pltpu.VMEM((NX, NEAR_ROWS, 128), BF16),
        ],
        compiler_params=params(limit=16 * MIB),
        cost_estimate=cost(COST["expand_near"]),
        name="expand_near",
    )(place, mine, other, up, earlier)


def expand_late_kernel(place_ref, mine_ref, other_ref, up_ref, _, *refs):
    outs, wides, total = refs[:NX], refs[NX : NX + 2], refs[NX + 2]
    z = place_ref[1]
    shrunk = (mine_ref[...].astype(F32) + other_ref[...].astype(F32)).astype(BF16)
    total[...] = jnp.zeros_like(total)
    for k, low, skip in spans(FAR):
        wide_up = wides[k]
        wide_up[...] = jnp.zeros_like(wide_up)
        widen(up_ref, (z + FAR[k]) & (NZ - 1), wide_up)
        rows = jnp.concatenate([shrunk[e, low : low + WIDE] for e in range(NX)], axis=0)
        y = expanded_rows(rows, wide_up, skip, NX)
        for e in range(NX):
            total[e, low : low + WIDE, :] += y[e * WIDE : (e + 1) * WIDE]
    for wide_up, first in ((wides[1], 0), (wides[0], 2)):
        rows = jnp.concatenate([shrunk[first + e, FAR_ROWS:] for e in range(2)], axis=0)
        y = expanded_rows(rows, wide_up, 0, 2)
        for e in range(2):
            total[first + e, FAR_ROWS:, :] = y[e * WIDE : (e + 1) * WIDE]
    for e in range(NX):
        outs[e][...] = total[e].astype(BF16)


def expand_late(place, mine, other, up, earlier):
    return pl.pallas_call(
        expand_late_kernel,
        out_shape=[jax.ShapeDtypeStruct((LATE_ROWS, 256), BF16)] * NX,
        in_specs=[scalars()] + [whole()] * 3 + [pl.BlockSpec(memory_space=pl.ANY)],
        out_specs=[whole()] * NX,
        scratch_shapes=[
            pltpu.VMEM((LOCAL * 128, 256), BF16),
            pltpu.VMEM((LOCAL * 128, 256), BF16),
            pltpu.VMEM((NX, LATE_ROWS, 256), F32),
        ],
        compiler_params=params(limit=16 * MIB),
        cost_estimate=cost(COST["expand_late"]),
        name="expand_late",
    )(place, mine, other, up, earlier)


def gather_kernel(col_ref, base_ref, *refs):
    deltas, out_ref, table = refs[:NX], refs[NX], refs[NX + 1]
    full = table.shape[0]
    filled = NX * NEAR_ROWS

    @pl.when(pl.program_id(0) == 0)
    def _():
        for e in range(NX):
            table[e * NEAR_ROWS : (e + 1) * NEAR_ROWS, :] = deltas[e][...]
        table[filled:, :] = jnp.zeros((full - filled, 256), BF16)

    place = iota((1, full), 1)
    slots = jnp.where(place < filled, place, -1)
    for e in range(1, NX):
        slots = jnp.where(
            (place >= e * NEAR_ROWS) & (place < filled), place + e * LATE_ROWS, slots
        )
    hot = (col_ref[:, :1] == slots).astype(BF16)
    out_ref[...] = base_ref[...].astype(F32) + jnp.dot(
        hot, table[...], preferred_element_type=F32
    )


def gather(col, summed, deltas):
    count = col.shape[0]
    step = 512
    return pl.pallas_call(
        gather_kernel,
        grid=(count // step,),
        out_shape=jax.ShapeDtypeStruct((count, 256), F32),
        in_specs=[
            pl.BlockSpec((step, 128), lambda i: (i, 0)),
            pl.BlockSpec((step, 256), lambda i: (i, 0)),
        ]
        + [pl.BlockSpec(d.shape, lambda i: (0, 0)) for d in deltas],
        out_specs=pl.BlockSpec((step, 256), lambda i: (i, 0)),
        scratch_shapes=[pltpu.VMEM((1536, 256), BF16)],
        compiler_params=params("arbitrary", limit=24 * MIB),
        cost_estimate=cost(COST["gather"]),
        name="gather",
    )(col, summed, *deltas)


def finish_kernel(col_ref, total_ref, *refs):
    deltas, guests, out_ref, both, table = refs[:NX], refs[NX : NX + 2], refs[-3], refs[-2], refs[-1]
    rows, full = col_ref.shape[0], table.shape[0]
    far = NX * FAR_ROWS

    @pl.when(pl.program_id(0) == 0)
    def _():
        for e in range(NX):
            table[e * FAR_ROWS : (e + 1) * FAR_ROWS, :] = deltas[e][:FAR_ROWS, :]
            low = far + e * WIDE
            table[low : low + WIDE, :] = guests[e // 2][e % 2]

    place = iota((1, full), 1)
    slots = place
    for e in range(NX):
        start = e * ROWS + NEAR_ROWS - e * FAR_ROWS
        slots = jnp.where((place >= e * FAR_ROWS) & (place < far), place + start, slots)
        low = far + e * WIDE
        start = e * ROWS + NEAR_ROWS + FAR_ROWS - low
        slots = jnp.where(place >= low, place + start, slots)
    hot = (col_ref[:, :1] == slots).astype(BF16)
    total = total_ref[...] + jnp.dot(hot, table[...], preferred_element_type=F32)
    both[pl.ds(0, rows, stride=2), :] = total[:, :128]
    both[pl.ds(1, rows, stride=2), :] = total[:, 128:]
    out_ref[...] = both[...].astype(BF16)


def finish(col, total, deltas, guests):
    count = col.shape[0]
    step = 512
    return pl.pallas_call(
        finish_kernel,
        grid=(count // step,),
        out_shape=jax.ShapeDtypeStruct((2 * count, 128), BF16),
        in_specs=[
            pl.BlockSpec((step, 128), lambda i: (i, 0)),
            pl.BlockSpec((step, 256), lambda i: (i, 0)),
        ]
        + [pl.BlockSpec(d.shape, lambda i: (0, 0)) for d in deltas]
        + [pl.BlockSpec(g.shape, lambda i: (0, 0, 0)) for g in guests],
        out_specs=pl.BlockSpec((2 * step, 128), lambda i: (i, 0)),
        scratch_shapes=[
            pltpu.VMEM((2 * step, 128), F32),
            pltpu.VMEM((NX * (FAR_ROWS + WIDE), 256), BF16),
        ],
        compiler_params=params("arbitrary", limit=24 * MIB),
        cost_estimate=cost(COST["finish"]),
        name="finish",
    )(col, total, *deltas, *guests)


def along_z(array, d):
    pairs = [(x * NZ + z, x * NZ + (z + d) % NZ) for x in range(NX) for z in range(NZ)]
    return lax.ppermute(array, "ad", pairs)


def along_x(array, d):
    pairs = [(x * NZ + z, (x + d) % NX * NZ + z) for x in range(NX) for z in range(NZ)]
    return lax.ppermute(array, "ad", pairs)


def with_core(array):
    return lax.ppermute(array, "tp", [(i, i ^ 1) for i in range(2 * NY)])


def with_even(array):
    return lax.ppermute(array, "tp", [(i, i ^ 2) for i in range(2 * NY)])


def with_odd(array):
    pairs = [(y * 2 + c, (NY - 1 - y) * 2 + c) for y in range(NY) for c in range(2)]
    return lax.ppermute(array, "tp", pairs)


def add(a, b):
    return (a.astype(F32) + b.astype(F32)).astype(BF16)


def home(deltas):
    return [deltas[0]] + [along_x(deltas[e], -e) for e in (1, 2, 3)]


def body(tokens, weight, down, up, ident, store):
    index, part = lax.axis_index("ad"), lax.axis_index("tp")
    place = jnp.stack([index >> 3, index & 7, part & 1]).astype(I32)
    groups = [[x * NZ + z for z in range(NZ)] for x in range(NX)]

    cw1, ccw1 = along_z(down, 1), along_z(down, -1)
    row, col = route(place, ident.reshape(1, -1), store.reshape(1, -1))
    packed = {e: pack(e, row, tokens) for e in (2, 1, 3)}
    moved = {e: along_x(packed[e], e) for e in (2, 1, 3)}
    xs = [pack(0, row, tokens)] + [moved[e] for e in (1, 2, 3)]
    ups = lax.all_gather(up, "ad", axis_index_groups=groups, tiled=True)

    partial_base = base(tokens, weight, lax.axis_size("tp"), *packed.values())
    cw1, ccw1, partial_base = lax.optimization_barrier((cw1, ccw1, partial_base))
    summed = lax.psum_scatter(partial_base, "tp", scatter_dimension=0, tiled=True)[0]
    cw2, ccw2 = along_z(cw1, 1), along_z(ccw1, -1)
    cw3, ccw3 = along_z(cw2, 1), along_z(ccw2, -1)
    upward, downward = carve(xs)
    guests = [along_z(upward, 1), along_z(downward, -1)]

    keep, send = shrink_near(place, xs, [down, cw1, ccw1, cw2, ccw2], upward)
    near_chip = add(keep, with_core(send))
    near_pair = add(near_chip, with_even(near_chip))
    near = add(near_pair, with_odd(near_pair))
    near = home(expand_near(place, near, with_core(near), ups, near_chip))

    late = shrink_far(xs, [cw3, ccw3], near_chip, ups)
    late = shrink_late(late, guests, [cw3, ccw3], near_pair)
    late = add(late, with_core(late))
    late = add(late, with_even(late))
    total = gather(col, summed, near)
    late = home(expand_late(place, late, with_odd(late), ups, total))
    opposite = [d[FAR_ROWS:] for d in late]
    back = [along_z(jnp.stack(opposite[:2]), -1), along_z(jnp.stack(opposite[2:]), 1)]

    out = finish(col, total, late, back)
    return out.reshape(tokens.shape[0], 2, 128)


def solution(mesh):
    return jax.shard_map(
        body,
        mesh=mesh,
        in_specs=(
            P("ad", "tp"),
            P(None, "tp", None),
            P("ad", "tp", None),
            P("ad", None, None, "tp"),
            P("ad", None),
            P(),
        ),
        out_specs=P("ad", None, "tp"),
        check_vma=False,
    )
```

time: 183 us -> 172 us (0.940)
  Pallas kernels: 58.9 us -> 41.6 us
  starting transfers between devices: 49.1 us -> 39.3 us
  waiting for transfers between devices: 52.3 us -> 61.9 us
  local copies, waits for them, and re-layouts: 1.97 us -> 7.46 us
    pallas_call x10 -> x13, Pallas kernels: 56.2 us -> 38.8 us  [the longest x4 11.3 us: pack(): pl.pallas_call(functools.partial(pack_kernel, e), out_shape=jax.ShapeDtyp...]
    ppermute x8 -> x10, waiting for transfers between devices: 20.8 us -> 35.8 us  [along_z(): return lax.ppermute(array, 'ad', pairs)]
    ppermute x12 -> x7, waiting for transfers between devices: 20.1 us -> 8.28 us  [the longest x2 6.85 us: with_even(): return lax.ppermute(array, 'tp', [(i, i ^ 2) for i in range(2 * NY)])]
    reduce_scatter x1, waiting for transfers between devices: 0.03 us -> 9.64 us  [body(): lax.psum_scatter(partial_base, 'tp', scatter_dimension=0, tiled=True)[0]]
    ppermute x12 -> x7, starting transfers between devices: 18.9 us -> 10.5 us  [the longest x2 6.3 us: with_odd(): return lax.ppermute(array, 'tp', pairs)]
    unnamed x50 -> x32, local copies, waits for them, and re-layouts: 1.9 us -> 7.45 us
    ppermute x12 -> x9, starting transfers between devices: 17.7 us -> 13.8 us  [along_x(): return lax.ppermute(array, 'ad', pairs)]
    ppermute x12 -> x9, waiting for transfers between devices: 11.3 us -> 8.12 us  [along_x(): return lax.ppermute(array, 'ad', pairs)]
  transfers between devices with their start and end apart: 34 -> 28, of which waited for: 9 -> 12; matrix products, arithmetic and copies ran while one was open for 2% -> 2% of each run, Pallas kernels for 30% -> 23%
where the time goes in v2:
time: 172 us; the launch traced here: 168 us
  waiting for transfers between devices  61.9 us (36%)
  Pallas kernels  41.6 us (24%)
  starting transfers between devices  39.3 us (23%)
  between operations  15.1 us (9%)
  local copies, waits for them, and re-layouts  7.46 us (4%)
  other arithmetic  2.83 us (2%)
    ppermute x10, waiting for transfers between devices, along_z(): return lax.ppermute(array, 'ad', pairs)  35.8 us
    ppermute x10, starting transfers between devices, along_z(): return lax.ppermute(array, 'ad', pairs)  15 us
    ppermute x9, starting transfers between devices, along_x(): return lax.ppermute(array, 'ad', pairs)  13.8 us
    pallas_call x4, Pallas kernels, pack(): pl.pallas_call(functools.partial(pack_kernel, e), out_shape=jax.ShapeDtyp...  11.3 us
    pallas_call x1, Pallas kernels, base(): pl.pallas_call(base_kernel, grid=(parts // step,), out_shape=jax.ShapeDty...  10.7 us
    reduce_scatter x1, waiting for transfers between devices, body(): lax.psum_scatter(partial_base, 'tp', scatter_dimension=0, tiled=True)[0]  9.64 us
    ppermute x9, waiting for transfers between devices, along_x(): return lax.ppermute(array, 'ad', pairs)  8.12 us
    unnamed x32, local copies, waits for them, and re-layouts  7.45 us
  transfers between devices with their start and end apart: 28, of which 12 were waited for; matrix products, arithmetic and copies ran while one was open for 2% of the time, Pallas kernels for 23%

profile of v2, /device:TPU:64, one launch (start us, length us, event | category | flops | bytes accessed | tf_op | source)
XLA Modules:
  0.0 168.2 jit_solution(5522465023902867503)
XLA Ops:
  10.1 2.8 %route.1 = (s32[1,1536]{1,0:T(1,128)}, s32[1536,128]{1,0:T(8,128)}) custom-call(s32[3]{0:T(128)} %pad_add_fusion.place_ref, s32[1,1536]{1,0:T(1,128)} %bitcast.16, s32[1,128]{1,0:T(1,128)} %bitcast.17), custom_call_target="tpu_custom_call" | custom-call | flops 3300000000 | bytes 1000 | tf_op jit(solution)/shard_map/route/pallas_call | solution.py:95
  13.5 3.1 %pack.5.refs_1_ = bf16[592,1024]{1,0:T(8,128)(2,1)} custom-call(s32[1,1536]{1,0:T(1,128)S(1)} %copy-done.14, bf16[1536,1024]{1,0:T(8,128)(2,1)S(1)} %copy-done.6), custom_call_target="tpu_custom_call" | custom-call | flops 3300000000 | bytes 1000 | tf_op jit(solution)/shard_map/pack/pallas_call | solution.py:117
  18.1 3.1 %pack.4.refs_0_ = bf16[592,1024]{1,0:T(8,128)(2,1)} custom-call(s32[1,1536]{1,0:T(1,128)S(1)} %copy-done.14, bf16[1536,1024]{1,0:T(8,128)(2,1)S(1)} %copy-done.6), custom_call_target="tpu_custom_call" | custom-call | flops 3300000000 | bytes 1000 | tf_op jit(solution)/shard_map/pack/pallas_call | solution.py:117
  21.2 2.7 %collective-permute-start.3 = (bf16[592,1024]{1,0:T(8,128)(2,1)}, bf16[592,1024]{1,0:T(8,128)(2,1)S(1)}, u32[]{:S(2)}, u32[]{:S(2)}) collective-permute-start(bf16[592,1024]{1,0:T(8,128)(2,1)} %pack.4.refs_0_), channel_id=1, source_target_pairs={{0,128},{8,136},{16,144},{24,152},{32,160},{40,168},{48,176},{56,1... | collective-permute-start | bytes 3637256 | tf_op jit(solution)/shard_map/ppermute | solution.py:477
  23.9 3.1 %pack.6.refs_2_ = bf16[592,1024]{1,0:T(8,128)(2,1)} custom-call(s32[1,1536]{1,0:T(1,128)S(1)} %copy-done.14, bf16[1536,1024]{1,0:T(8,128)(2,1)S(1)} %copy-done.6), custom_call_target="tpu_custom_call" | custom-call | flops 3300000000 | bytes 1000 | tf_op jit(solution)/shard_map/pack/pallas_call | solution.py:117
  28.5 10.7 %base.1 = bf16[8,1536,256]{2,1,0:T(8,128)(2,1)} custom-call(bf16[1536,1024]{1,0:T(8,128)(2,1)} %tok_ref.9, bf16[2,1024,1024]{2,1,0:T(8,128)(2,1)} %w_ref.1, bf16[592,1024]{1,0:T(8,128)(2,1)} %pack.4.refs_0_, bf16[592,1024]{1,0:T(8,128)(2,1)} %pack.5.refs_1_, bf16[592,1024]{1,0:T(8,128)(2,1)} %pack.6.refs_2_), custom_call_target="tpu_custom_call" | custom-call | flops 12099999744 | bytes 1000 | tf_op jit(solution)/shard_map/base/pallas_call | solution.py:139
  39.1 3.1 %collective-permute-start.5 = (bf16[4,1024,128]{2,1,0:T(8,128)(2,1)S(1)}, bf16[4,1024,128]{2,1,0:T(8,128)(2,1)}, u32[]{:S(2)}, u32[]{:S(2)}) collective-permute-start(bf16[4,1024,128]{2,1,0:T(8,128)(2,1)S(1)} %collective-permute-done.refs_5_), channel_id=1, source_target_pairs={{0,8},{8,16},{16,24},{24,32},{32,40},{40,48},{48,56},{56,0},{64,72... | collective-permute-start | bytes 3145736 | tf_op jit(solution)/shard_map/ppermute | solution.py:472
  46.3 23.3 %collective-permute-done.5.refs_7_ = bf16[4,1024,128]{2,1,0:T(8,128)(2,1)} collective-permute-done((bf16[4,1024,128]{2,1,0:T(8,128)(2,1)S(1)}, bf16[4,1024,128]{2,1,0:T(8,128)(2,1)}, u32[]{:S(2)}, u32[]{:S(2)}) %collective-permute-start.5) | collective-permute-done | bytes 1048608 | tf_op jit(solution)/shard_map/ppermute | solution.py:472
  69.6 4.5 %collective-permute-start.14 = (bf16[4,1024,128]{2,1,0:T(8,128)(2,1)}, bf16[4,1024,128]{2,1,0:T(8,128)(2,1)}, u32[]{:S(2)}, u32[]{:S(2)}) collective-permute-start(bf16[4,1024,128]{2,1,0:T(8,128)(2,1)} %collective-permute-done.5.refs_7_), channel_id=1, source_target_pairs={{0,8},{8,16},{16,24},{24,32},{32,40},{40,48},{48,56},{56,0},{64,72... | collective-permute-start | bytes 3145736 | tf_op jit(solution)/shard_map/ppermute | solution.py:472
  76.9 4.2 %shrink_near.1 = (bf16[2,368,128]{2,1,0:T(8,128)(2,1)S(1)}, bf16[2,368,128]{2,1,0:T(8,128)(2,1)S(1)}) custom-call(s32[3]{0:T(128)S(1)} %copy-done.5, bf16[592,1024]{1,0:T(8,128)(2,1)S(1)} %pack.7.refs_0_, bf16[592,1024]{1,0:T(8,128)(2,1)S(1)} %collective-permute-done.2.refs_1_, bf16[592,1024]{1,0:T(8,128)(2,1)S(1)} %collective-permute-done.3.refs_2_, ...), custom_call_target="tpu_custom_call" | custom-call | flops 1100000000 | bytes 1000 | tf_op jit(solution)/shard_map/shrink_near/pallas_call | solution.py:201
  84.4 3.2 %collective-permute-start.16 = (bf16[2,80,1024]{2,1,0:T(8,128)(2,1)S(1)}, bf16[2,80,1024]{2,1,0:T(8,128)(2,1)}, u32[]{:S(2)}, u32[]{:S(2)}) collective-permute-start(bf16[2,80,1024]{2,1,0:T(8,128)(2,1)S(1)} %copy-done.4), channel_id=1, source_target_pairs={{0,8},{8,16},{16,24},{24,32},{32,40},{40,48},{48,56},{56,0},{64,72... | collective-permute-start | bytes 983048 | tf_op jit(solution)/shard_map/ppermute | solution.py:472
  90.6 3.1 %collective-permute-start.9 = (bf16[2,368,128]{2,1,0:T(8,128)(2,1)S(1)}, bf16[2,368,128]{2,1,0:T(8,128)(2,1)}, u32[]{:S(2)}, u32[]{:S(2)}) collective-permute-start(bf16[2,368,128]{2,1,0:T(8,128)(2,1)S(1)} %add_convert_fusion.3._), channel_id=1, source_target_pairs={{0,6},{1,7},{2,4},{3,5},{4,2},{5,3},{6,0},{7,1},{8,14},{9,15},{10,... | collective-permute-start | bytes 565256 | tf_op jit(solution)/shard_map/ppermute | solution.py:490
  93.7 5.7 %collective-permute-done.14.refs_4_.low_ref = bf16[4,1024,128]{2,1,0:T(8,128)(2,1)} collective-permute-done((bf16[4,1024,128]{2,1,0:T(8,128)(2,1)}, bf16[4,1024,128]{2,1,0:T(8,128)(2,1)}, u32[]{:S(2)}, u32[]{:S(2)}) %collective-permute-start.14) | collective-permute-done | bytes 1048608 | tf_op jit(solution)/shard_map/ppermute | solution.py:472
  99.4 3.8 %collective-permute-done.15.refs_5_.high_ref = bf16[4,1024,128]{2,1,0:T(8,128)(2,1)} collective-permute-done((bf16[4,1024,128]{2,1,0:T(8,128)(2,1)}, bf16[4,1024,128]{2,1,0:T(8,128)(2,1)}, u32[]{:S(2)}, u32[]{:S(2)}) %collective-permute-start.15) | collective-permute-done | bytes 1048608 | tf_op jit(solution)/shard_map/ppermute | solution.py:472
  105.8 2.5 %shrink_far.1.far_ref = bf16[4,144,128]{2,1,0:T(8,128)(2,1)S(1)} custom-call(bf16[592,1024]{1,0:T(8,128)(2,1)S(1)} %copy-done.1, bf16[592,1024]{1,0:T(8,128)(2,1)S(1)} %collective-permute-done.2.refs_1_, bf16[592,1024]{1,0:T(8,128)(2,1)S(1)} %collective-permute-done.3.refs_2_, bf16[592,1024]{1,0:T(8,128)(2,1)} %collective-permute-done.4.refs_3_, ...), custom_call_target="tpu_custom_call" | custom-call | flops 131999997952 | bytes 1000 | tf_op jit(solution)/shard_map/shrink_far/pallas_call | solution.py:249
  108.3 2.3 %shrink_late.1 = bf16[4,224,128]{2,1,0:T(8,128)(2,1)S(1)} custom-call(bf16[4,144,128]{2,1,0:T(8,128)(2,1)S(1)} %shrink_far.1.far_ref, bf16[2,80,1024]{2,1,0:T(8,128)(2,1)} %collective-permute-done.16.from_low, bf16[2,80,1024]{2,1,0:T(8,128)(2,1)} %collective-permute-done.17.from_high, bf16[4,1024,128]{2,1,0:T(8,128)(2,1)} %collective-permute-done.14.refs_4_.low_ref, ...), custom_call_target="tpu_custom_call" | custom-call | flops 3300000000 | bytes 1000 | tf_op jit(solution)/shard_map/shrink_late/pallas_call | solution.py:276
  115.9 2.3 %collective-permute-start.12 = (bf16[368,256]{1,0:T(8,128)(2,1)S(1)}, bf16[368,256]{1,0:T(8,128)(2,1)S(1)}, u32[]{:S(2)}, u32[]{:S(2)}) collective-permute-start(bf16[368,256]{1,0:T(8,128)(2,1)S(1)} %get-tuple-element.32), channel_id=1, source_target_pairs={{0,128},{8,136},{16,144},{24,152},{32,160},{40,168},{48,176},{56,1... | collective-permute-start | bytes 565256 | tf_op jit(solution)/shard_map/ppermute | solution.py:477
  118.2 4.8 %collective-permute-done.19 = bf16[4,224,128]{2,1,0:T(8,128)(2,1)S(1)} collective-permute-done((bf16[4,224,128]{2,1,0:T(8,128)(2,1)S(1)}, bf16[4,224,128]{2,1,0:T(8,128)(2,1)S(1)}, u32[]{:S(2)}, u32[]{:S(2)}) %collective-permute-start.19) | collective-permute-done | bytes 229408 | tf_op jit(solution)/shard_map/ppermute | solution.py:485
  123.0 3.2 %collective-permute-start.20 = (bf16[4,224,128]{2,1,0:T(8,128)(2,1)S(1)}, bf16[4,224,128]{2,1,0:T(8,128)(2,1)S(1)}, u32[]{:S(2)}, u32[]{:S(2)}) collective-permute-start(bf16[4,224,128]{2,1,0:T(8,128)(2,1)S(1)} %add_convert_fusion.mine_ref), channel_id=1, source_target_pairs={{0,6},{1,7},{2,4},{3,5},{4,2},{5,3},{6,0},{7,1},{8,14},{9,15},{10,... | collective-permute-start | bytes 688136 | tf_op jit(solution)/shard_map/ppermute | solution.py:490
  127.7 9.6 %reduce-scatter.2.cloned.1.call-done = bf16[1,1536,256]{2,1,0:T(8,128)(2,1)} async-done(((bf16[8,1536,256]{2,1,0:T(8,128)(2,1)}), bf16[1,1536,256]{2,1,0:T(8,128)(2,1)}) %reduce-scatter.2.cloned.1.call-update) | async-done | bytes 786448 | tf_op jit(solution)/shard_map/reduce_scatter | solution.py:515
  142.7 3.4 %collective-permute-start.21 = (bf16[224,256]{1,0:T(8,128)(2,1)S(1)}, bf16[224,256]{1,0:T(8,128)(2,1)S(1)}, u32[]{:S(2)}, u32[]{:S(2)}) collective-permute-start(bf16[224,256]{1,0:T(8,128)(2,1)S(1)} %get-tuple-element.36), channel_id=1, source_target_pairs={{0,192},{8,200},{16,208},{24,216},{32,224},{40,232},{48,240},{56,2... | collective-permute-start | bytes 344072 | tf_op jit(solution)/shard_map/ppermute | solution.py:477
  150.8 2.9 %collective-permute-done.23.refs_3_ = bf16[224,256]{1,0:T(8,128)(2,1)S(1)} collective-permute-done((bf16[224,256]{1,0:T(8,128)(2,1)S(1)}, bf16[224,256]{1,0:T(8,128)(2,1)S(1)}, u32[]{:S(2)}, u32[]{:S(2)}) %collective-permute-start.23) | collective-permute-done | bytes 114720 | tf_op jit(solution)/shard_map/ppermute | solution.py:477
  155.2 3.0 %collective-permute-done.25.refs_5_ = bf16[2,80,256]{2,1,0:T(8,128)(2,1)S(1)} collective-permute-done((bf16[2,80,256]{2,1,0:T(8,128)(2,1)S(1)}, bf16[2,80,256]{2,1,0:T(8,128)(2,1)S(1)}, u32[]{:S(2)}, u32[]{:S(2)}) %collective-permute-start.25) | collective-permute-done | bytes 81952 | tf_op jit(solution)/shard_map/ppermute | solution.py:472
  158.2 2.6 %finish.1 = bf16[3072,128]{1,0:T(8,128)(2,1)} custom-call(s32[1536,128]{1,0:T(8,128)S(1)} %copy-done.13, f32[1536,256]{1,0:T(8,128)S(1)} %gather.1._.total_ref, bf16[224,256]{1,0:T(8,128)(2,1)S(1)} %get-tuple-element.35.refs_0_, bf16[224,256]{1,0:T(8,128)(2,1)S(1)} %collective-permute-done.21.refs_1_, bf16[224,256]{1,0:T(8,128)(2,1)S(1)} %collective-permute-done.22.refs_2_, ...), custom_call_target="tpu_custom_call" | custom-call | flops 5500000256 | bytes 1000 | tf_op jit(solution)/shard_map/finish/pallas_call | solution.py:449
  (92 shorter events, 40.1 us)
Async XLA Ops:
  7.4 86.4 %all-gather.2.cloned.1.call-start = ((), (), s32[]{:S(2)}) async-start(), calls=%async_computation.2 | async-start | bytes 1179648 | tf_op jit(solution)/shard_map/all_gather | solution.py:511
  7.4 31.8 %collective-permute-start = (bf16[4,1024,128]{2,1,0:T(8,128)(2,1)}, bf16[4,1024,128]{2,1,0:T(8,128)(2,1)S(1)}, u32[]{:S(2)}, u32[]{:S(2)}) collective-permute-start(bf16[4,1024,128]{2,1,0:T(8,128)(2,1)} %refs_4_.1), channel_id=1, source_target_pairs={{0,8},{8,16},{16,24},{24,32},{32,40},{40,48},{48,56},{56,0},{64,72... | collective-permute-start | bytes 3145736 | tf_op jit(solution)/shard_map/ppermute | solution.py:472
  9.3 29.8 %collective-permute-start.1 = (bf16[4,1024,128]{2,1,0:T(8,128)(2,1)}, bf16[4,1024,128]{2,1,0:T(8,128)(2,1)}, u32[]{:S(2)}, u32[]{:S(2)}) collective-permute-start(bf16[4,1024,128]{2,1,0:T(8,128)(2,1)} %refs_4_.1), channel_id=1, source_target_pairs={{0,56},{8,0},{16,8},{24,16},{32,24},{40,32},{48,40},{56,48},{64,12... | collective-permute-start | bytes 3145736 | tf_op jit(solution)/shard_map/ppermute | solution.py:472
  16.6 57.5 %collective-permute-start.2 = (bf16[592,1024]{1,0:T(8,128)(2,1)}, bf16[592,1024]{1,0:T(8,128)(2,1)S(1)}, u32[]{:S(2)}, u32[]{:S(2)}) collective-permute-start(bf16[592,1024]{1,0:T(8,128)(2,1)} %pack.5.refs_1_), channel_id=1, source_target_pairs={{0,64},{8,72},{16,80},{24,88},{32,96},{40,104},{48,112},{56,120},{... | collective-permute-start | bytes 3637256 | tf_op jit(solution)/shard_map/ppermute | solution.py:477
  21.2 52.9 %collective-permute-start.3 = (bf16[592,1024]{1,0:T(8,128)(2,1)}, bf16[592,1024]{1,0:T(8,128)(2,1)S(1)}, u32[]{:S(2)}, u32[]{:S(2)}) collective-permute-start(bf16[592,1024]{1,0:T(8,128)(2,1)} %pack.4.refs_0_), channel_id=1, source_target_pairs={{0,128},{8,136},{16,144},{24,152},{32,160},{40,168},{48,176},{56,1... | collective-permute-start | bytes 3637256 | tf_op jit(solution)/shard_map/ppermute | solution.py:477
  27.0 48.8 %collective-permute-start.4 = (bf16[592,1024]{1,0:T(8,128)(2,1)}, bf16[592,1024]{1,0:T(8,128)(2,1)}, u32[]{:S(2)}, u32[]{:S(2)}) collective-permute-start(bf16[592,1024]{1,0:T(8,128)(2,1)} %pack.6.refs_2_), channel_id=1, source_target_pairs={{0,192},{8,200},{16,208},{24,216},{32,224},{40,232},{48,240},{56,2... | collective-permute-start | bytes 3637256 | tf_op jit(solution)/shard_map/ppermute | solution.py:477
  39.1 30.5 %collective-permute-start.5 = (bf16[4,1024,128]{2,1,0:T(8,128)(2,1)S(1)}, bf16[4,1024,128]{2,1,0:T(8,128)(2,1)}, u32[]{:S(2)}, u32[]{:S(2)}) collective-permute-start(bf16[4,1024,128]{2,1,0:T(8,128)(2,1)S(1)} %collective-permute-done.refs_5_), channel_id=1, source_target_pairs={{0,8},{8,16},{16,24},{24,32},{32,40},{40,48},{48,56},{56,0},{64,72... | collective-permute-start | bytes 3145736 | tf_op jit(solution)/shard_map/ppermute | solution.py:472
  42.2 31.9 %collective-permute-start.6 = (bf16[4,1024,128]{2,1,0:T(8,128)(2,1)}, bf16[4,1024,128]{2,1,0:T(8,128)(2,1)}, u32[]{:S(2)}, u32[]{:S(2)}) collective-permute-start(bf16[4,1024,128]{2,1,0:T(8,128)(2,1)} %collective-permute-done.1.refs_6_), channel_id=1, source_target_pairs={{0,56},{8,0},{16,8},{24,16},{32,24},{40,32},{48,40},{56,48},{64,12... | collective-permute-start | bytes 3145736 | tf_op jit(solution)/shard_map/ppermute | solution.py:472
  42.2 95.1 %reduce-scatter.2.cloned.1.call-start = ((), (), s32[]{:S(2)}) async-start(), calls=%async_computation.1 | async-start | bytes 7077888 | tf_op jit(solution)/shard_map/reduce_scatter | solution.py:515
  69.6 29.8 %collective-permute-start.14 = (bf16[4,1024,128]{2,1,0:T(8,128)(2,1)}, bf16[4,1024,128]{2,1,0:T(8,128)(2,1)}, u32[]{:S(2)}, u32[]{:S(2)}) collective-permute-start(bf16[4,1024,128]{2,1,0:T(8,128)(2,1)} %collective-permute-done.5.refs_7_), channel_id=1, source_target_pairs={{0,8},{8,16},{16,24},{24,32},{32,40},{40,48},{48,56},{56,0},{64,72... | collective-permute-start | bytes 3145736 | tf_op jit(solution)/shard_map/ppermute | solution.py:472
  74.1 29.1 %collective-permute-start.15 = (bf16[4,1024,128]{2,1,0:T(8,128)(2,1)}, bf16[4,1024,128]{2,1,0:T(8,128)(2,1)}, u32[]{:S(2)}, u32[]{:S(2)}) collective-permute-start(bf16[4,1024,128]{2,1,0:T(8,128)(2,1)} %collective-permute-done.6.refs_8_), channel_id=1, source_target_pairs={{0,56},{8,0},{16,8},{24,16},{32,24},{40,32},{48,40},{56,48},{64,12... | collective-permute-start | bytes 3145736 | tf_op jit(solution)/shard_map/ppermute | solution.py:472
  82.7 7.0 %collective-permute-start.8 = (bf16[2,368,128]{2,1,0:T(8,128)(2,1)S(1)}, bf16[2,368,128]{2,1,0:T(8,128)(2,1)}, u32[]{:S(2)}, u32[]{:S(2)}) collective-permute-start(bf16[2,368,128]{2,1,0:T(8,128)(2,1)S(1)} %add_convert_fusion.4._.refs_6_), channel_id=1, source_target_pairs={{0,2},{1,3},{2,0},{3,1},{4,6},{5,7},{6,4},{7,5},{8,10},{9,11},{10,... | collective-permute-start | bytes 565256 | tf_op jit(solution)/shard_map/ppermute | solution.py:485
  84.4 23.9 %collective-permute-start.16 = (bf16[2,80,1024]{2,1,0:T(8,128)(2,1)S(1)}, bf16[2,80,1024]{2,1,0:T(8,128)(2,1)}, u32[]{:S(2)}, u32[]{:S(2)}) collective-permute-start(bf16[2,80,1024]{2,1,0:T(8,128)(2,1)S(1)} %copy-done.4), channel_id=1, source_target_pairs={{0,8},{8,16},{16,24},{24,32},{32,40},{40,48},{48,56},{56,0},{64,72... | collective-permute-start | bytes 983048 | tf_op jit(solution)/shard_map/ppermute | solution.py:472
  87.6 20.7 %collective-permute-start.17 = (bf16[2,80,1024]{2,1,0:T(8,128)(2,1)S(1)}, bf16[2,80,1024]{2,1,0:T(8,128)(2,1)}, u32[]{:S(2)}, u32[]{:S(2)}) collective-permute-start(bf16[2,80,1024]{2,1,0:T(8,128)(2,1)S(1)} %copy-done.12), channel_id=1, source_target_pairs={{0,56},{8,0},{16,8},{24,16},{32,24},{40,32},{48,40},{56,48},{64,12... | collective-permute-start | bytes 983048 | tf_op jit(solution)/shard_map/ppermute | solution.py:472
  90.6 20.1 %collective-permute-start.9 = (bf16[2,368,128]{2,1,0:T(8,128)(2,1)S(1)}, bf16[2,368,128]{2,1,0:T(8,128)(2,1)}, u32[]{:S(2)}, u32[]{:S(2)}) collective-permute-start(bf16[2,368,128]{2,1,0:T(8,128)(2,1)S(1)} %add_convert_fusion.3._), channel_id=1, source_target_pairs={{0,6},{1,7},{2,4},{3,5},{4,2},{5,3},{6,0},{7,1},{8,14},{9,15},{10,... | collective-permute-start | bytes 565256 | tf_op jit(solution)/shard_map/ppermute | solution.py:490
  112.4 10.6 %collective-permute-start.19 = (bf16[4,224,128]{2,1,0:T(8,128)(2,1)S(1)}, bf16[4,224,128]{2,1,0:T(8,128)(2,1)S(1)}, u32[]{:S(2)}, u32[]{:S(2)}) collective-permute-start(bf16[4,224,128]{2,1,0:T(8,128)(2,1)S(1)} %add_convert_fusion.1), channel_id=1, source_target_pairs={{0,2},{1,3},{2,0},{3,1},{4,6},{5,7},{6,4},{7,5},{8,10},{9,11},{10,... | collective-permute-start | bytes 688136 | tf_op jit(solution)/shard_map/ppermute | solution.py:485
  115.4 10.8 %collective-permute-start.11 = (bf16[368,256]{1,0:T(8,128)(2,1)S(1)}, bf16[368,256]{1,0:T(8,128)(2,1)S(1)}, u32[]{:S(2)}, u32[]{:S(2)}) collective-permute-start(bf16[368,256]{1,0:T(8,128)(2,1)S(1)} %get-tuple-element.31), channel_id=1, source_target_pairs={{0,192},{8,200},{16,208},{24,216},{32,224},{40,232},{48,240},{56,2... | collective-permute-start | bytes 565256 | tf_op jit(solution)/shard_map/ppermute | solution.py:477
  115.9 10.4 %collective-permute-start.12 = (bf16[368,256]{1,0:T(8,128)(2,1)S(1)}, bf16[368,256]{1,0:T(8,128)(2,1)S(1)}, u32[]{:S(2)}, u32[]{:S(2)}) collective-permute-start(bf16[368,256]{1,0:T(8,128)(2,1)S(1)} %get-tuple-element.32), channel_id=1, source_target_pairs={{0,128},{8,136},{16,144},{24,152},{32,160},{40,168},{48,176},{56,1... | collective-permute-start | bytes 565256 | tf_op jit(solution)/shard_map/ppermute | solution.py:477
  118.2 9.6 %collective-permute-start.13 = (bf16[368,256]{1,0:T(8,128)(2,1)S(1)}, bf16[368,256]{1,0:T(8,128)(2,1)S(1)}, u32[]{:S(2)}, u32[]{:S(2)}) collective-permute-start(bf16[368,256]{1,0:T(8,128)(2,1)S(1)} %get-tuple-element.33), channel_id=1, source_target_pairs={{0,64},{8,72},{16,80},{24,88},{32,96},{40,104},{48,112},{56,120},{... | collective-permute-start | bytes 565256 | tf_op jit(solution)/shard_map/ppermute | solution.py:477
  123.0 18.6 %collective-permute-start.20 = (bf16[4,224,128]{2,1,0:T(8,128)(2,1)S(1)}, bf16[4,224,128]{2,1,0:T(8,128)(2,1)S(1)}, u32[]{:S(2)}, u32[]{:S(2)}) collective-permute-start(bf16[4,224,128]{2,1,0:T(8,128)(2,1)S(1)} %add_convert_fusion.mine_ref), channel_id=1, source_target_pairs={{0,6},{1,7},{2,4},{3,5},{4,2},{5,3},{6,0},{7,1},{8,14},{9,15},{10,... | collective-permute-start | bytes 688136 | tf_op jit(solution)/shard_map/ppermute | solution.py:490
  142.7 7.4 %collective-permute-start.21 = (bf16[224,256]{1,0:T(8,128)(2,1)S(1)}, bf16[224,256]{1,0:T(8,128)(2,1)S(1)}, u32[]{:S(2)}, u32[]{:S(2)}) collective-permute-start(bf16[224,256]{1,0:T(8,128)(2,1)S(1)} %get-tuple-element.36), channel_id=1, source_target_pairs={{0,192},{8,200},{16,208},{24,216},{32,224},{40,232},{48,240},{56,2... | collective-permute-start | bytes 344072 | tf_op jit(solution)/shard_map/ppermute | solution.py:477
  146.1 7.5 %collective-permute-start.22 = (bf16[224,256]{1,0:T(8,128)(2,1)S(1)}, bf16[224,256]{1,0:T(8,128)(2,1)S(1)}, u32[]{:S(2)}, u32[]{:S(2)}) collective-permute-start(bf16[224,256]{1,0:T(8,128)(2,1)S(1)} %get-tuple-element.37), channel_id=1, source_target_pairs={{0,128},{8,136},{16,144},{24,152},{32,160},{40,168},{48,176},{56,1... | collective-permute-start | bytes 344072 | tf_op jit(solution)/shard_map/ppermute | solution.py:477
  146.7 6.9 %collective-permute-start.23 = (bf16[224,256]{1,0:T(8,128)(2,1)S(1)}, bf16[224,256]{1,0:T(8,128)(2,1)S(1)}, u32[]{:S(2)}, u32[]{:S(2)}) collective-permute-start(bf16[224,256]{1,0:T(8,128)(2,1)S(1)} %get-tuple-element.38), channel_id=1, source_target_pairs={{0,64},{8,72},{16,80},{24,88},{32,96},{40,104},{48,112},{56,120},{... | collective-permute-start | bytes 344072 | tf_op jit(solution)/shard_map/ppermute | solution.py:477
  150.1 5.0 %collective-permute-start.24 = (bf16[2,80,256]{2,1,0:T(8,128)(2,1)S(1)}, bf16[2,80,256]{2,1,0:T(8,128)(2,1)S(1)}, u32[]{:S(2)}, u32[]{:S(2)}) collective-permute-start(bf16[2,80,256]{2,1,0:T(8,128)(2,1)S(1)} %pad_maximum_fusion), channel_id=1, source_target_pairs={{0,56},{8,0},{16,8},{24,16},{32,24},{40,32},{48,40},{56,48},{64,12... | collective-permute-start | bytes 245768 | tf_op jit(solution)/shard_map/ppermute | solution.py:472
  (20 other events, 144.5 us)
Sparse Core Ops, SparseCore 0:
  42.4 41.2 all-gather.1
Sparse Core Ops, SparseCore 1:
  84.5 52.8 reduce-scatter.1

commit v3 on v2

--- a/solution.py
+++ b/solution.py
@@ -32,8 +32,8 @@
 MIB = 1024 * 1024
 VMEM = 56 * MIB
 COST = {
-    "route": 3, "pack": 3, "base": 11, "carve": 1, "shrink_near": 1, "expand_near": 1,
-    "shrink_far": 120, "shrink_late": 3, "expand_late": 30, "gather": 5, "finish": 5,
+    "route": 3, "pack": 3, "base": 6, "carve": 1, "shrink_near": 3, "expand_near": 3,
+    "shrink_far": 100, "shrink_late": 3, "expand_late": 30, "gather": 5, "finish": 5,
 }
 VMEM = 56 * 1024 * 1024
 
@@ -62,7 +62,7 @@
     return pl.BlockSpec(memory_space=pltpu.SMEM)
 
 
-def route_kernel(place_ref, ids_ref, store_ref, row_ref, col_ref):
+def route_kernel(place_ref, ids_ref, store_ref, _, row_ref, col_ref):
     x, z = place_ref[0], place_ref[1]
     count = ids_ref.shape[1]
     ids = jnp.broadcast_to(ids_ref[...], (128, count))
@@ -90,7 +90,7 @@
     col_ref[...] = jnp.broadcast_to(row_ref[...], (128, count)).T
 
 
-def route(place, ids, store):
+def route(place, ids, store, earlier):
     count = ids.shape[1]
     return pl.pallas_call(
         route_kernel,
@@ -98,12 +98,12 @@
             jax.ShapeDtypeStruct((1, count), I32),
             jax.ShapeDtypeStruct((count, 128), I32),
         ),
-        in_specs=[scalars(), whole(), whole()],
+        in_specs=[scalars(), whole(), whole(), pl.BlockSpec(memory_space=pl.ANY)],
         out_specs=(whole(), whole()),
         compiler_params=params(),
         cost_estimate=cost(COST['route']),
         name="route",
-    )(place, ids, store)
+    )(place, ids, store, earlier)
 
 
 def pack_kernel(e, row_ref, tok_ref, out_ref):
@@ -125,31 +125,45 @@
     )(row, tokens)
 
 
-def base_kernel(tok_ref, w_ref, *refs):
-    out_ref = refs[-1]
-    for p in range(out_ref.shape[0]):
-        columns = slice(p * 128, (p + 1) * 128)
-        both = jnp.concatenate([w_ref[0, :, columns], w_ref[1, :, columns]], axis=1)
-        out_ref[p] = jnp.dot(tok_ref[...], both, preferred_element_type=F32).astype(BF16)
-
-
-def base(tokens, weight, parts, *earlier):
+def base_kernel(place_ref, tok_ref, w_ref, add_ref, out_ref):
+    both = jnp.concatenate([w_ref[0], w_ref[1]], axis=1)
+    y = jnp.dot(tok_ref[...], both, preferred_element_type=F32)
+    if add_ref is not None:
+        y = y + add_ref[0].astype(F32)
+    out_ref[0] = y.astype(BF16)
+
+
+def base(place, tokens, weight, mine, received=None, *earlier):
     count, width = tokens.shape
-    step = 2
-    return pl.pallas_call(
-        base_kernel,
-        grid=(parts // step,),
-        out_shape=jax.ShapeDtypeStruct((parts, count, 256), BF16),
-        in_specs=[
-            pl.BlockSpec((count, width), lambda i: (0, 0)),
-            pl.BlockSpec((2, width, step * 128), lambda i: (0, 0, i)),
-        ]
-        + [pl.BlockSpec(memory_space=pl.ANY)] * len(earlier),
-        out_specs=pl.BlockSpec((step, count, 256), lambda i: (i, 0, 0)),
+
+    def column(i, place_ref):
+        core = place_ref[2]
+        return (0, 0, i * 2 + (core if mine else 1 - core))
+
+    def kernel(place_ref, tok_ref, w_ref, *refs):
+        add_ref = None if received is None else refs[0]
+        base_kernel(place_ref, tok_ref, w_ref, add_ref, refs[-1])
+
+    block = pl.BlockSpec((1, count, 256), lambda i, _: (i, 0, 0))
+    extra = [] if received is None else [received]
+    return pl.pallas_call(
+        kernel,
+        grid_spec=pltpu.PrefetchScalarGridSpec(
+            num_scalar_prefetch=1,
+            grid=(NY,),
+            in_specs=[
+                pl.BlockSpec((count, width), lambda i, _: (0, 0)),
+                pl.BlockSpec((2, width, 128), column),
+            ]
+            + [block] * len(extra)
+            + [pl.BlockSpec(memory_space=pl.ANY)] * len(earlier),
+            out_specs=block,
+        ),
+        out_shape=jax.ShapeDtypeStruct((NY, count, 256), BF16),
         compiler_params=params("arbitrary"),
         cost_estimate=cost(COST["base"]),
         name="base",
-    )(tokens, weight, *earlier)
+    )(place, tokens, weight, *extra, *earlier)
 
 
 def adapter_of(skip, copies):
@@ -187,7 +201,7 @@
 
 def shrink_near_kernel(place_ref, *refs):
     xs, panels = refs[:NX], refs[NX : NX + len(NEAR)]
-    keep_ref, send_ref, total = refs[NX + len(NEAR) + 1 :]
+    keep_ref, send_ref, total = refs[-3:]
     total[...] = jnp.zeros_like(total)
     shrink_blocks(xs, panels, NEAR, total)
     core = place_ref[2]
@@ -195,7 +209,7 @@
     send_ref[...] = total[pl.ds(2 - core * 2, 2)].astype(BF16)
 
 
-def shrink_near(place, xs, panels, earlier):
+def shrink_near(place, xs, panels, *earlier):
     width = xs[0].shape[1]
     half = jax.ShapeDtypeStruct((2, NEAR_ROWS, 128), BF16)
     return pl.pallas_call(
@@ -204,14 +218,14 @@
         out_shape=(half, half),
         in_specs=[scalars()]
         + [pl.BlockSpec((pl.Element(NEAR_ROWS), pl.Element(width)), lambda i: (0, 0))] * NX
-        + [pl.BlockSpec(w.shape, lambda i: (0, 0, 0)) for w in panels]
-        + [pl.BlockSpec(memory_space=pl.ANY)],
+        + [pl.BlockSpec((LOCAL, width, 128), lambda i: (0, 0, 0)) for w in panels]
+        + [pl.BlockSpec(memory_space=pl.ANY)] * len(earlier),
         out_specs=(pl.BlockSpec(half.shape, lambda i: (0, 0, 0)),) * 2,
         scratch_shapes=[pltpu.VMEM((NX, NEAR_ROWS, 128), F32)],
-        compiler_params=params("arbitrary", limit=32 * MIB),
+        compiler_params=params("arbitrary"),
         cost_estimate=cost(COST["shrink_near"]),
         name="shrink_near",
-    )(place, *xs, *panels, earlier)
+    )(place, *xs, *panels, *earlier)
 
 
 def carve_kernel(*refs):
@@ -238,7 +252,7 @@
 
 def shrink_far_kernel(*refs):
     xs, panels = refs[:NX], refs[NX : NX + 2]
-    out_ref, total = refs[NX + 4 :]
+    out_ref, total = refs[-2:]
     total[...] = jnp.zeros_like(total)
     shrink_blocks(xs, panels, FAR, total)
     out_ref[...] = total[...].astype(BF16)
@@ -254,11 +268,11 @@
             pl.BlockSpec((pl.Element(FAR_ROWS), pl.Element(width)), lambda i: (NEAR_ROWS, 0))
         ]
         * NX
-        + [pl.BlockSpec(w.shape, lambda i: (0, 0, 0)) for w in panels]
+        + [pl.BlockSpec((LOCAL, width, 128), lambda i: (0, 0, 0)) for w in panels]
         + [pl.BlockSpec(memory_space=pl.ANY)] * len(earlier),
         out_specs=pl.BlockSpec((NX, FAR_ROWS, 128), lambda i: (0, 0, 0)),
         scratch_shapes=[pltpu.VMEM((NX, FAR_ROWS, 128), F32)],
-        compiler_params=params("arbitrary", limit=16 * MIB),
+        compiler_params=params("arbitrary"),
         cost_estimate=cost(COST["shrink_far"]),
         name="shrink_far",
     )(*xs, *panels, *earlier)
@@ -273,23 +287,31 @@
 
 
 def shrink_late(far, guests, panels, earlier):
+    width = guests[0].shape[2]
     return pl.pallas_call(
         shrink_late_kernel,
+        grid=(1,),
         out_shape=jax.ShapeDtypeStruct((NX, LATE_ROWS, 128), BF16),
-        in_specs=[whole()] * 5 + [pl.BlockSpec(memory_space=pl.ANY)],
-        out_specs=whole(),
-        compiler_params=params(limit=16 * MIB),
+        in_specs=[pl.BlockSpec(a.shape, lambda i: (0, 0, 0)) for a in (far, *guests)]
+        + [pl.BlockSpec((LOCAL, width, 128), lambda i: (0, 0, 0)) for w in panels]
+        + [pl.BlockSpec(memory_space=pl.ANY)],
+        out_specs=pl.BlockSpec((NX, LATE_ROWS, 128), lambda i: (0, 0, 0)),
+        compiler_params=params("arbitrary"),
         cost_estimate=cost(COST["shrink_late"]),
         name="shrink_late",
     )(far, *guests, *panels, earlier)
 
 
-def widen(up_ref, owner, wide_up):
+def widen(up_ref, wide_up):
     for a in range(LOCAL):
         for c in range(2):
             wide_up[a * 128 + c * 64 : a * 128 + c * 64 + 64, c * 128 : (c + 1) * 128] = up_ref[
-                owner * LOCAL + a, c
+                a, c * 64 : (c + 1) * 64
             ]
+
+
+def up_block(panel):
+    return pl.BlockSpec((LOCAL, 128, 128), lambda i: (0, panel.shape[1] // 128 - 1, 0))
 
 
 def expanded_rows(rows, wide_up, skip, copies):
@@ -300,15 +322,16 @@
     return jnp.dot(lhs, wide_up[...], preferred_element_type=F32)
 
 
-def expand_near_kernel(place_ref, mine_ref, other_ref, up_ref, _, *refs):
-    outs, wide_up, total, shrunk = refs[:NX], refs[NX], refs[NX + 1], refs[NX + 2]
-    z, core = place_ref[1], place_ref[2]
+def expand_near_kernel(place_ref, mine_ref, other_ref, *refs):
+    ups, outs = refs[: len(NEAR)], refs[len(NEAR) : len(NEAR) + NX]
+    wide_up, total, shrunk = refs[len(NEAR) + NX :]
+    core = place_ref[2]
     shrunk[pl.ds(core * 2, 2)] = mine_ref[...]
     shrunk[pl.ds(2 - core * 2, 2)] = other_ref[...]
     wide_up[...] = jnp.zeros_like(wide_up)
     total[...] = jnp.zeros_like(total)
     for k, low, skip in spans(NEAR):
-        widen(up_ref, (z + NEAR[k]) & (NZ - 1), wide_up)
+        widen(ups[k], wide_up)
         rows = jnp.concatenate([shrunk[e, low : low + WIDE] for e in range(NX)], axis=0)
         y = expanded_rows(rows, wide_up, skip, NX)
         for e in range(NX):
@@ -317,32 +340,34 @@
         outs[e][...] = total[e].astype(BF16)
 
 
-def expand_near(place, mine, other, up, earlier):
+def expand_near(place, mine, other, panels):
+    half = pl.BlockSpec(mine.shape, lambda i: (0, 0, 0))
     return pl.pallas_call(
         expand_near_kernel,
+        grid=(1,),
         out_shape=[jax.ShapeDtypeStruct((NEAR_ROWS, 256), BF16)] * NX,
-        in_specs=[scalars()] + [whole()] * 3 + [pl.BlockSpec(memory_space=pl.ANY)],
-        out_specs=[whole()] * NX,
+        in_specs=[scalars(), half, half] + [up_block(w) for w in panels],
+        out_specs=[pl.BlockSpec((NEAR_ROWS, 256), lambda i: (0, 0))] * NX,
         scratch_shapes=[
             pltpu.VMEM((LOCAL * 128, 256), BF16),
             pltpu.VMEM((NX, NEAR_ROWS, 256), F32),
             pltpu.VMEM((NX, NEAR_ROWS, 128), BF16),
         ],
-        compiler_params=params(limit=16 * MIB),
+        compiler_params=params("arbitrary", limit=24 * MIB),
         cost_estimate=cost(COST["expand_near"]),
         name="expand_near",
-    )(place, mine, other, up, earlier)
-
-
-def expand_late_kernel(place_ref, mine_ref, other_ref, up_ref, _, *refs):
-    outs, wides, total = refs[:NX], refs[NX : NX + 2], refs[NX + 2]
-    z = place_ref[1]
+    )(place, mine, other, *panels)
+
+
+def expand_late_kernel(mine_ref, other_ref, *refs):
+    ups, outs = refs[: len(FAR)], refs[len(FAR) + 1 : len(FAR) + 1 + NX]
+    wides, total = refs[-3:-1], refs[-1]
     shrunk = (mine_ref[...].astype(F32) + other_ref[...].astype(F32)).astype(BF16)
     total[...] = jnp.zeros_like(total)
     for k, low, skip in spans(FAR):
         wide_up = wides[k]
         wide_up[...] = jnp.zeros_like(wide_up)
-        widen(up_ref, (z + FAR[k]) & (NZ - 1), wide_up)
+        widen(ups[k], wide_up)
         rows = jnp.concatenate([shrunk[e, low : low + WIDE] for e in range(NX)], axis=0)
         y = expanded_rows(rows, wide_up, skip, NX)
         for e in range(NX):
@@ -356,21 +381,25 @@
         outs[e][...] = total[e].astype(BF16)
 
 
-def expand_late(place, mine, other, up, earlier):
+def expand_late(mine, other, panels, earlier):
+    full = pl.BlockSpec(mine.shape, lambda i: (0, 0, 0))
     return pl.pallas_call(
         expand_late_kernel,
+        grid=(1,),
         out_shape=[jax.ShapeDtypeStruct((LATE_ROWS, 256), BF16)] * NX,
-        in_specs=[scalars()] + [whole()] * 3 + [pl.BlockSpec(memory_space=pl.ANY)],
-        out_specs=[whole()] * NX,
+        in_specs=[full, full]
+        + [up_block(w) for w in panels]
+        + [pl.BlockSpec(memory_space=pl.ANY)],
+        out_specs=[pl.BlockSpec((LATE_ROWS, 256), lambda i: (0, 0))] * NX,
         scratch_shapes=[
             pltpu.VMEM((LOCAL * 128, 256), BF16),
             pltpu.VMEM((LOCAL * 128, 256), BF16),
             pltpu.VMEM((NX, LATE_ROWS, 256), F32),
         ],
-        compiler_params=params(limit=16 * MIB),
+        compiler_params=params("arbitrary", limit=24 * MIB),
         cost_estimate=cost(COST["expand_late"]),
         name="expand_late",
-    )(place, mine, other, up, earlier)
+    )(mine, other, *panels, earlier)
 
 
 def gather_kernel(col_ref, base_ref, *refs):
@@ -391,12 +420,13 @@
             (place >= e * NEAR_ROWS) & (place < filled), place + e * LATE_ROWS, slots
         )
     hot = (col_ref[:, :1] == slots).astype(BF16)
-    out_ref[...] = base_ref[...].astype(F32) + jnp.dot(
-        hot, table[...], preferred_element_type=F32
-    )
-
-
-def gather(col, summed, deltas):
+    total = jnp.dot(hot, table[...], preferred_element_type=F32)
+    for part in range(NY):
+        total = total + base_ref[part].astype(F32)
+    out_ref[...] = total
+
+
+def gather(col, parts, deltas):
     count = col.shape[0]
     step = 512
     return pl.pallas_call(
@@ -405,15 +435,15 @@
         out_shape=jax.ShapeDtypeStruct((count, 256), F32),
         in_specs=[
             pl.BlockSpec((step, 128), lambda i: (i, 0)),
-            pl.BlockSpec((step, 256), lambda i: (i, 0)),
+            pl.BlockSpec((NY, step, 256), lambda i: (0, i, 0)),
         ]
         + [pl.BlockSpec(d.shape, lambda i: (0, 0)) for d in deltas],
         out_specs=pl.BlockSpec((step, 256), lambda i: (i, 0)),
         scratch_shapes=[pltpu.VMEM((1536, 256), BF16)],
-        compiler_params=params("arbitrary", limit=24 * MIB),
+        compiler_params=params("arbitrary"),
         cost_estimate=cost(COST["gather"]),
         name="gather",
-    )(col, summed, *deltas)
+    )(col, parts, *deltas)
 
 
 def finish_kernel(col_ref, total_ref, *refs):
@@ -501,35 +531,39 @@
 def body(tokens, weight, down, up, ident, store):
     index, part = lax.axis_index("ad"), lax.axis_index("tp")
     place = jnp.stack([index >> 3, index & 7, part & 1]).astype(I32)
-    groups = [[x * NZ + z for z in range(NZ)] for x in range(NX)]
-
-    cw1, ccw1 = along_z(down, 1), along_z(down, -1)
-    row, col = route(place, ident.reshape(1, -1), store.reshape(1, -1))
+    columns = [[y * 2 + c for y in range(NY)] for c in range(2)]
+
+    panels = jnp.concatenate([down, up.reshape(LOCAL, 128, 128)], axis=1)
+    cw1, ccw1 = along_z(panels, 1), along_z(panels, -1)
+
+    sent = base(place, tokens, weight, False)
+    received = with_core(sent)
+    row, col = route(place, ident.reshape(1, -1), store.reshape(1, -1), sent)
     packed = {e: pack(e, row, tokens) for e in (2, 1, 3)}
     moved = {e: along_x(packed[e], e) for e in (2, 1, 3)}
     xs = [pack(0, row, tokens)] + [moved[e] for e in (1, 2, 3)]
-    ups = lax.all_gather(up, "ad", axis_index_groups=groups, tiled=True)
-
-    partial_base = base(tokens, weight, lax.axis_size("tp"), *packed.values())
-    cw1, ccw1, partial_base = lax.optimization_barrier((cw1, ccw1, partial_base))
-    summed = lax.psum_scatter(partial_base, "tp", scatter_dimension=0, tiled=True)[0]
+    chip_base = base(place, tokens, weight, True, received, *packed.values())
+    cw1, ccw1, chip_base = lax.optimization_barrier((cw1, ccw1, chip_base))
+    parts = lax.all_to_all(chip_base, "tp", 0, 0, axis_index_groups=columns, tiled=True)
+
     cw2, ccw2 = along_z(cw1, 1), along_z(ccw1, -1)
     cw3, ccw3 = along_z(cw2, 1), along_z(ccw2, -1)
     upward, downward = carve(xs)
     guests = [along_z(upward, 1), along_z(downward, -1)]
 
-    keep, send = shrink_near(place, xs, [down, cw1, ccw1, cw2, ccw2], upward)
+    held = [panels, cw1, ccw1, cw2, ccw2]
+    keep, send = shrink_near(place, xs, held, upward)
     near_chip = add(keep, with_core(send))
     near_pair = add(near_chip, with_even(near_chip))
     near = add(near_pair, with_odd(near_pair))
-    near = home(expand_near(place, near, with_core(near), ups, near_chip))
-
-    late = shrink_far(xs, [cw3, ccw3], near_chip, ups)
+    near = home(expand_near(place, near, with_core(near), held))
+
+    late = shrink_far(xs, [cw3, ccw3], near_chip, parts)
     late = shrink_late(late, guests, [cw3, ccw3], near_pair)
     late = add(late, with_core(late))
     late = add(late, with_even(late))
-    total = gather(col, summed, near)
-    late = home(expand_late(place, late, with_odd(late), ups, total))
+    total = gather(col, parts, near)
+    late = home(expand_late(late, with_odd(late), [cw3, ccw3], total))
     opposite = [d[FAR_ROWS:] for d in late]
     back = [along_z(jnp.stack(opposite[:2]), -1), along_z(jnp.stack(opposite[2:]), 1)]
 

time: 172 us -> 158 us (0.919)
  the two profiles are of different devices: /device:TPU:64 before, /device:TPU:16 now
where the time goes in v3:
time: 158 us
  Pallas kernels  55.3 us (35%)
  waiting for transfers between devices  51.9 us (33%)
  starting transfers between devices  40.6 us (26%)
  local copies, waits for them, and re-layouts  6.94 us (4%)
  other arithmetic  2.89 us (2%)
    ppermute x10, waiting for transfers between devices, along_z(): return lax.ppermute(array, 'ad', pairs)  25.2 us
    ppermute x9, waiting for transfers between devices, along_x(): return lax.ppermute(array, 'ad', pairs)  21.7 us
    ppermute x10, starting transfers between devices, along_z(): return lax.ppermute(array, 'ad', pairs)  18.4 us
    pallas_call x2, Pallas kernels, base(): pl.pallas_call(kernel, grid_spec=pltpu.PrefetchScalarGridSpec(num_scalar_...  16.8 us
    ppermute x9, starting transfers between devices, along_x(): return lax.ppermute(array, 'ad', pairs)  13.2 us
    pallas_call x4, Pallas kernels, pack(): pl.pallas_call(functools.partial(pack_kernel, e), out_shape=jax.ShapeDtyp...  11.3 us
    unnamed x50, local copies, waits for them, and re-layouts  6.92 us
    pallas_call x1, Pallas kernels, shrink_near(): pl.pallas_call(shrink_near_kernel, grid=(1,), out_shape=(half, half), in_...  6.06 us
  transfers between devices with their start and end apart: 28, of which 15 were waited for; matrix products, arithmetic and copies ran while one was open for 1% of the time, Pallas kernels for 27%

profile of v3, /device:TPU:16, one launch (start us, length us, event | category | flops | bytes accessed | tf_op | source)
XLA Modules:
  0.0 157.8 jit_solution(7781405166294106019)
XLA Ops:
  0.6 8.2 %base.2._ = bf16[4,1536,256]{2,1,0:T(8,128)(2,1)} custom-call(s32[3]{0:T(128)} %pad_add_fusion.place_ref, bf16[1536,1024]{1,0:T(8,128)(2,1)} %tok_ref.11, bf16[2,1024,1024]{2,1,0:T(8,128)(2,1)} %w_ref.3), custom_call_target="tpu_custom_call" | custom-call | flops 6600000000 | bytes 1000 | tf_op jit(solution)/shard_map/base/pallas_call | solution.py:149
  10.9 4.0 %collective-permute-start.1 = (bf16[4,1152,128]{2,1,0:T(8,128)(2,1)S(1)}, bf16[4,1152,128]{2,1,0:T(8,128)(2,1)}, u32[]{:S(2)}, u32[]{:S(2)}) collective-permute-start(bf16[4,1152,128]{2,1,0:T(8,128)(2,1)S(1)} %pad_maximum_fusion.refs_4_.refs_0_), channel_id=1, source_target_pairs={{0,56},{8,0},{16,8},{24,16},{32,24},{40,32},{48,40},{56,48},{64,12... | collective-permute-start | bytes 3538952 | tf_op jit(solution)/shard_map/ppermute | solution.py:502
  14.9 2.8 %route.1 = (s32[1,1536]{1,0:T(1,128)}, s32[1536,128]{1,0:T(8,128)}) custom-call(s32[3]{0:T(128)} %pad_add_fusion.place_ref, s32[1,1536]{1,0:T(1,128)} %bitcast.16, s32[1,128]{1,0:T(1,128)} %bitcast.17, bf16[4,1536,256]{2,1,0:T(8,128)(2,1)} %base.2._), custom_call_target="tpu_custom_call" | custom-call | flops 3300000000 | bytes 1000 | tf_op jit(solution)/shard_map/route/pallas_call | solution.py:95
  18.4 3.1 %pack.5.refs_2_ = bf16[592,1024]{1,0:T(8,128)(2,1)} custom-call(s32[1,1536]{1,0:T(1,128)S(1)} %copy-done.13, bf16[1536,1024]{1,0:T(8,128)(2,1)S(1)} %copy-done.6), custom_call_target="tpu_custom_call" | custom-call | flops 3300000000 | bytes 1000 | tf_op jit(solution)/shard_map/pack/pallas_call | solution.py:117
  23.0 3.1 %pack.4.refs_1_ = bf16[592,1024]{1,0:T(8,128)(2,1)} custom-call(s32[1,1536]{1,0:T(1,128)S(1)} %copy-done.13, bf16[1536,1024]{1,0:T(8,128)(2,1)S(1)} %copy-done.6), custom_call_target="tpu_custom_call" | custom-call | flops 3300000000 | bytes 1000 | tf_op jit(solution)/shard_map/pack/pallas_call | solution.py:117
  26.1 2.7 %collective-permute-start.4 = (bf16[592,1024]{1,0:T(8,128)(2,1)}, bf16[592,1024]{1,0:T(8,128)(2,1)S(1)}, u32[]{:S(2)}, u32[]{:S(2)}) collective-permute-start(bf16[592,1024]{1,0:T(8,128)(2,1)} %pack.4.refs_1_), channel_id=1, source_target_pairs={{0,128},{8,136},{16,144},{24,152},{32,160},{40,168},{48,176},{56,1... | collective-permute-start | bytes 3637256 | tf_op jit(solution)/shard_map/ppermute | solution.py:507
  28.8 3.1 %pack.6.refs_3_ = bf16[592,1024]{1,0:T(8,128)(2,1)} custom-call(s32[1,1536]{1,0:T(1,128)S(1)} %copy-done.13, bf16[1536,1024]{1,0:T(8,128)(2,1)S(1)} %copy-done.6), custom_call_target="tpu_custom_call" | custom-call | flops 3300000000 | bytes 1000 | tf_op jit(solution)/shard_map/pack/pallas_call | solution.py:117
  33.4 8.6 %base.3 = bf16[4,1536,256]{2,1,0:T(8,128)(2,1)} custom-call(s32[3]{0:T(128)} %pad_add_fusion.place_ref, bf16[1536,1024]{1,0:T(8,128)(2,1)} %tok_ref.11, bf16[2,1024,1024]{2,1,0:T(8,128)(2,1)} %w_ref.3, bf16[4,1536,256]{2,1,0:T(8,128)(2,1)} %collective-permute-done.2.refs_0_, bf16[592,1024]{1,0:T(8,128)(2,1)} %pack.4.refs_1_, bf16[592,1024]{1,0:T(8,128)(2,1)} %pack.5.refs_2_, ...), custom_call_target="tpu_custom_call" | custom-call | flops 6600000000 | bytes 1000 | tf_op jit(solution)/shard_map/base/pallas_call | solution.py:149
  42.2 3.2 %collective-permute-start.7 = (bf16[4,1152,128]{2,1,0:T(8,128)(2,1)}, bf16[4,1152,128]{2,1,0:T(8,128)(2,1)}, u32[]{:S(2)}, u32[]{:S(2)}) collective-permute-start(bf16[4,1152,128]{2,1,0:T(8,128)(2,1)} %collective-permute-done.1.refs_6_.refs_2_), channel_id=1, source_target_pairs={{0,56},{8,0},{16,8},{24,16},{32,24},{40,32},{48,40},{56,48},{64,12... | collective-permute-start | bytes 3538952 | tf_op jit(solution)/shard_map/ppermute | solution.py:502
  45.5 5.0 %all-to-all-start = ((bf16[4,1536,256]{2,1,0:T(8,128)(2,1)}), bf16[4,1536,256]{2,1,0:T(8,128)(2,1)}, u32[]{:S(2)}, u32[]{:S(2)}) async-start(bf16[4,1536,256]{2,1,0:T(8,128)(2,1)} %base.3), calls=%async_computation | async-start | bytes 6291456 | tf_op jit(solution)/shard_map/all_to_all | solution.py:547
  54.4 16.6 %collective-permute-done.6.refs_7_.refs_3_ = bf16[4,1152,128]{2,1,0:T(8,128)(2,1)} collective-permute-done((bf16[4,1152,128]{2,1,0:T(8,128)(2,1)}, bf16[4,1152,128]{2,1,0:T(8,128)(2,1)}, u32[]{:S(2)}, u32[]{:S(2)}) %collective-permute-start.6) | collective-permute-done | bytes 1179680 | tf_op jit(solution)/shard_map/ppermute | solution.py:502
  71.0 3.2 %collective-permute-start.16 = (bf16[4,1152,128]{2,1,0:T(8,128)(2,1)}, bf16[4,1152,128]{2,1,0:T(8,128)(2,1)}, u32[]{:S(2)}, u32[]{:S(2)}) collective-permute-start(bf16[4,1152,128]{2,1,0:T(8,128)(2,1)} %collective-permute-done.7.refs_8_.refs_4_), channel_id=1, source_target_pairs={{0,56},{8,0},{16,8},{24,16},{32,24},{40,32},{48,40},{56,48},{64,12... | collective-permute-start | bytes 3538952 | tf_op jit(solution)/shard_map/ppermute | solution.py:502
  74.2 4.4 %collective-permute-done.4.refs_2_ = bf16[592,1024]{1,0:T(8,128)(2,1)S(1)} collective-permute-done((bf16[592,1024]{1,0:T(8,128)(2,1)}, bf16[592,1024]{1,0:T(8,128)(2,1)S(1)}, u32[]{:S(2)}, u32[]{:S(2)}) %collective-permute-start.4) | collective-permute-done | bytes 1212448 | tf_op jit(solution)/shard_map/ppermute | solution.py:507
  78.7 2.8 %collective-permute-done.5.refs_3_ = bf16[592,1024]{1,0:T(8,128)(2,1)} collective-permute-done((bf16[592,1024]{1,0:T(8,128)(2,1)}, bf16[592,1024]{1,0:T(8,128)(2,1)}, u32[]{:S(2)}, u32[]{:S(2)}) %collective-permute-start.5) | collective-permute-done | bytes 1212448 | tf_op jit(solution)/shard_map/ppermute | solution.py:507
  83.2 6.1 %shrink_near.1 = (bf16[2,368,128]{2,1,0:T(8,128)(2,1)}, bf16[2,368,128]{2,1,0:T(8,128)(2,1)}) custom-call(s32[3]{0:T(128)} %pad_add_fusion.place_ref, bf16[592,1024]{1,0:T(8,128)(2,1)} %copy-done.2, bf16[592,1024]{1,0:T(8,128)(2,1)} %copy-done, bf16[592,1024]{1,0:T(8,128)(2,1)} %copy-done.1, bf16[592,1024]{1,0:T(8,128)(2,1)} %collective-permute-done.5.refs_3_, ...), custom_call_target="tpu_custom_call" | custom-call | flops 3300000000 | bytes 1000 | tf_op jit(solution)/shard_map/shrink_near/pallas_call | solution.py:215
  93.3 3.2 %collective-permute-start.18 = (bf16[2,80,1024]{2,1,0:T(8,128)(2,1)S(1)}, bf16[2,80,1024]{2,1,0:T(8,128)(2,1)S(1)}, u32[]{:S(2)}, u32[]{:S(2)}) collective-permute-start(bf16[2,80,1024]{2,1,0:T(8,128)(2,1)S(1)} %get-tuple-element.34), channel_id=1, source_target_pairs={{0,56},{8,0},{16,8},{24,16},{32,24},{40,32},{48,40},{56,48},{64,12... | collective-permute-start | bytes 983048 | tf_op jit(solution)/shard_map/ppermute | solution.py:502
  100.5 3.4 %shrink_far.1.far_ref = bf16[4,144,128]{2,1,0:T(8,128)(2,1)} custom-call(bf16[592,1024]{1,0:T(8,128)(2,1)} %copy-done.2, bf16[592,1024]{1,0:T(8,128)(2,1)} %copy-done, bf16[592,1024]{1,0:T(8,128)(2,1)} %copy-done.1, bf16[592,1024]{1,0:T(8,128)(2,1)} %collective-permute-done.5.refs_3_, bf16[4,1152,128]{2,1,0:T(8,128)(2,1)} %collective-permute-done.15.refs_4_.low_ref.refs_0_, ...), custom_call_target="tpu_custom_call" | custom-call | flops 109999996928 | bytes 1000 | tf_op jit(solution)/shard_map/shrink_far/pallas_call | solution.py:263
  107.2 3.0 %shrink_late.1 = bf16[4,224,128]{2,1,0:T(8,128)(2,1)} custom-call(bf16[4,144,128]{2,1,0:T(8,128)(2,1)} %shrink_far.1.far_ref, bf16[2,80,1024]{2,1,0:T(8,128)(2,1)} %copy-done.20, bf16[2,80,1024]{2,1,0:T(8,128)(2,1)} %copy-done.21, bf16[4,1152,128]{2,1,0:T(8,128)(2,1)} %collective-permute-done.15.refs_4_.low_ref.refs_0_, ...), custom_call_target="tpu_custom_call" | custom-call | flops 3300000000 | bytes 1000 | tf_op jit(solution)/shard_map/shrink_late/pallas_call | solution.py:291
  116.1 3.6 %collective-permute-start.12 = (bf16[368,256]{1,0:T(8,128)(2,1)S(1)}, bf16[368,256]{1,0:T(8,128)(2,1)S(1)}, u32[]{:S(2)}, u32[]{:S(2)}) collective-permute-start(bf16[368,256]{1,0:T(8,128)(2,1)S(1)} %get-tuple-element.31), channel_id=1, source_target_pairs={{0,192},{8,200},{16,208},{24,216},{32,224},{40,232},{48,240},{56,2... | collective-permute-start | bytes 565256 | tf_op jit(solution)/shard_map/ppermute | solution.py:507
  121.6 6.2 %collective-permute-done.12.refs_1_ = bf16[368,256]{1,0:T(8,128)(2,1)S(1)} collective-permute-done((bf16[368,256]{1,0:T(8,128)(2,1)S(1)}, bf16[368,256]{1,0:T(8,128)(2,1)S(1)}, u32[]{:S(2)}, u32[]{:S(2)}) %collective-permute-start.12) | collective-permute-done | bytes 188448 | tf_op jit(solution)/shard_map/ppermute | solution.py:507
  132.1 5.1 %gather.1.refs_2_.total_ref = f32[1536,256]{1,0:T(8,128)} custom-call(s32[1536,128]{1,0:T(8,128)} %get-tuple-element.22.col_ref, bf16[4,1536,256]{2,1,0:T(8,128)(2,1)} %all-to-all-done.base_ref.refs_7_, bf16[368,256]{1,0:T(8,128)(2,1)} %copy-done.12, bf16[368,256]{1,0:T(8,128)(2,1)} %copy-done.22, bf16[368,256]{1,0:T(8,128)(2,1)} %copy-done.23, ...), custom_call_target="tpu_custom_call" | custom-call | flops 5500000256 | bytes 1000 | tf_op jit(solution)/shard_map/gather/pallas_call | solution.py:432
  142.6 3.8 %collective-permute-done.22.refs_1_ = bf16[224,256]{1,0:T(8,128)(2,1)S(1)} collective-permute-done((bf16[224,256]{1,0:T(8,128)(2,1)S(1)}, bf16[224,256]{1,0:T(8,128)(2,1)S(1)}, u32[]{:S(2)}, u32[]{:S(2)}) %collective-permute-start.22) | collective-permute-done | bytes 114720 | tf_op jit(solution)/shard_map/ppermute | solution.py:507
  150.9 4.4 %collective-permute-done.26.refs_5_ = bf16[2,80,256]{2,1,0:T(8,128)(2,1)S(1)} collective-permute-done((bf16[2,80,256]{2,1,0:T(8,128)(2,1)S(1)}, bf16[2,80,256]{2,1,0:T(8,128)(2,1)S(1)}, u32[]{:S(2)}, u32[]{:S(2)}) %collective-permute-start.26) | collective-permute-done | bytes 81952 | tf_op jit(solution)/shard_map/ppermute | solution.py:502
  155.2 2.6 %finish.1 = bf16[3072,128]{1,0:T(8,128)(2,1)} custom-call(s32[1536,128]{1,0:T(8,128)S(1)} %copy-done.10, f32[1536,256]{1,0:T(8,128)S(1)} %copy-done.11, bf16[224,256]{1,0:T(8,128)(2,1)S(1)} %get-tuple-element.35.refs_0_, bf16[224,256]{1,0:T(8,128)(2,1)S(1)} %collective-permute-done.22.refs_1_, bf16[224,256]{1,0:T(8,128)(2,1)S(1)} %collective-permute-done.23.refs_2_, ...), custom_call_target="tpu_custom_call" | custom-call | flops 5500000256 | bytes 1000 | tf_op jit(solution)/shard_map/finish/pallas_call | solution.py:479
  (110 shorter events, 45.3 us)
Async XLA Ops:
  8.8 23.1 %collective-permute-start.2 = (bf16[4,1536,256]{2,1,0:T(8,128)(2,1)}, bf16[4,1536,256]{2,1,0:T(8,128)(2,1)}, u32[]{:S(2)}, u32[]{:S(2)}) collective-permute-start(bf16[4,1536,256]{2,1,0:T(8,128)(2,1)} %base.2._), channel_id=1, source_target_pairs={{0,1},{1,0},{2,3},{3,2},{4,5},{5,4},{6,7},{7,6},{8,9},{9,8},{10,11... | collective-permute-start | bytes 9437192 | tf_op jit(solution)/shard_map/ppermute | solution.py:511
  8.9 33.0 %collective-permute-start = (bf16[4,1152,128]{2,1,0:T(8,128)(2,1)S(1)}, bf16[4,1152,128]{2,1,0:T(8,128)(2,1)}, u32[]{:S(2)}, u32[]{:S(2)}) collective-permute-start(bf16[4,1152,128]{2,1,0:T(8,128)(2,1)S(1)} %pad_maximum_fusion.refs_4_.refs_0_), channel_id=1, source_target_pairs={{0,8},{8,16},{16,24},{24,32},{32,40},{40,48},{48,56},{56,0},{64,72... | collective-permute-start | bytes 3538952 | tf_op jit(solution)/shard_map/ppermute | solution.py:502
  10.9 31.1 %collective-permute-start.1 = (bf16[4,1152,128]{2,1,0:T(8,128)(2,1)S(1)}, bf16[4,1152,128]{2,1,0:T(8,128)(2,1)}, u32[]{:S(2)}, u32[]{:S(2)}) collective-permute-start(bf16[4,1152,128]{2,1,0:T(8,128)(2,1)S(1)} %pad_maximum_fusion.refs_4_.refs_0_), channel_id=1, source_target_pairs={{0,56},{8,0},{16,8},{24,16},{32,24},{40,32},{48,40},{56,48},{64,12... | collective-permute-start | bytes 3538952 | tf_op jit(solution)/shard_map/ppermute | solution.py:502
  21.5 52.7 %collective-permute-start.3 = (bf16[592,1024]{1,0:T(8,128)(2,1)}, bf16[592,1024]{1,0:T(8,128)(2,1)S(1)}, u32[]{:S(2)}, u32[]{:S(2)}) collective-permute-start(bf16[592,1024]{1,0:T(8,128)(2,1)} %pack.5.refs_2_), channel_id=1, source_target_pairs={{0,64},{8,72},{16,80},{24,88},{32,96},{40,104},{48,112},{56,120},{... | collective-permute-start | bytes 3637256 | tf_op jit(solution)/shard_map/ppermute | solution.py:507
  26.1 52.6 %collective-permute-start.4 = (bf16[592,1024]{1,0:T(8,128)(2,1)}, bf16[592,1024]{1,0:T(8,128)(2,1)S(1)}, u32[]{:S(2)}, u32[]{:S(2)}) collective-permute-start(bf16[592,1024]{1,0:T(8,128)(2,1)} %pack.4.refs_1_), channel_id=1, source_target_pairs={{0,128},{8,136},{16,144},{24,152},{32,160},{40,168},{48,176},{56,1... | collective-permute-start | bytes 3637256 | tf_op jit(solution)/shard_map/ppermute | solution.py:507
  31.9 49.6 %collective-permute-start.5 = (bf16[592,1024]{1,0:T(8,128)(2,1)}, bf16[592,1024]{1,0:T(8,128)(2,1)}, u32[]{:S(2)}, u32[]{:S(2)}) collective-permute-start(bf16[592,1024]{1,0:T(8,128)(2,1)} %pack.6.refs_3_), channel_id=1, source_target_pairs={{0,192},{8,200},{16,208},{24,216},{32,224},{40,232},{48,240},{56,2... | collective-permute-start | bytes 3637256 | tf_op jit(solution)/shard_map/ppermute | solution.py:507
  42.0 29.0 %collective-permute-start.6 = (bf16[4,1152,128]{2,1,0:T(8,128)(2,1)}, bf16[4,1152,128]{2,1,0:T(8,128)(2,1)}, u32[]{:S(2)}, u32[]{:S(2)}) collective-permute-start(bf16[4,1152,128]{2,1,0:T(8,128)(2,1)} %collective-permute-done.refs_5_.refs_1_), channel_id=1, source_target_pairs={{0,8},{8,16},{16,24},{24,32},{32,40},{40,48},{48,56},{56,0},{64,72... | collective-permute-start | bytes 3538952 | tf_op jit(solution)/shard_map/ppermute | solution.py:502
  42.2 28.8 %collective-permute-start.7 = (bf16[4,1152,128]{2,1,0:T(8,128)(2,1)}, bf16[4,1152,128]{2,1,0:T(8,128)(2,1)}, u32[]{:S(2)}, u32[]{:S(2)}) collective-permute-start(bf16[4,1152,128]{2,1,0:T(8,128)(2,1)} %collective-permute-done.1.refs_6_.refs_2_), channel_id=1, source_target_pairs={{0,56},{8,0},{16,8},{24,16},{32,24},{40,32},{48,40},{56,48},{64,12... | collective-permute-start | bytes 3538952 | tf_op jit(solution)/shard_map/ppermute | solution.py:502
  45.5 53.9 %all-to-all-start = ((bf16[4,1536,256]{2,1,0:T(8,128)(2,1)}), bf16[4,1536,256]{2,1,0:T(8,128)(2,1)}, u32[]{:S(2)}, u32[]{:S(2)}) async-start(bf16[4,1536,256]{2,1,0:T(8,128)(2,1)} %base.3), calls=%async_computation | async-start | bytes 6291456 | tf_op jit(solution)/shard_map/all_to_all | solution.py:547
  71.0 29.5 %collective-permute-start.15 = (bf16[4,1152,128]{2,1,0:T(8,128)(2,1)}, bf16[4,1152,128]{2,1,0:T(8,128)(2,1)}, u32[]{:S(2)}, u32[]{:S(2)}) collective-permute-start(bf16[4,1152,128]{2,1,0:T(8,128)(2,1)} %collective-permute-done.6.refs_7_.refs_3_), channel_id=1, source_target_pairs={{0,8},{8,16},{16,24},{24,32},{32,40},{40,48},{48,56},{56,0},{64,72... | collective-permute-start | bytes 3538952 | tf_op jit(solution)/shard_map/ppermute | solution.py:502
  71.0 29.5 %collective-permute-start.16 = (bf16[4,1152,128]{2,1,0:T(8,128)(2,1)}, bf16[4,1152,128]{2,1,0:T(8,128)(2,1)}, u32[]{:S(2)}, u32[]{:S(2)}) collective-permute-start(bf16[4,1152,128]{2,1,0:T(8,128)(2,1)} %collective-permute-done.7.refs_8_.refs_4_), channel_id=1, source_target_pairs={{0,56},{8,0},{16,8},{24,16},{32,24},{40,32},{48,40},{56,48},{64,12... | collective-permute-start | bytes 3538952 | tf_op jit(solution)/shard_map/ppermute | solution.py:502
  91.9 6.9 %collective-permute-start.9 = (bf16[2,368,128]{2,1,0:T(8,128)(2,1)S(1)}, bf16[2,368,128]{2,1,0:T(8,128)(2,1)S(1)}, u32[]{:S(2)}, u32[]{:S(2)}) collective-permute-start(bf16[2,368,128]{2,1,0:T(8,128)(2,1)S(1)} %add_convert_fusion.4.refs_6_), channel_id=1, source_target_pairs={{0,2},{1,3},{2,0},{3,1},{4,6},{5,7},{6,4},{7,5},{8,10},{9,11},{10,... | collective-permute-start | bytes 565256 | tf_op jit(solution)/shard_map/ppermute | solution.py:515
  93.3 12.5 %collective-permute-start.17 = (bf16[2,80,1024]{2,1,0:T(8,128)(2,1)S(1)}, bf16[2,80,1024]{2,1,0:T(8,128)(2,1)S(1)}, u32[]{:S(2)}, u32[]{:S(2)}) collective-permute-start(bf16[2,80,1024]{2,1,0:T(8,128)(2,1)S(1)} %copy-done.9), channel_id=1, source_target_pairs={{0,8},{8,16},{16,24},{24,32},{32,40},{40,48},{48,56},{56,0},{64,72... | collective-permute-start | bytes 983048 | tf_op jit(solution)/shard_map/ppermute | solution.py:502
  93.3 12.5 %collective-permute-start.18 = (bf16[2,80,1024]{2,1,0:T(8,128)(2,1)S(1)}, bf16[2,80,1024]{2,1,0:T(8,128)(2,1)S(1)}, u32[]{:S(2)}, u32[]{:S(2)}) collective-permute-start(bf16[2,80,1024]{2,1,0:T(8,128)(2,1)S(1)} %get-tuple-element.34), channel_id=1, source_target_pairs={{0,56},{8,0},{16,8},{24,16},{32,24},{40,32},{48,40},{56,48},{64,12... | collective-permute-start | bytes 983048 | tf_op jit(solution)/shard_map/ppermute | solution.py:502
  98.9 11.4 %collective-permute-start.10 = (bf16[2,368,128]{2,1,0:T(8,128)(2,1)S(1)}, bf16[2,368,128]{2,1,0:T(8,128)(2,1)S(1)}, u32[]{:S(2)}, u32[]{:S(2)}) collective-permute-start(bf16[2,368,128]{2,1,0:T(8,128)(2,1)S(1)} %add_convert_fusion.3._), channel_id=1, source_target_pairs={{0,6},{1,7},{2,4},{3,5},{4,2},{5,3},{6,0},{7,1},{8,14},{9,15},{10,... | collective-permute-start | bytes 565256 | tf_op jit(solution)/shard_map/ppermute | solution.py:520
  112.9 8.5 %collective-permute-start.20 = (bf16[4,224,128]{2,1,0:T(8,128)(2,1)S(1)}, bf16[4,224,128]{2,1,0:T(8,128)(2,1)S(1)}, u32[]{:S(2)}, u32[]{:S(2)}) collective-permute-start(bf16[4,224,128]{2,1,0:T(8,128)(2,1)S(1)} %add_convert_fusion.1), channel_id=1, source_target_pairs={{0,2},{1,3},{2,0},{3,1},{4,6},{5,7},{6,4},{7,5},{8,10},{9,11},{10,... | collective-permute-start | bytes 688136 | tf_op jit(solution)/shard_map/ppermute | solution.py:515
  116.1 11.6 %collective-permute-start.12 = (bf16[368,256]{1,0:T(8,128)(2,1)S(1)}, bf16[368,256]{1,0:T(8,128)(2,1)S(1)}, u32[]{:S(2)}, u32[]{:S(2)}) collective-permute-start(bf16[368,256]{1,0:T(8,128)(2,1)S(1)} %get-tuple-element.31), channel_id=1, source_target_pairs={{0,192},{8,200},{16,208},{24,216},{32,224},{40,232},{48,240},{56,2... | collective-permute-start | bytes 565256 | tf_op jit(solution)/shard_map/ppermute | solution.py:507
  119.7 9.2 %collective-permute-start.13 = (bf16[368,256]{1,0:T(8,128)(2,1)S(1)}, bf16[368,256]{1,0:T(8,128)(2,1)S(1)}, u32[]{:S(2)}, u32[]{:S(2)}) collective-permute-start(bf16[368,256]{1,0:T(8,128)(2,1)S(1)} %get-tuple-element.32), channel_id=1, source_target_pairs={{0,128},{8,136},{16,144},{24,152},{32,160},{40,168},{48,176},{56,1... | collective-permute-start | bytes 565256 | tf_op jit(solution)/shard_map/ppermute | solution.py:507
  120.5 10.9 %collective-permute-start.14 = (bf16[368,256]{1,0:T(8,128)(2,1)S(1)}, bf16[368,256]{1,0:T(8,128)(2,1)S(1)}, u32[]{:S(2)}, u32[]{:S(2)}) collective-permute-start(bf16[368,256]{1,0:T(8,128)(2,1)S(1)} %get-tuple-element.33), channel_id=1, source_target_pairs={{0,64},{8,72},{16,80},{24,88},{32,96},{40,104},{48,112},{56,120},{... | collective-permute-start | bytes 565256 | tf_op jit(solution)/shard_map/ppermute | solution.py:507
  121.5 15.8 %collective-permute-start.21 = (bf16[4,224,128]{2,1,0:T(8,128)(2,1)S(1)}, bf16[4,224,128]{2,1,0:T(8,128)(2,1)S(1)}, u32[]{:S(2)}, u32[]{:S(2)}) collective-permute-start(bf16[4,224,128]{2,1,0:T(8,128)(2,1)S(1)} %add_convert_fusion.mine_ref), channel_id=1, source_target_pairs={{0,6},{1,7},{2,4},{3,5},{4,2},{5,3},{6,0},{7,1},{8,14},{9,15},{10,... | collective-permute-start | bytes 688136 | tf_op jit(solution)/shard_map/ppermute | solution.py:520
  140.3 6.1 %collective-permute-start.22 = (bf16[224,256]{1,0:T(8,128)(2,1)S(1)}, bf16[224,256]{1,0:T(8,128)(2,1)S(1)}, u32[]{:S(2)}, u32[]{:S(2)}) collective-permute-start(bf16[224,256]{1,0:T(8,128)(2,1)S(1)} %get-tuple-element.36), channel_id=1, source_target_pairs={{0,192},{8,200},{16,208},{24,216},{32,224},{40,232},{48,240},{56,2... | collective-permute-start | bytes 344072 | tf_op jit(solution)/shard_map/ppermute | solution.py:507
  141.0 8.5 %collective-permute-start.23 = (bf16[224,256]{1,0:T(8,128)(2,1)S(1)}, bf16[224,256]{1,0:T(8,128)(2,1)S(1)}, u32[]{:S(2)}, u32[]{:S(2)}) collective-permute-start(bf16[224,256]{1,0:T(8,128)(2,1)S(1)} %get-tuple-element.37), channel_id=1, source_target_pairs={{0,128},{8,136},{16,144},{24,152},{32,160},{40,168},{48,176},{56,1... | collective-permute-start | bytes 344072 | tf_op jit(solution)/shard_map/ppermute | solution.py:507
  141.7 7.7 %collective-permute-start.24 = (bf16[224,256]{1,0:T(8,128)(2,1)S(1)}, bf16[224,256]{1,0:T(8,128)(2,1)S(1)}, u32[]{:S(2)}, u32[]{:S(2)}) collective-permute-start(bf16[224,256]{1,0:T(8,128)(2,1)S(1)} %get-tuple-element.38), channel_id=1, source_target_pairs={{0,64},{8,72},{16,80},{24,88},{32,96},{40,104},{48,112},{56,120},{... | collective-permute-start | bytes 344072 | tf_op jit(solution)/shard_map/ppermute | solution.py:507
  149.5 5.7 %collective-permute-start.26 = (bf16[2,80,256]{2,1,0:T(8,128)(2,1)S(1)}, bf16[2,80,256]{2,1,0:T(8,128)(2,1)S(1)}, u32[]{:S(2)}, u32[]{:S(2)}) collective-permute-start(bf16[2,80,256]{2,1,0:T(8,128)(2,1)S(1)} %pad_maximum_fusion.2), channel_id=1, source_target_pairs={{0,8},{8,16},{16,24},{24,32},{32,40},{40,48},{48,56},{56,0},{64,72... | collective-permute-start | bytes 245768 | tf_op jit(solution)/shard_map/ppermute | solution.py:502
  (29 other events, 171.4 us)

commit v4 on v3

--- a/solution.py
+++ b/solution.py
@@ -32,7 +32,7 @@
 MIB = 1024 * 1024
 VMEM = 56 * MIB
 COST = {
-    "route": 3, "pack": 3, "base": 6, "carve": 1, "shrink_near": 3, "expand_near": 3,
+    "route": 3, "pack": 3, "columns": 2, "base": 11, "carve": 1, "shrink_near": 3, "expand_near": 3,
     "shrink_far": 100, "shrink_late": 3, "expand_late": 30, "gather": 5, "finish": 5,
 }
 VMEM = 56 * 1024 * 1024
@@ -62,7 +62,7 @@
     return pl.BlockSpec(memory_space=pltpu.SMEM)
 
 
-def route_kernel(place_ref, ids_ref, store_ref, _, row_ref, col_ref):
+def route_kernel(place_ref, ids_ref, store_ref, row_ref, col_ref):
     x, z = place_ref[0], place_ref[1]
     count = ids_ref.shape[1]
     ids = jnp.broadcast_to(ids_ref[...], (128, count))
@@ -90,7 +90,7 @@
     col_ref[...] = jnp.broadcast_to(row_ref[...], (128, count)).T
 
 
-def route(place, ids, store, earlier):
+def route(place, ids, store):
     count = ids.shape[1]
     return pl.pallas_call(
         route_kernel,
@@ -98,72 +98,87 @@
             jax.ShapeDtypeStruct((1, count), I32),
             jax.ShapeDtypeStruct((count, 128), I32),
         ),
-        in_specs=[scalars(), whole(), whole(), pl.BlockSpec(memory_space=pl.ANY)],
+        in_specs=[scalars(), whole(), whole()],
         out_specs=(whole(), whole()),
         compiler_params=params(),
         cost_estimate=cost(COST['route']),
         name="route",
-    )(place, ids, store, earlier)
-
-
-def pack_kernel(e, row_ref, tok_ref, out_ref):
+    )(place, ids, store)
+
+
+def pack_kernel(e, row_ref, tok_ref, *refs):
+    out_ref = refs[-1]
     hot = row_ref[...] == iota((ROWS, row_ref.shape[1]), 0) + e * ROWS
     out_ref[...] = jnp.dot(
         hot.astype(BF16), tok_ref[...], preferred_element_type=F32
     ).astype(BF16)
 
 
-def pack(e, row, tokens):
+def pack(e, row, tokens, *earlier):
     return pl.pallas_call(
         functools.partial(pack_kernel, e),
         out_shape=jax.ShapeDtypeStruct((ROWS, tokens.shape[1]), BF16),
-        in_specs=[whole()] * 2,
+        in_specs=[whole()] * 2 + [pl.BlockSpec(memory_space=pl.ANY)] * len(earlier),
         out_specs=whole(),
         compiler_params=params(limit=24 * MIB),
         cost_estimate=cost(COST["pack"]),
         name="pack",
-    )(row, tokens)
-
-
-def base_kernel(place_ref, tok_ref, w_ref, add_ref, out_ref):
-    both = jnp.concatenate([w_ref[0], w_ref[1]], axis=1)
-    y = jnp.dot(tok_ref[...], both, preferred_element_type=F32)
-    if add_ref is not None:
-        y = y + add_ref[0].astype(F32)
-    out_ref[0] = y.astype(BF16)
-
-
-def base(place, tokens, weight, mine, received=None, *earlier):
-    count, width = tokens.shape
-
-    def column(i, place_ref):
-        core = place_ref[2]
-        return (0, 0, i * 2 + (core if mine else 1 - core))
-
-    def kernel(place_ref, tok_ref, w_ref, *refs):
-        add_ref = None if received is None else refs[0]
-        base_kernel(place_ref, tok_ref, w_ref, add_ref, refs[-1])
-
-    block = pl.BlockSpec((1, count, 256), lambda i, _: (i, 0, 0))
-    extra = [] if received is None else [received]
-    return pl.pallas_call(
-        kernel,
+    )(row, tokens, *earlier)
+
+
+def columns_kernel(place_ref, w_ref, out_ref):
+    out_ref[...] = w_ref[...]
+
+
+def other_columns(place, weight):
+    width = weight.shape[1]
+    return pl.pallas_call(
+        columns_kernel,
         grid_spec=pltpu.PrefetchScalarGridSpec(
             num_scalar_prefetch=1,
             grid=(NY,),
             in_specs=[
-                pl.BlockSpec((count, width), lambda i, _: (0, 0)),
-                pl.BlockSpec((2, width, 128), column),
+                pl.BlockSpec((2, width, 128), lambda i, place: (0, 0, i * 2 + 1 - place[2]))
+            ],
+            out_specs=pl.BlockSpec((2, width, 128), lambda i, place: (0, 0, i)),
+        ),
+        out_shape=jax.ShapeDtypeStruct((2, width, NY * 128), BF16),
+        compiler_params=params("arbitrary"),
+        cost_estimate=cost(COST["columns"]),
+        name="columns",
+    )(place, weight)
+
+
+def base_kernel(place_ref, tok_ref, w_ref, other_tok_ref, other_w_ref, *refs):
+    total = jnp.zeros(refs[-1].shape[1:], F32)
+    for t_ref, panel_ref in ((tok_ref, w_ref), (other_tok_ref, other_w_ref)):
+        both = jnp.concatenate([panel_ref[0], panel_ref[1]], axis=1)
+        total = total + jnp.dot(t_ref[...], both, preferred_element_type=F32)
+    refs[-1][0] = total.astype(BF16)
+
+
+def base(place, tokens, weight, other_tokens, other_weight, *earlier):
+    count, width = tokens.shape
+    rows = pl.BlockSpec((count, width), lambda i, place: (0, 0))
+    return pl.pallas_call(
+        base_kernel,
+        grid_spec=pltpu.PrefetchScalarGridSpec(
+            num_scalar_prefetch=1,
+            grid=(NY,),
+            in_specs=[
+                rows,
+                pl.BlockSpec((2, width, 128), lambda i, place: (0, 0, i * 2 + place[2])),
+                rows,
+                pl.BlockSpec((2, width, 128), lambda i, place: (0, 0, i)),
             ]
-            + [block] * len(extra)
             + [pl.BlockSpec(memory_space=pl.ANY)] * len(earlier),
-            out_specs=block,
+            out_specs=pl.BlockSpec((1, count, 256), lambda i, place: (i, 0, 0)),
         ),
         out_shape=jax.ShapeDtypeStruct((NY, count, 256), BF16),
         compiler_params=params("arbitrary"),
         cost_estimate=cost(COST["base"]),
         name="base",
-    )(place, tokens, weight, *extra, *earlier)
+    )(place, tokens, weight, other_tokens, other_weight, *earlier)
 
 
 def adapter_of(skip, copies):
@@ -222,7 +237,7 @@
         + [pl.BlockSpec(memory_space=pl.ANY)] * len(earlier),
         out_specs=(pl.BlockSpec(half.shape, lambda i: (0, 0, 0)),) * 2,
         scratch_shapes=[pltpu.VMEM((NX, NEAR_ROWS, 128), F32)],
-        compiler_params=params("arbitrary"),
+        compiler_params=params("arbitrary", limit=32 * MIB),
         cost_estimate=cost(COST["shrink_near"]),
         name="shrink_near",
     )(place, *xs, *panels, *earlier)
@@ -272,7 +287,7 @@
         + [pl.BlockSpec(memory_space=pl.ANY)] * len(earlier),
         out_specs=pl.BlockSpec((NX, FAR_ROWS, 128), lambda i: (0, 0, 0)),
         scratch_shapes=[pltpu.VMEM((NX, FAR_ROWS, 128), F32)],
-        compiler_params=params("arbitrary"),
+        compiler_params=params("arbitrary", limit=16 * MIB),
         cost_estimate=cost(COST["shrink_far"]),
         name="shrink_far",
     )(*xs, *panels, *earlier)
@@ -296,7 +311,7 @@
         + [pl.BlockSpec((LOCAL, width, 128), lambda i: (0, 0, 0)) for w in panels]
         + [pl.BlockSpec(memory_space=pl.ANY)],
         out_specs=pl.BlockSpec((NX, LATE_ROWS, 128), lambda i: (0, 0, 0)),
-        compiler_params=params("arbitrary"),
+        compiler_params=params("arbitrary", limit=16 * MIB),
         cost_estimate=cost(COST["shrink_late"]),
         name="shrink_late",
     )(far, *guests, *panels, earlier)
@@ -360,7 +375,7 @@
 
 
 def expand_late_kernel(mine_ref, other_ref, *refs):
-    ups, outs = refs[: len(FAR)], refs[len(FAR) + 1 : len(FAR) + 1 + NX]
+    ups, outs = refs[: len(FAR)], refs[-3 - NX : -3]
     wides, total = refs[-3:-1], refs[-1]
     shrunk = (mine_ref[...].astype(F32) + other_ref[...].astype(F32)).astype(BF16)
     total[...] = jnp.zeros_like(total)
@@ -381,7 +396,7 @@
         outs[e][...] = total[e].astype(BF16)
 
 
-def expand_late(mine, other, panels, earlier):
+def expand_late(mine, other, panels, *earlier):
     full = pl.BlockSpec(mine.shape, lambda i: (0, 0, 0))
     return pl.pallas_call(
         expand_late_kernel,
@@ -389,7 +404,7 @@
         out_shape=[jax.ShapeDtypeStruct((LATE_ROWS, 256), BF16)] * NX,
         in_specs=[full, full]
         + [up_block(w) for w in panels]
-        + [pl.BlockSpec(memory_space=pl.ANY)],
+        + [pl.BlockSpec(memory_space=pl.ANY)] * len(earlier),
         out_specs=[pl.BlockSpec((LATE_ROWS, 256), lambda i: (0, 0))] * NX,
         scratch_shapes=[
             pltpu.VMEM((LOCAL * 128, 256), BF16),
@@ -399,7 +414,7 @@
         compiler_params=params("arbitrary", limit=24 * MIB),
         cost_estimate=cost(COST["expand_late"]),
         name="expand_late",
-    )(mine, other, *panels, earlier)
+    )(mine, other, *panels, *earlier)
 
 
 def gather_kernel(col_ref, base_ref, *refs):
@@ -536,13 +551,13 @@
     panels = jnp.concatenate([down, up.reshape(LOCAL, 128, 128)], axis=1)
     cw1, ccw1 = along_z(panels, 1), along_z(panels, -1)
 
-    sent = base(place, tokens, weight, False)
-    received = with_core(sent)
-    row, col = route(place, ident.reshape(1, -1), store.reshape(1, -1), sent)
-    packed = {e: pack(e, row, tokens) for e in (2, 1, 3)}
-    moved = {e: along_x(packed[e], e) for e in (2, 1, 3)}
+    other_tokens = with_core(tokens)
+    other_weight = with_core(other_columns(place, weight))
+    row, col = route(place, ident.reshape(1, -1), store.reshape(1, -1))
+    packed = {e: pack(e, row, tokens) for e in (1, 3, 2)}
+    moved = {e: along_x(packed[e], e) for e in (1, 3, 2)}
     xs = [pack(0, row, tokens)] + [moved[e] for e in (1, 2, 3)]
-    chip_base = base(place, tokens, weight, True, received, *packed.values())
+    chip_base = base(place, tokens, weight, other_tokens, other_weight, *packed.values())
     cw1, ccw1, chip_base = lax.optimization_barrier((cw1, ccw1, chip_base))
     parts = lax.all_to_all(chip_base, "tp", 0, 0, axis_index_groups=columns, tiled=True)
 
@@ -563,7 +578,7 @@
     late = add(late, with_core(late))
     late = add(late, with_even(late))
     total = gather(col, parts, near)
-    late = home(expand_late(late, with_odd(late), [cw3, ccw3], total))
+    late = home(expand_late(late, with_odd(late), [cw3, ccw3], *near[1:]))
     opposite = [d[FAR_ROWS:] for d in late]
     back = [along_z(jnp.stack(opposite[:2]), -1), along_z(jnp.stack(opposite[2:]), 1)]
 

time: 158 us -> 158 us (level)
  the two profiles are of different devices: /device:TPU:16 before, /device:TPU:64 now
where the time goes in v4:
time: 158 us; the launch traced here: 157 us
  waiting for transfers between devices  59.7 us (38%)
  Pallas kernels  53.7 us (34%)
  starting transfers between devices  36.8 us (23%)
  local copies, waits for them, and re-layouts  5.57 us (4%)
    ppermute x10, waiting for transfers between devices, along_z(): return lax.ppermute(array, 'ad', pairs)  25.2 us
    ppermute x9, waiting for transfers between devices, along_x(): return lax.ppermute(array, 'ad', pairs)  23.9 us
    ppermute x10, starting transfers between devices, along_z(): return lax.ppermute(array, 'ad', pairs)  14.6 us
    pallas_call x1, Pallas kernels, base(): pl.pallas_call(base_kernel, grid_spec=pltpu.PrefetchScalarGridSpec(num_sc...  12.1 us
    pallas_call x4, Pallas kernels, pack(): pl.pallas_call(functools.partial(pack_kernel, e), out_shape=jax.ShapeDtyp...  11.3 us
    ppermute x9, starting transfers between devices, along_x(): return lax.ppermute(array, 'ad', pairs)  10.2 us
    unnamed x40, local copies, waits for them, and re-layouts  5.56 us
    pallas_call x1, Pallas kernels, gather(): pl.pallas_call(gather_kernel, grid=(count // step,), out_shape=jax.ShapeD...  5.21 us
  transfers between devices with their start and end apart: 29, of which 15 were waited for; matrix products, arithmetic and copies ran while one was open for 1% of the time, Pallas kernels for 30%

profile of v4, /device:TPU:64, one launch (start us, length us, event | category | flops | bytes accessed | tf_op | source)
XLA Modules:
  0.0 157.2 jit_solution(9491158172161829662)
XLA Ops:
  0.7 4.7 %columns.1 = bf16[2,1024,512]{2,1,0:T(8,128)(2,1)} custom-call(s32[3]{0:T(128)} %pad_add_fusion.place_ref, bf16[2,1024,1024]{2,1,0:T(8,128)(2,1)} %w_ref.3), custom_call_target="tpu_custom_call" | custom-call | flops 2200000000 | bytes 1000 | tf_op jit(solution)/shard_map/columns/pallas_call | solution.py:135
  8.0 2.8 %route.1 = (s32[1,1536]{1,0:T(1,128)}, s32[1536,128]{1,0:T(8,128)}) custom-call(s32[3]{0:T(128)} %pad_add_fusion.place_ref, s32[1,1536]{1,0:T(1,128)} %bitcast.16, s32[1,128]{1,0:T(1,128)} %bitcast.17), custom_call_target="tpu_custom_call" | custom-call | flops 3300000000 | bytes 1000 | tf_op jit(solution)/shard_map/route/pallas_call | solution.py:95
  11.5 3.1 %pack.4.refs_0_ = bf16[592,1024]{1,0:T(8,128)(2,1)} custom-call(s32[1,1536]{1,0:T(1,128)S(1)} %copy-done.15, bf16[1536,1024]{1,0:T(8,128)(2,1)S(1)} %copy-done.7), custom_call_target="tpu_custom_call" | custom-call | flops 3300000000 | bytes 1000 | tf_op jit(solution)/shard_map/pack/pallas_call | solution.py:118
  16.1 3.1 %pack.5.refs_1_ = bf16[592,1024]{1,0:T(8,128)(2,1)} custom-call(s32[1,1536]{1,0:T(1,128)S(1)} %copy-done.15, bf16[1536,1024]{1,0:T(8,128)(2,1)S(1)} %copy-done.7), custom_call_target="tpu_custom_call" | custom-call | flops 3300000000 | bytes 1000 | tf_op jit(solution)/shard_map/pack/pallas_call | solution.py:118
  19.2 3.1 %pack.6.refs_2_ = bf16[592,1024]{1,0:T(8,128)(2,1)} custom-call(s32[1,1536]{1,0:T(1,128)S(1)} %copy-done.15, bf16[1536,1024]{1,0:T(8,128)(2,1)S(1)} %copy-done.7), custom_call_target="tpu_custom_call" | custom-call | flops 3300000000 | bytes 1000 | tf_op jit(solution)/shard_map/pack/pallas_call | solution.py:118
  22.3 2.7 %collective-permute-start.5 = (bf16[592,1024]{1,0:T(8,128)(2,1)}, bf16[592,1024]{1,0:T(8,128)(2,1)}, u32[]{:S(2)}, u32[]{:S(2)}) collective-permute-start(bf16[592,1024]{1,0:T(8,128)(2,1)} %pack.6.refs_2_), channel_id=1, source_target_pairs={{0,128},{8,136},{16,144},{24,152},{32,160},{40,168},{48,176},{56,1... | collective-permute-start | bytes 3637256 | tf_op jit(solution)/shard_map/ppermute | solution.py:522
  26.7 12.1 %base.1 = bf16[4,1536,256]{2,1,0:T(8,128)(2,1)} custom-call(s32[3]{0:T(128)} %pad_add_fusion.place_ref, bf16[1536,1024]{1,0:T(8,128)(2,1)} %tok_ref.9, bf16[2,1024,1024]{2,1,0:T(8,128)(2,1)} %w_ref.3, bf16[1536,1024]{1,0:T(8,128)(2,1)} %copy-done.19, bf16[2,1024,512]{2,1,0:T(8,128)(2,1)} %collective-permute-done.3.other_w_ref, ...), custom_call_target="tpu_custom_call" | custom-call | flops 12099999744 | bytes 1000 | tf_op jit(solution)/shard_map/base/pallas_call | solution.py:163
  38.9 3.1 %collective-permute-start.7 = (bf16[4,1152,128]{2,1,0:T(8,128)(2,1)}, bf16[4,1152,128]{2,1,0:T(8,128)(2,1)}, u32[]{:S(2)}, u32[]{:S(2)}) collective-permute-start(bf16[4,1152,128]{2,1,0:T(8,128)(2,1)} %collective-permute-done.refs_5_.refs_1_), channel_id=1, source_target_pairs={{0,8},{8,16},{16,24},{24,32},{32,40},{40,48},{48,56},{56,0},{64,72... | collective-permute-start | bytes 3538952 | tf_op jit(solution)/shard_map/ppermute | solution.py:517
  42.0 4.5 %all-to-all-start = ((bf16[4,1536,256]{2,1,0:T(8,128)(2,1)}), bf16[4,1536,256]{2,1,0:T(8,128)(2,1)S(1)}, u32[]{:S(2)}, u32[]{:S(2)}) async-start(bf16[4,1536,256]{2,1,0:T(8,128)(2,1)} %base.1), calls=%async_computation | async-start | bytes 6291456 | tf_op jit(solution)/shard_map/all_to_all | solution.py:562
  50.4 16.4 %collective-permute-done.7.refs_7_.refs_3_ = bf16[4,1152,128]{2,1,0:T(8,128)(2,1)} collective-permute-done((bf16[4,1152,128]{2,1,0:T(8,128)(2,1)}, bf16[4,1152,128]{2,1,0:T(8,128)(2,1)}, u32[]{:S(2)}, u32[]{:S(2)}) %collective-permute-start.7) | collective-permute-done | bytes 1179680 | tf_op jit(solution)/shard_map/ppermute | solution.py:517
  66.9 3.0 %collective-permute-start.16 = (bf16[4,1152,128]{2,1,0:T(8,128)(2,1)}, bf16[4,1152,128]{2,1,0:T(8,128)(2,1)}, u32[]{:S(2)}, u32[]{:S(2)}) collective-permute-start(bf16[4,1152,128]{2,1,0:T(8,128)(2,1)} %collective-permute-done.7.refs_7_.refs_3_), channel_id=1, source_target_pairs={{0,8},{8,16},{16,24},{24,32},{32,40},{40,48},{48,56},{56,0},{64,72... | collective-permute-start | bytes 3538952 | tf_op jit(solution)/shard_map/ppermute | solution.py:517
  71.3 5.8 %collective-permute-done.6.refs_3_ = bf16[592,1024]{1,0:T(8,128)(2,1)} collective-permute-done((bf16[592,1024]{1,0:T(8,128)(2,1)}, bf16[592,1024]{1,0:T(8,128)(2,1)}, u32[]{:S(2)}, u32[]{:S(2)}) %collective-permute-start.6) | collective-permute-done | bytes 1212448 | tf_op jit(solution)/shard_map/ppermute | solution.py:522
  79.1 4.8 %shrink_near.1 = (bf16[2,368,128]{2,1,0:T(8,128)(2,1)S(1)}, bf16[2,368,128]{2,1,0:T(8,128)(2,1)S(1)}) custom-call(s32[3]{0:T(128)S(1)} %copy-done.6, bf16[592,1024]{1,0:T(8,128)(2,1)S(1)} %pack.7.refs_0_, bf16[592,1024]{1,0:T(8,128)(2,1)} %collective-permute-done.4.refs_1_, bf16[592,1024]{1,0:T(8,128)(2,1)} %collective-permute-done.5.refs_2_, ...), custom_call_target="tpu_custom_call" | custom-call | flops 3300000000 | bytes 1000 | tf_op jit(solution)/shard_map/shrink_near/pallas_call | solution.py:230
  87.2 3.1 %collective-permute-start.18 = (bf16[2,80,1024]{2,1,0:T(8,128)(2,1)}, bf16[2,80,1024]{2,1,0:T(8,128)(2,1)}, u32[]{:S(2)}, u32[]{:S(2)}) collective-permute-start(bf16[2,80,1024]{2,1,0:T(8,128)(2,1)} %get-tuple-element.27.refs_9_), channel_id=1, source_target_pairs={{0,8},{8,16},{16,24},{24,32},{32,40},{40,48},{48,56},{56,0},{64,72... | collective-permute-start | bytes 983048 | tf_op jit(solution)/shard_map/ppermute | solution.py:517
  92.4 3.9 %collective-permute-done.16.refs_4_.low_ref.refs_0_ = bf16[4,1152,128]{2,1,0:T(8,128)(2,1)} collective-permute-done((bf16[4,1152,128]{2,1,0:T(8,128)(2,1)}, bf16[4,1152,128]{2,1,0:T(8,128)(2,1)}, u32[]{:S(2)}, u32[]{:S(2)}) %collective-permute-start.16) | collective-permute-done | bytes 1179680 | tf_op jit(solution)/shard_map/ppermute | solution.py:517
  96.3 4.4 %collective-permute-done.17.refs_5_.high_ref.refs_1_ = bf16[4,1152,128]{2,1,0:T(8,128)(2,1)} collective-permute-done((bf16[4,1152,128]{2,1,0:T(8,128)(2,1)}, bf16[4,1152,128]{2,1,0:T(8,128)(2,1)}, u32[]{:S(2)}, u32[]{:S(2)}) %collective-permute-start.17) | collective-permute-done | bytes 1179680 | tf_op jit(solution)/shard_map/ppermute | solution.py:517
  107.1 3.3 %collective-permute-start.11 = (bf16[2,368,128]{2,1,0:T(8,128)(2,1)S(1)}, bf16[2,368,128]{2,1,0:T(8,128)(2,1)S(1)}, u32[]{:S(2)}, u32[]{:S(2)}) collective-permute-start(bf16[2,368,128]{2,1,0:T(8,128)(2,1)S(1)} %add_convert_fusion.3._), channel_id=1, source_target_pairs={{0,6},{1,7},{2,4},{3,5},{4,2},{5,3},{6,0},{7,1},{8,14},{9,15},{10,... | collective-permute-start | bytes 565256 | tf_op jit(solution)/shard_map/ppermute | solution.py:535
  110.7 4.8 %collective-permute-done.11 = bf16[2,368,128]{2,1,0:T(8,128)(2,1)S(1)} collective-permute-done((bf16[2,368,128]{2,1,0:T(8,128)(2,1)S(1)}, bf16[2,368,128]{2,1,0:T(8,128)(2,1)S(1)}, u32[]{:S(2)}, u32[]{:S(2)}) %collective-permute-start.11) | collective-permute-done | bytes 188448 | tf_op jit(solution)/shard_map/ppermute | solution.py:535
  123.8 5.3 %collective-permute-done.13.refs_1_.refs_2_ = bf16[368,256]{1,0:T(8,128)(2,1)S(1)} collective-permute-done((bf16[368,256]{1,0:T(8,128)(2,1)S(1)}, bf16[368,256]{1,0:T(8,128)(2,1)S(1)}, u32[]{:S(2)}, u32[]{:S(2)}) %collective-permute-start.13) | collective-permute-done | bytes 188448 | tf_op jit(solution)/shard_map/ppermute | solution.py:522
  129.1 2.9 %collective-permute-done.14.refs_2_.refs_3_ = bf16[368,256]{1,0:T(8,128)(2,1)S(1)} collective-permute-done((bf16[368,256]{1,0:T(8,128)(2,1)S(1)}, bf16[368,256]{1,0:T(8,128)(2,1)S(1)}, u32[]{:S(2)}, u32[]{:S(2)}) %collective-permute-start.14) | collective-permute-done | bytes 188448 | tf_op jit(solution)/shard_map/ppermute | solution.py:522
  137.8 4.0 %collective-permute-done.23.refs_1_ = bf16[224,256]{1,0:T(8,128)(2,1)S(1)} collective-permute-done((bf16[224,256]{1,0:T(8,128)(2,1)S(1)}, bf16[224,256]{1,0:T(8,128)(2,1)S(1)}, u32[]{:S(2)}, u32[]{:S(2)}) %collective-permute-start.23) | collective-permute-done | bytes 114720 | tf_op jit(solution)/shard_map/ppermute | solution.py:522
  141.9 2.8 %collective-permute-done.25.refs_3_ = bf16[224,256]{1,0:T(8,128)(2,1)S(1)} collective-permute-done((bf16[224,256]{1,0:T(8,128)(2,1)S(1)}, bf16[224,256]{1,0:T(8,128)(2,1)S(1)}, u32[]{:S(2)}, u32[]{:S(2)}) %collective-permute-start.25) | collective-permute-done | bytes 114720 | tf_op jit(solution)/shard_map/ppermute | solution.py:522
  144.7 3.2 %collective-permute-start.27 = (bf16[2,80,256]{2,1,0:T(8,128)(2,1)S(1)}, bf16[2,80,256]{2,1,0:T(8,128)(2,1)S(1)}, u32[]{:S(2)}, u32[]{:S(2)}) collective-permute-start(bf16[2,80,256]{2,1,0:T(8,128)(2,1)S(1)} %pad_maximum_fusion.2), channel_id=1, source_target_pairs={{0,8},{8,16},{16,24},{24,32},{32,40},{40,48},{48,56},{56,0},{64,72... | collective-permute-start | bytes 245768 | tf_op jit(solution)/shard_map/ppermute | solution.py:517
  148.0 5.2 %gather.1.total_ref = f32[1536,256]{1,0:T(8,128)} custom-call(s32[1536,128]{1,0:T(8,128)} %get-tuple-element.22.col_ref, bf16[4,1536,256]{2,1,0:T(8,128)(2,1)} %copy-done, bf16[368,256]{1,0:T(8,128)(2,1)} %copy-done.13, bf16[368,256]{1,0:T(8,128)(2,1)} %copy-done.9, bf16[368,256]{1,0:T(8,128)(2,1)} %copy-done.10, bf16[368,256]{1,0:T(8,128)(2,1)} %copy-done.11), custom_call_target="tpu_custom_call" | custom-call | flops 5500000256 | bytes 1000 | tf_op jit(solution)/shard_map/gather/pallas_call | solution.py:447
  (102 shorter events, 44.7 us)
Async XLA Ops:
  0.0 25.1 %collective-permute-start.2 = (bf16[1536,1024]{1,0:T(8,128)(2,1)}, bf16[1536,1024]{1,0:T(8,128)(2,1)S(1)}, u32[]{:S(2)}, u32[]{:S(2)}) collective-permute-start(bf16[1536,1024]{1,0:T(8,128)(2,1)} %tok_ref.9), channel_id=1, source_target_pairs={{0,1},{1,0},{2,3},{3,2},{4,5},{5,4},{6,7},{7,6},{8,9},{9,8},{10,11... | collective-permute-start | bytes 9437192 | tf_op jit(solution)/shard_map/ppermute | solution.py:526
  5.3 17.0 %collective-permute-start.3 = (bf16[2,1024,512]{2,1,0:T(8,128)(2,1)}, bf16[2,1024,512]{2,1,0:T(8,128)(2,1)}, u32[]{:S(2)}, u32[]{:S(2)}) collective-permute-start(bf16[2,1024,512]{2,1,0:T(8,128)(2,1)} %columns.1), channel_id=1, source_target_pairs={{0,1},{1,0},{2,3},{3,2},{4,5},{5,4},{6,7},{7,6},{8,9},{9,8},{10,11... | collective-permute-start | bytes 6291464 | tf_op jit(solution)/shard_map/ppermute | solution.py:526
  5.9 32.9 %collective-permute-start = (bf16[4,1152,128]{2,1,0:T(8,128)(2,1)S(1)}, bf16[4,1152,128]{2,1,0:T(8,128)(2,1)}, u32[]{:S(2)}, u32[]{:S(2)}) collective-permute-start(bf16[4,1152,128]{2,1,0:T(8,128)(2,1)S(1)} %pad_maximum_fusion.refs_4_.refs_0_), channel_id=1, source_target_pairs={{0,8},{8,16},{16,24},{24,32},{32,40},{40,48},{48,56},{56,0},{64,72... | collective-permute-start | bytes 3538952 | tf_op jit(solution)/shard_map/ppermute | solution.py:517
  7.9 30.9 %collective-permute-start.1 = (bf16[4,1152,128]{2,1,0:T(8,128)(2,1)S(1)}, bf16[4,1152,128]{2,1,0:T(8,128)(2,1)}, u32[]{:S(2)}, u32[]{:S(2)}) collective-permute-start(bf16[4,1152,128]{2,1,0:T(8,128)(2,1)S(1)} %pad_maximum_fusion.refs_4_.refs_0_), channel_id=1, source_target_pairs={{0,56},{8,0},{16,8},{24,16},{32,24},{40,32},{48,40},{56,48},{64,12... | collective-permute-start | bytes 3538952 | tf_op jit(solution)/shard_map/ppermute | solution.py:517
  14.6 55.6 %collective-permute-start.4 = (bf16[592,1024]{1,0:T(8,128)(2,1)}, bf16[592,1024]{1,0:T(8,128)(2,1)}, u32[]{:S(2)}, u32[]{:S(2)}) collective-permute-start(bf16[592,1024]{1,0:T(8,128)(2,1)} %pack.4.refs_0_), channel_id=1, source_target_pairs={{0,64},{8,72},{16,80},{24,88},{32,96},{40,104},{48,112},{56,120},{... | collective-permute-start | bytes 3637256 | tf_op jit(solution)/shard_map/ppermute | solution.py:522
  22.3 49.0 %collective-permute-start.5 = (bf16[592,1024]{1,0:T(8,128)(2,1)}, bf16[592,1024]{1,0:T(8,128)(2,1)}, u32[]{:S(2)}, u32[]{:S(2)}) collective-permute-start(bf16[592,1024]{1,0:T(8,128)(2,1)} %pack.6.refs_2_), channel_id=1, source_target_pairs={{0,128},{8,136},{16,144},{24,152},{32,160},{40,168},{48,176},{56,1... | collective-permute-start | bytes 3637256 | tf_op jit(solution)/shard_map/ppermute | solution.py:522
  25.1 52.1 %collective-permute-start.6 = (bf16[592,1024]{1,0:T(8,128)(2,1)}, bf16[592,1024]{1,0:T(8,128)(2,1)}, u32[]{:S(2)}, u32[]{:S(2)}) collective-permute-start(bf16[592,1024]{1,0:T(8,128)(2,1)} %pack.5.refs_1_), channel_id=1, source_target_pairs={{0,192},{8,200},{16,208},{24,216},{32,224},{40,232},{48,240},{56,2... | collective-permute-start | bytes 3637256 | tf_op jit(solution)/shard_map/ppermute | solution.py:522
  38.9 28.0 %collective-permute-start.7 = (bf16[4,1152,128]{2,1,0:T(8,128)(2,1)}, bf16[4,1152,128]{2,1,0:T(8,128)(2,1)}, u32[]{:S(2)}, u32[]{:S(2)}) collective-permute-start(bf16[4,1152,128]{2,1,0:T(8,128)(2,1)} %collective-permute-done.refs_5_.refs_1_), channel_id=1, source_target_pairs={{0,8},{8,16},{16,24},{24,32},{32,40},{40,48},{48,56},{56,0},{64,72... | collective-permute-start | bytes 3538952 | tf_op jit(solution)/shard_map/ppermute | solution.py:517
  42.0 28.3 %collective-permute-start.8 = (bf16[4,1152,128]{2,1,0:T(8,128)(2,1)}, bf16[4,1152,128]{2,1,0:T(8,128)(2,1)}, u32[]{:S(2)}, u32[]{:S(2)}) collective-permute-start(bf16[4,1152,128]{2,1,0:T(8,128)(2,1)} %collective-permute-done.1.refs_6_.refs_2_), channel_id=1, source_target_pairs={{0,56},{8,0},{16,8},{24,16},{32,24},{40,32},{48,40},{56,48},{64,12... | collective-permute-start | bytes 3538952 | tf_op jit(solution)/shard_map/ppermute | solution.py:517
  42.0 50.4 %all-to-all-start = ((bf16[4,1536,256]{2,1,0:T(8,128)(2,1)}), bf16[4,1536,256]{2,1,0:T(8,128)(2,1)S(1)}, u32[]{:S(2)}, u32[]{:S(2)}) async-start(bf16[4,1536,256]{2,1,0:T(8,128)(2,1)} %base.1), calls=%async_computation | async-start | bytes 6291456 | tf_op jit(solution)/shard_map/all_to_all | solution.py:562
  66.9 29.5 %collective-permute-start.16 = (bf16[4,1152,128]{2,1,0:T(8,128)(2,1)}, bf16[4,1152,128]{2,1,0:T(8,128)(2,1)}, u32[]{:S(2)}, u32[]{:S(2)}) collective-permute-start(bf16[4,1152,128]{2,1,0:T(8,128)(2,1)} %collective-permute-done.7.refs_7_.refs_3_), channel_id=1, source_target_pairs={{0,8},{8,16},{16,24},{24,32},{32,40},{40,48},{48,56},{56,0},{64,72... | collective-permute-start | bytes 3538952 | tf_op jit(solution)/shard_map/ppermute | solution.py:517
  70.3 30.4 %collective-permute-start.17 = (bf16[4,1152,128]{2,1,0:T(8,128)(2,1)}, bf16[4,1152,128]{2,1,0:T(8,128)(2,1)}, u32[]{:S(2)}, u32[]{:S(2)}) collective-permute-start(bf16[4,1152,128]{2,1,0:T(8,128)(2,1)} %collective-permute-done.8.refs_8_.refs_4_), channel_id=1, source_target_pairs={{0,56},{8,0},{16,8},{24,16},{32,24},{40,32},{48,40},{56,48},{64,12... | collective-permute-start | bytes 3538952 | tf_op jit(solution)/shard_map/ppermute | solution.py:517
  87.2 17.5 %collective-permute-start.18 = (bf16[2,80,1024]{2,1,0:T(8,128)(2,1)}, bf16[2,80,1024]{2,1,0:T(8,128)(2,1)}, u32[]{:S(2)}, u32[]{:S(2)}) collective-permute-start(bf16[2,80,1024]{2,1,0:T(8,128)(2,1)} %get-tuple-element.27.refs_9_), channel_id=1, source_target_pairs={{0,8},{8,16},{16,24},{24,32},{32,40},{40,48},{48,56},{56,0},{64,72... | collective-permute-start | bytes 983048 | tf_op jit(solution)/shard_map/ppermute | solution.py:517
  90.3 14.4 %collective-permute-start.19 = (bf16[2,80,1024]{2,1,0:T(8,128)(2,1)}, bf16[2,80,1024]{2,1,0:T(8,128)(2,1)}, u32[]{:S(2)}, u32[]{:S(2)}) collective-permute-start(bf16[2,80,1024]{2,1,0:T(8,128)(2,1)} %get-tuple-element.34), channel_id=1, source_target_pairs={{0,56},{8,0},{16,8},{24,16},{32,24},{40,32},{48,40},{56,48},{64,12... | collective-permute-start | bytes 983048 | tf_op jit(solution)/shard_map/ppermute | solution.py:517
  107.1 8.4 %collective-permute-start.11 = (bf16[2,368,128]{2,1,0:T(8,128)(2,1)S(1)}, bf16[2,368,128]{2,1,0:T(8,128)(2,1)S(1)}, u32[]{:S(2)}, u32[]{:S(2)}) collective-permute-start(bf16[2,368,128]{2,1,0:T(8,128)(2,1)S(1)} %add_convert_fusion.3._), channel_id=1, source_target_pairs={{0,6},{1,7},{2,4},{3,5},{4,2},{5,3},{6,0},{7,1},{8,14},{9,15},{10,... | collective-permute-start | bytes 565256 | tf_op jit(solution)/shard_map/ppermute | solution.py:535
  110.5 7.5 %collective-permute-start.21 = (bf16[4,224,128]{2,1,0:T(8,128)(2,1)S(1)}, bf16[4,224,128]{2,1,0:T(8,128)(2,1)S(1)}, u32[]{:S(2)}, u32[]{:S(2)}) collective-permute-start(bf16[4,224,128]{2,1,0:T(8,128)(2,1)S(1)} %add_convert_fusion.1), channel_id=1, source_target_pairs={{0,2},{1,3},{2,0},{3,1},{4,6},{5,7},{6,4},{7,5},{8,10},{9,11},{10,... | collective-permute-start | bytes 688136 | tf_op jit(solution)/shard_map/ppermute | solution.py:530
  118.1 16.0 %collective-permute-start.22 = (bf16[4,224,128]{2,1,0:T(8,128)(2,1)S(1)}, bf16[4,224,128]{2,1,0:T(8,128)(2,1)S(1)}, u32[]{:S(2)}, u32[]{:S(2)}) collective-permute-start(bf16[4,224,128]{2,1,0:T(8,128)(2,1)S(1)} %add_convert_fusion.mine_ref), channel_id=1, source_target_pairs={{0,6},{1,7},{2,4},{3,5},{4,2},{5,3},{6,0},{7,1},{8,14},{9,15},{10,... | collective-permute-start | bytes 688136 | tf_op jit(solution)/shard_map/ppermute | solution.py:535
  121.4 7.7 %collective-permute-start.13 = (bf16[368,256]{1,0:T(8,128)(2,1)S(1)}, bf16[368,256]{1,0:T(8,128)(2,1)S(1)}, u32[]{:S(2)}, u32[]{:S(2)}) collective-permute-start(bf16[368,256]{1,0:T(8,128)(2,1)S(1)} %get-tuple-element.31), channel_id=1, source_target_pairs={{0,192},{8,200},{16,208},{24,216},{32,224},{40,232},{48,240},{56,2... | collective-permute-start | bytes 565256 | tf_op jit(solution)/shard_map/ppermute | solution.py:522
  122.9 9.2 %collective-permute-start.14 = (bf16[368,256]{1,0:T(8,128)(2,1)S(1)}, bf16[368,256]{1,0:T(8,128)(2,1)S(1)}, u32[]{:S(2)}, u32[]{:S(2)}) collective-permute-start(bf16[368,256]{1,0:T(8,128)(2,1)S(1)} %get-tuple-element.32), channel_id=1, source_target_pairs={{0,128},{8,136},{16,144},{24,152},{32,160},{40,168},{48,176},{56,1... | collective-permute-start | bytes 565256 | tf_op jit(solution)/shard_map/ppermute | solution.py:522
  123.3 10.8 %collective-permute-start.15 = (bf16[368,256]{1,0:T(8,128)(2,1)S(1)}, bf16[368,256]{1,0:T(8,128)(2,1)S(1)}, u32[]{:S(2)}, u32[]{:S(2)}) collective-permute-start(bf16[368,256]{1,0:T(8,128)(2,1)S(1)} %get-tuple-element.33), channel_id=1, source_target_pairs={{0,64},{8,72},{16,80},{24,88},{32,96},{40,104},{48,112},{56,120},{... | collective-permute-start | bytes 565256 | tf_op jit(solution)/shard_map/ppermute | solution.py:522
  136.5 8.2 %collective-permute-start.24 = (bf16[224,256]{1,0:T(8,128)(2,1)S(1)}, bf16[224,256]{1,0:T(8,128)(2,1)S(1)}, u32[]{:S(2)}, u32[]{:S(2)}) collective-permute-start(bf16[224,256]{1,0:T(8,128)(2,1)S(1)} %get-tuple-element.37), channel_id=1, source_target_pairs={{0,128},{8,136},{16,144},{24,152},{32,160},{40,168},{48,176},{56,1... | collective-permute-start | bytes 344072 | tf_op jit(solution)/shard_map/ppermute | solution.py:522
  136.9 7.8 %collective-permute-start.25 = (bf16[224,256]{1,0:T(8,128)(2,1)S(1)}, bf16[224,256]{1,0:T(8,128)(2,1)S(1)}, u32[]{:S(2)}, u32[]{:S(2)}) collective-permute-start(bf16[224,256]{1,0:T(8,128)(2,1)S(1)} %get-tuple-element.38), channel_id=1, source_target_pairs={{0,64},{8,72},{16,80},{24,88},{32,96},{40,104},{48,112},{56,120},{... | collective-permute-start | bytes 344072 | tf_op jit(solution)/shard_map/ppermute | solution.py:522
  141.8 11.4 %collective-permute-start.26 = (bf16[2,80,256]{2,1,0:T(8,128)(2,1)S(1)}, bf16[2,80,256]{2,1,0:T(8,128)(2,1)S(1)}, u32[]{:S(2)}, u32[]{:S(2)}) collective-permute-start(bf16[2,80,256]{2,1,0:T(8,128)(2,1)S(1)} %pad_maximum_fusion.1), channel_id=1, source_target_pairs={{0,56},{8,0},{16,8},{24,16},{32,24},{40,32},{48,40},{56,48},{64,12... | collective-permute-start | bytes 245768 | tf_op jit(solution)/shard_map/ppermute | solution.py:517
  144.7 8.5 %collective-permute-start.27 = (bf16[2,80,256]{2,1,0:T(8,128)(2,1)S(1)}, bf16[2,80,256]{2,1,0:T(8,128)(2,1)S(1)}, u32[]{:S(2)}, u32[]{:S(2)}) collective-permute-start(bf16[2,80,256]{2,1,0:T(8,128)(2,1)S(1)} %pad_maximum_fusion.2), channel_id=1, source_target_pairs={{0,8},{8,16},{16,24},{24,32},{32,40},{40,48},{48,56},{56,0},{64,72... | collective-permute-start | bytes 245768 | tf_op jit(solution)/shard_map/ppermute | solution.py:517
  (25 other events, 196.7 us)

commit v5 on v4

--- a/solution.py
+++ b/solution.py
@@ -32,7 +32,7 @@
 MIB = 1024 * 1024
 VMEM = 56 * MIB
 COST = {
-    "route": 3, "pack": 3, "columns": 2, "base": 11, "carve": 1, "shrink_near": 3, "expand_near": 3,
+    "route": 3, "pack": 3, "base": 11, "carve": 1, "shrink_near": 3, "expand_near": 3,
     "shrink_far": 100, "shrink_late": 3, "expand_late": 30, "gather": 5, "finish": 5,
 }
 VMEM = 56 * 1024 * 1024
@@ -126,29 +126,6 @@
     )(row, tokens, *earlier)
 
 
-def columns_kernel(place_ref, w_ref, out_ref):
-    out_ref[...] = w_ref[...]
-
-
-def other_columns(place, weight):
-    width = weight.shape[1]
-    return pl.pallas_call(
-        columns_kernel,
-        grid_spec=pltpu.PrefetchScalarGridSpec(
-            num_scalar_prefetch=1,
-            grid=(NY,),
-            in_specs=[
-                pl.BlockSpec((2, width, 128), lambda i, place: (0, 0, i * 2 + 1 - place[2]))
-            ],
-            out_specs=pl.BlockSpec((2, width, 128), lambda i, place: (0, 0, i)),
-        ),
-        out_shape=jax.ShapeDtypeStruct((2, width, NY * 128), BF16),
-        compiler_params=params("arbitrary"),
-        cost_estimate=cost(COST["columns"]),
-        name="columns",
-    )(place, weight)
-
-
 def base_kernel(place_ref, tok_ref, w_ref, other_tok_ref, other_w_ref, *refs):
     total = jnp.zeros(refs[-1].shape[1:], F32)
     for t_ref, panel_ref in ((tok_ref, w_ref), (other_tok_ref, other_w_ref)):
@@ -160,17 +137,13 @@
 def base(place, tokens, weight, other_tokens, other_weight, *earlier):
     count, width = tokens.shape
     rows = pl.BlockSpec((count, width), lambda i, place: (0, 0))
+    columns = pl.BlockSpec((2, width, 128), lambda i, place: (0, 0, i * 2 + place[2]))
     return pl.pallas_call(
         base_kernel,
         grid_spec=pltpu.PrefetchScalarGridSpec(
             num_scalar_prefetch=1,
             grid=(NY,),
-            in_specs=[
-                rows,
-                pl.BlockSpec((2, width, 128), lambda i, place: (0, 0, i * 2 + place[2])),
-                rows,
-                pl.BlockSpec((2, width, 128), lambda i, place: (0, 0, i)),
-            ]
+            in_specs=[rows, columns, rows, columns]
             + [pl.BlockSpec(memory_space=pl.ANY)] * len(earlier),
             out_specs=pl.BlockSpec((1, count, 256), lambda i, place: (i, 0, 0)),
         ),
@@ -287,7 +260,7 @@
         + [pl.BlockSpec(memory_space=pl.ANY)] * len(earlier),
         out_specs=pl.BlockSpec((NX, FAR_ROWS, 128), lambda i: (0, 0, 0)),
         scratch_shapes=[pltpu.VMEM((NX, FAR_ROWS, 128), F32)],
-        compiler_params=params("arbitrary", limit=16 * MIB),
+        compiler_params=params("arbitrary"),
         cost_estimate=cost(COST["shrink_far"]),
         name="shrink_far",
     )(*xs, *panels, *earlier)
@@ -311,7 +284,7 @@
         + [pl.BlockSpec((LOCAL, width, 128), lambda i: (0, 0, 0)) for w in panels]
         + [pl.BlockSpec(memory_space=pl.ANY)],
         out_specs=pl.BlockSpec((NX, LATE_ROWS, 128), lambda i: (0, 0, 0)),
-        compiler_params=params("arbitrary", limit=16 * MIB),
+        compiler_params=params("arbitrary"),
         cost_estimate=cost(COST["shrink_late"]),
         name="shrink_late",
     )(far, *guests, *panels, earlier)
@@ -368,7 +341,7 @@
             pltpu.VMEM((NX, NEAR_ROWS, 256), F32),
             pltpu.VMEM((NX, NEAR_ROWS, 128), BF16),
         ],
-        compiler_params=params("arbitrary", limit=24 * MIB),
+        compiler_params=params("arbitrary"),
         cost_estimate=cost(COST["expand_near"]),
         name="expand_near",
     )(place, mine, other, *panels)
@@ -411,7 +384,7 @@
             pltpu.VMEM((LOCAL * 128, 256), BF16),
             pltpu.VMEM((NX, LATE_ROWS, 256), F32),
         ],
-        compiler_params=params("arbitrary", limit=24 * MIB),
+        compiler_params=params("arbitrary"),
         cost_estimate=cost(COST["expand_late"]),
         name="expand_late",
     )(mine, other, *panels, *earlier)
@@ -552,7 +525,7 @@
     cw1, ccw1 = along_z(panels, 1), along_z(panels, -1)
 
     other_tokens = with_core(tokens)
-    other_weight = with_core(other_columns(place, weight))
+    other_weight = with_core(weight)
     row, col = route(place, ident.reshape(1, -1), store.reshape(1, -1))
     packed = {e: pack(e, row, tokens) for e in (1, 3, 2)}
     moved = {e: along_x(packed[e], e) for e in (1, 3, 2)}
@@ -570,11 +543,12 @@
     keep, send = shrink_near(place, xs, held, upward)
     near_chip = add(keep, with_core(send))
     near_pair = add(near_chip, with_even(near_chip))
-    near = add(near_pair, with_odd(near_pair))
-    near = home(expand_near(place, near, with_core(near), held))
-
-    late = shrink_far(xs, [cw3, ccw3], near_chip, parts)
-    late = shrink_late(late, guests, [cw3, ccw3], near_pair)
+    near_pair, cw3, ccw3 = lax.optimization_barrier((near_pair, cw3, ccw3))
+    near_sum = add(near_pair, with_odd(near_pair))
+    near = home(expand_near(place, near_sum, with_core(near_sum), held))
+
+    late = shrink_far(xs, [cw3, ccw3], near_pair, parts)
+    late = shrink_late(late, guests, [cw3, ccw3], near_sum)
     late = add(late, with_core(late))
     late = add(late, with_even(late))
     total = gather(col, parts, near)

time: 158 us -> 166 us (1.051)
  other arithmetic: 1.04 us -> 5.92 us
  local copies, waits for them, and re-layouts: 5.57 us -> 10.4 us
  starting transfers between devices: 36.8 us -> 39.8 us
  Pallas kernels: 53.7 us -> 51.4 us
    ppermute x2, waiting for transfers between devices: 4.4 us -> 9.24 us  [with_even(): return lax.ppermute(array, 'tp', [(i, i ^ 2) for i in range(2 * NY)])]
    pallas_call x1 -> x0, Pallas kernels: 4.67 us -> none  [other_columns(): pl.pallas_call(columns_kernel, grid_spec=pltpu.PrefetchScalarGridSpec(num...]
    ppermute x2, waiting for transfers between devices: 4.78 us -> 0.35 us  [with_odd(): return lax.ppermute(array, 'tp', pairs)]
    unnamed x40 -> x46, local copies, waits for them, and re-layouts: 5.56 us -> 9.63 us
    ppermute x9, waiting for transfers between devices: 23.9 us -> 21.1 us  [along_x(): return lax.ppermute(array, 'ad', pairs)]
    convert_element_type x5, other arithmetic: 0.29 us -> 2.84 us  [add(): return (a.astype(F32) + b.astype(F32)).astype(BF16)]
    concatenate x1, other arithmetic: 0.08 us -> 2.4 us  [body(): panels = jnp.concatenate([down, up.reshape(LOCAL, 128, 128)], axis=1)]
    ppermute x5, waiting for transfers between devices: 1.43 us -> 3.12 us  [with_core(): return lax.ppermute(array, 'tp', [(i, i ^ 1) for i in range(2 * NY)])]
  transfers between devices with their start and end apart: 29 -> 29, of which waited for: 15 -> 16; matrix products, arithmetic and copies ran while one was open for 1% -> 3% of each run, Pallas kernels for 30% -> 26%
where the time goes in v5:
time: 166 us
  waiting for transfers between devices  58.1 us (35%)
  Pallas kernels  51.4 us (31%)
  starting transfers between devices  39.8 us (24%)
  local copies, waits for them, and re-layouts  10.4 us (6%)
  other arithmetic  5.92 us (4%)
    ppermute x10, waiting for transfers between devices, along_z(): return lax.ppermute(array, 'ad', pairs)  24.3 us
    ppermute x9, waiting for transfers between devices, along_x(): return lax.ppermute(array, 'ad', pairs)  21.1 us
    ppermute x10, starting transfers between devices, along_z(): return lax.ppermute(array, 'ad', pairs)  14.7 us
    pallas_call x1, Pallas kernels, base(): pl.pallas_call(base_kernel, grid_spec=pltpu.PrefetchScalarGridSpec(num_sc...  12.1 us
    ppermute x9, starting transfers between devices, along_x(): return lax.ppermute(array, 'ad', pairs)  11.5 us
    pallas_call x4, Pallas kernels, pack(): pl.pallas_call(functools.partial(pack_kernel, e), out_shape=jax.ShapeDtyp...  11.4 us
    unnamed x46, local copies, waits for them, and re-layouts  9.63 us
    ppermute x2, waiting for transfers between devices, with_even(): return lax.ppermute(array, 'tp', [(i, i ^ 2) for i in range(2 * NY)])  9.24 us
  transfers between devices with their start and end apart: 29, of which 16 were waited for; matrix products, arithmetic and copies ran while one was open for 3% of the time, Pallas kernels for 26%

profile of v5, /device:TPU:64, one launch (start us, length us, event | category | flops | bytes accessed | tf_op | source)
XLA Modules:
  0.0 165.9 jit_solution(5520242714824827926)
XLA Ops:
  5.6 2.8 %route.1 = (s32[1,1536]{1,0:T(1,128)}, s32[1536,128]{1,0:T(8,128)}) custom-call(s32[3]{0:T(128)} %pad_add_fusion.place_ref, s32[1,1536]{1,0:T(1,128)} %bitcast.16, s32[1,128]{1,0:T(1,128)} %bitcast.17), custom_call_target="tpu_custom_call" | custom-call | flops 3300000000 | bytes 1000 | tf_op jit(solution)/shard_map/route/pallas_call | solution.py:95
  9.1 3.1 %pack.4.refs_0_ = bf16[592,1024]{1,0:T(8,128)(2,1)} custom-call(s32[1,1536]{1,0:T(1,128)S(1)} %copy-done.9, bf16[1536,1024]{1,0:T(8,128)(2,1)S(1)} %copy-done.5), custom_call_target="tpu_custom_call" | custom-call | flops 3300000000 | bytes 1000 | tf_op jit(solution)/shard_map/pack/pallas_call | solution.py:118
  13.7 3.2 %pack.5.refs_1_ = bf16[592,1024]{1,0:T(8,128)(2,1)} custom-call(s32[1,1536]{1,0:T(1,128)S(1)} %copy-done.9, bf16[1536,1024]{1,0:T(8,128)(2,1)S(1)} %copy-done.5), custom_call_target="tpu_custom_call" | custom-call | flops 3300000000 | bytes 1000 | tf_op jit(solution)/shard_map/pack/pallas_call | solution.py:118
  16.8 3.1 %pack.6.refs_2_ = bf16[592,1024]{1,0:T(8,128)(2,1)} custom-call(s32[1,1536]{1,0:T(1,128)S(1)} %copy-done.9, bf16[1536,1024]{1,0:T(8,128)(2,1)S(1)} %copy-done.5), custom_call_target="tpu_custom_call" | custom-call | flops 3300000000 | bytes 1000 | tf_op jit(solution)/shard_map/pack/pallas_call | solution.py:118
  24.1 12.1 %base.1 = bf16[4,1536,256]{2,1,0:T(8,128)(2,1)} custom-call(s32[3]{0:T(128)} %pad_add_fusion.place_ref, bf16[1536,1024]{1,0:T(8,128)(2,1)} %tok_ref.9, bf16[2,1024,1024]{2,1,0:T(8,128)(2,1)} %w_ref.1, bf16[1536,1024]{1,0:T(8,128)(2,1)} %collective-permute-done.2.other_tok_ref, bf16[2,1024,1024]{2,1,0:T(8,128)(2,1)} %collective-permute-done.3.other_w_ref, ...), custom_call_target="tpu_custom_call" | custom-call | flops 12099999744 | bytes 1000 | tf_op jit(solution)/shard_map/base/pallas_call | solution.py:141
  36.2 3.3 %collective-permute-start.7 = (bf16[4,1152,128]{2,1,0:T(8,128)(2,1)}, bf16[4,1152,128]{2,1,0:T(8,128)(2,1)}, u32[]{:S(2)}, u32[]{:S(2)}) collective-permute-start(bf16[4,1152,128]{2,1,0:T(8,128)(2,1)} %collective-permute-done.refs_5_.refs_1_), channel_id=1, source_target_pairs={{0,8},{8,16},{16,24},{24,32},{32,40},{40,48},{48,56},{56,0},{64,72... | collective-permute-start | bytes 3538952 | tf_op jit(solution)/shard_map/ppermute | solution.py:490
  39.5 4.7 %all-to-all-start = ((bf16[4,1536,256]{2,1,0:T(8,128)(2,1)}), bf16[4,1536,256]{2,1,0:T(8,128)(2,1)}, u32[]{:S(2)}, u32[]{:S(2)}) async-start(bf16[4,1536,256]{2,1,0:T(8,128)(2,1)} %base.1), calls=%async_computation | async-start | bytes 6291456 | tf_op jit(solution)/shard_map/all_to_all | solution.py:535
  48.1 15.9 %collective-permute-done.7.refs_7_.refs_3_ = bf16[4,1152,128]{2,1,0:T(8,128)(2,1)} collective-permute-done((bf16[4,1152,128]{2,1,0:T(8,128)(2,1)}, bf16[4,1152,128]{2,1,0:T(8,128)(2,1)}, u32[]{:S(2)}, u32[]{:S(2)}) %collective-permute-start.7) | collective-permute-done | bytes 1179680 | tf_op jit(solution)/shard_map/ppermute | solution.py:490
  64.1 3.0 %collective-permute-start.11 = (bf16[4,1152,128]{2,1,0:T(8,128)(2,1)}, bf16[4,1152,128]{2,1,0:T(8,128)(2,1)S(1)}, u32[]{:S(2)}, u32[]{:S(2)}) collective-permute-start(bf16[4,1152,128]{2,1,0:T(8,128)(2,1)} %collective-permute-done.7.refs_7_.refs_3_), channel_id=1, source_target_pairs={{0,8},{8,16},{16,24},{24,32},{32,40},{40,48},{48,56},{56,0},{64,72... | collective-permute-start | bytes 3538952 | tf_op jit(solution)/shard_map/ppermute | solution.py:490
  68.7 6.0 %collective-permute-done.6.refs_3_ = bf16[592,1024]{1,0:T(8,128)(2,1)} collective-permute-done((bf16[592,1024]{1,0:T(8,128)(2,1)}, bf16[592,1024]{1,0:T(8,128)(2,1)}, u32[]{:S(2)}, u32[]{:S(2)}) %collective-permute-start.6) | collective-permute-done | bytes 1212448 | tf_op jit(solution)/shard_map/ppermute | solution.py:495
  75.7 4.6 %shrink_near.1 = (bf16[2,368,128]{2,1,0:T(8,128)(2,1)S(1)}, bf16[2,368,128]{2,1,0:T(8,128)(2,1)S(1)}) custom-call(s32[3]{0:T(128)S(1)} %copy-done.4, bf16[592,1024]{1,0:T(8,128)(2,1)S(1)} %pack.7.refs_0_, bf16[592,1024]{1,0:T(8,128)(2,1)S(1)} %collective-permute-done.4.refs_1_, bf16[592,1024]{1,0:T(8,128)(2,1)S(1)} %collective-permute-done.5.refs_2_, ...), custom_call_target="tpu_custom_call" | custom-call | flops 3300000000 | bytes 1000 | tf_op jit(solution)/shard_map/shrink_near/pallas_call | solution.py:203
  83.6 3.1 %collective-permute-start.18 = (bf16[2,80,1024]{2,1,0:T(8,128)(2,1)S(1)}, bf16[2,80,1024]{2,1,0:T(8,128)(2,1)S(1)}, u32[]{:S(2)}, u32[]{:S(2)}) collective-permute-start(bf16[2,80,1024]{2,1,0:T(8,128)(2,1)S(1)} %get-tuple-element.30.refs_9_), channel_id=1, source_target_pairs={{0,8},{8,16},{16,24},{24,32},{32,40},{40,48},{48,56},{56,0},{64,72... | collective-permute-start | bytes 983048 | tf_op jit(solution)/shard_map/ppermute | solution.py:490
  88.9 4.9 %collective-permute-done.11.refs_4_.low_ref.refs_0_ = bf16[4,1152,128]{2,1,0:T(8,128)(2,1)S(1)} collective-permute-done((bf16[4,1152,128]{2,1,0:T(8,128)(2,1)}, bf16[4,1152,128]{2,1,0:T(8,128)(2,1)S(1)}, u32[]{:S(2)}, u32[]{:S(2)}) %collective-permute-start.11) | collective-permute-done | bytes 1179680 | tf_op jit(solution)/shard_map/ppermute | solution.py:490
  94.9 3.0 %collective-permute-done.12.refs_5_.high_ref.refs_1_ = bf16[4,1152,128]{2,1,0:T(8,128)(2,1)S(1)} collective-permute-done((bf16[4,1152,128]{2,1,0:T(8,128)(2,1)}, bf16[4,1152,128]{2,1,0:T(8,128)(2,1)S(1)}, u32[]{:S(2)}, u32[]{:S(2)}) %collective-permute-start.12) | collective-permute-done | bytes 1179680 | tf_op jit(solution)/shard_map/ppermute | solution.py:490
  98.9 3.0 %collective-permute-start.13 = (bf16[2,368,128]{2,1,0:T(8,128)(2,1)S(1)}, bf16[2,368,128]{2,1,0:T(8,128)(2,1)S(1)}, u32[]{:S(2)}, u32[]{:S(2)}) collective-permute-start(bf16[2,368,128]{2,1,0:T(8,128)(2,1)S(1)} %add_convert_fusion.3.refs_6_), channel_id=1, source_target_pairs={{0,6},{1,7},{2,4},{3,5},{4,2},{5,3},{6,0},{7,1},{8,14},{9,15},{10,... | collective-permute-start | bytes 565256 | tf_op jit(solution)/shard_map/ppermute | solution.py:508
  101.9 3.4 %shrink_far.1.far_ref = bf16[4,144,128]{2,1,0:T(8,128)(2,1)} custom-call(bf16[592,1024]{1,0:T(8,128)(2,1)} %copy-done.2, bf16[592,1024]{1,0:T(8,128)(2,1)} %copy-done, bf16[592,1024]{1,0:T(8,128)(2,1)} %copy-done.1, bf16[592,1024]{1,0:T(8,128)(2,1)} %collective-permute-done.6.refs_3_, bf16[4,1152,128]{2,1,0:T(8,128)(2,1)} %copy-done.14, ...), custom_call_target="tpu_custom_call" | custom-call | flops 109999996928 | bytes 1000 | tf_op jit(solution)/shard_map/shrink_far/pallas_call | solution.py:251
  108.8 3.0 %shrink_late.1 = bf16[4,224,128]{2,1,0:T(8,128)(2,1)} custom-call(bf16[4,144,128]{2,1,0:T(8,128)(2,1)} %shrink_far.1.far_ref, bf16[2,80,1024]{2,1,0:T(8,128)(2,1)} %copy-done.16, bf16[2,80,1024]{2,1,0:T(8,128)(2,1)} %copy-done.17, bf16[4,1152,128]{2,1,0:T(8,128)(2,1)} %copy-done.14, bf16[4,1152,128]{2,1,0:T(8,128)(2,1)} %copy-done.15, ...), custom_call_target="tpu_custom_call" | custom-call | flops 3300000000 | bytes 1000 | tf_op jit(solution)/shard_map/shrink_late/pallas_call | solution.py:279
  115.1 7.2 %collective-permute-done.21 = bf16[4,224,128]{2,1,0:T(8,128)(2,1)S(1)} collective-permute-done((bf16[4,224,128]{2,1,0:T(8,128)(2,1)S(1)}, bf16[4,224,128]{2,1,0:T(8,128)(2,1)S(1)}, u32[]{:S(2)}, u32[]{:S(2)}) %collective-permute-start.21) | collective-permute-done | bytes 229408 | tf_op jit(solution)/shard_map/ppermute | solution.py:503
  122.3 3.1 %collective-permute-start.22 = (bf16[4,224,128]{2,1,0:T(8,128)(2,1)S(1)}, bf16[4,224,128]{2,1,0:T(8,128)(2,1)S(1)}, u32[]{:S(2)}, u32[]{:S(2)}) collective-permute-start(bf16[4,224,128]{2,1,0:T(8,128)(2,1)S(1)} %add_convert_fusion.mine_ref), channel_id=1, source_target_pairs={{0,6},{1,7},{2,4},{3,5},{4,2},{5,3},{6,0},{7,1},{8,14},{9,15},{10,... | collective-permute-start | bytes 688136 | tf_op jit(solution)/shard_map/ppermute | solution.py:508
  126.1 2.8 %expand_near.1 = (bf16[368,256]{1,0:T(8,128)(2,1)}, bf16[368,256]{1,0:T(8,128)(2,1)}, bf16[368,256]{1,0:T(8,128)(2,1)}, bf16[368,256]{1,0:T(8,128)(2,1)}) custom-call(s32[3]{0:T(128)} %pad_add_fusion.place_ref, bf16[2,368,128]{2,1,0:T(8,128)(2,1)} %add_convert_fusion.2.mine_ref._, bf16[2,368,128]{2,1,0:T(8,128)(2,1)} %copy-done.22, ...), custom_call_target="tpu_custom_call" | custom-call | flops 3300000000 | bytes 1000 | tf_op jit(solution)/shard_map/expand_near/pallas_call | solution.py:333
  131.6 5.2 %collective-permute-done.15.refs_1_.refs_2_ = bf16[368,256]{1,0:T(8,128)(2,1)S(1)} collective-permute-done((bf16[368,256]{1,0:T(8,128)(2,1)}, bf16[368,256]{1,0:T(8,128)(2,1)S(1)}, u32[]{:S(2)}, u32[]{:S(2)}) %collective-permute-start.15) | collective-permute-done | bytes 188448 | tf_op jit(solution)/shard_map/ppermute | solution.py:495
  149.9 3.5 %collective-permute-done.25.refs_3_ = bf16[224,256]{1,0:T(8,128)(2,1)S(1)} collective-permute-done((bf16[224,256]{1,0:T(8,128)(2,1)}, bf16[224,256]{1,0:T(8,128)(2,1)S(1)}, u32[]{:S(2)}, u32[]{:S(2)}) %collective-permute-start.25) | collective-permute-done | bytes 114720 | tf_op jit(solution)/shard_map/ppermute | solution.py:495
  153.4 3.2 %collective-permute-start.27 = (bf16[2,80,256]{2,1,0:T(8,128)(2,1)S(1)}, bf16[2,80,256]{2,1,0:T(8,128)(2,1)S(1)}, u32[]{:S(2)}, u32[]{:S(2)}) collective-permute-start(bf16[2,80,256]{2,1,0:T(8,128)(2,1)S(1)} %pad_maximum_fusion.2), channel_id=1, source_target_pairs={{0,8},{8,16},{16,24},{24,32},{32,40},{40,48},{48,56},{56,0},{64,72... | collective-permute-start | bytes 245768 | tf_op jit(solution)/shard_map/ppermute | solution.py:490
  156.6 5.2 %gather.1.total_ref = f32[1536,256]{1,0:T(8,128)} custom-call(s32[1536,128]{1,0:T(8,128)} %get-tuple-element.25.col_ref, bf16[4,1536,256]{2,1,0:T(8,128)(2,1)} %all-to-all-done.base_ref.refs_7_, bf16[368,256]{1,0:T(8,128)(2,1)} %get-tuple-element.34.refs_0_, bf16[368,256]{1,0:T(8,128)(2,1)} %copy-done.19, bf16[368,256]{1,0:T(8,128)(2,1)} %copy-done.20, ...), custom_call_target="tpu_custom_call" | custom-call | flops 5500000256 | bytes 1000 | tf_op jit(solution)/shard_map/gather/pallas_call | solution.py:420
  (107 shorter events, 53.2 us)
Async XLA Ops:
  0.0 22.6 %collective-permute-start.3 = (bf16[2,1024,1024]{2,1,0:T(8,128)(2,1)}, bf16[2,1024,1024]{2,1,0:T(8,128)(2,1)}, u32[]{:S(2)}, u32[]{:S(2)}) collective-permute-start(bf16[2,1024,1024]{2,1,0:T(8,128)(2,1)} %w_ref.1), channel_id=1, source_target_pairs={{0,1},{1,0},{2,3},{3,2},{4,5},{5,4},{6,7},{7,6},{8,9},{9,8},{10,11... | collective-permute-start | bytes 12582920 | tf_op jit(solution)/shard_map/ppermute | solution.py:499
  0.0 19.9 %collective-permute-start.2 = (bf16[1536,1024]{1,0:T(8,128)(2,1)}, bf16[1536,1024]{1,0:T(8,128)(2,1)}, u32[]{:S(2)}, u32[]{:S(2)}) collective-permute-start(bf16[1536,1024]{1,0:T(8,128)(2,1)} %tok_ref.9), channel_id=1, source_target_pairs={{0,1},{1,0},{2,3},{3,2},{4,5},{5,4},{6,7},{7,6},{8,9},{9,8},{10,11... | collective-permute-start | bytes 9437192 | tf_op jit(solution)/shard_map/ppermute | solution.py:499
  2.9 33.3 %collective-permute-start = (bf16[4,1152,128]{2,1,0:T(8,128)(2,1)}, bf16[4,1152,128]{2,1,0:T(8,128)(2,1)}, u32[]{:S(2)}, u32[]{:S(2)}) collective-permute-start(bf16[4,1152,128]{2,1,0:T(8,128)(2,1)} %pad_maximum_fusion.refs_4_.refs_0_), channel_id=1, source_target_pairs={{0,8},{8,16},{16,24},{24,32},{32,40},{40,48},{48,56},{56,0},{64,72... | collective-permute-start | bytes 3538952 | tf_op jit(solution)/shard_map/ppermute | solution.py:490
  4.8 31.4 %collective-permute-start.1 = (bf16[4,1152,128]{2,1,0:T(8,128)(2,1)}, bf16[4,1152,128]{2,1,0:T(8,128)(2,1)}, u32[]{:S(2)}, u32[]{:S(2)}) collective-permute-start(bf16[4,1152,128]{2,1,0:T(8,128)(2,1)} %pad_maximum_fusion.refs_4_.refs_0_), channel_id=1, source_target_pairs={{0,56},{8,0},{16,8},{24,16},{32,24},{40,32},{48,40},{56,48},{64,12... | collective-permute-start | bytes 3538952 | tf_op jit(solution)/shard_map/ppermute | solution.py:490
  12.2 55.4 %collective-permute-start.4 = (bf16[592,1024]{1,0:T(8,128)(2,1)}, bf16[592,1024]{1,0:T(8,128)(2,1)S(1)}, u32[]{:S(2)}, u32[]{:S(2)}) collective-permute-start(bf16[592,1024]{1,0:T(8,128)(2,1)} %pack.4.refs_0_), channel_id=1, source_target_pairs={{0,64},{8,72},{16,80},{24,88},{32,96},{40,104},{48,112},{56,120},{... | collective-permute-start | bytes 3637256 | tf_op jit(solution)/shard_map/ppermute | solution.py:495
  19.9 48.8 %collective-permute-start.5 = (bf16[592,1024]{1,0:T(8,128)(2,1)}, bf16[592,1024]{1,0:T(8,128)(2,1)S(1)}, u32[]{:S(2)}, u32[]{:S(2)}) collective-permute-start(bf16[592,1024]{1,0:T(8,128)(2,1)} %pack.6.refs_2_), channel_id=1, source_target_pairs={{0,128},{8,136},{16,144},{24,152},{32,160},{40,168},{48,176},{56,1... | collective-permute-start | bytes 3637256 | tf_op jit(solution)/shard_map/ppermute | solution.py:495
  22.6 52.1 %collective-permute-start.6 = (bf16[592,1024]{1,0:T(8,128)(2,1)}, bf16[592,1024]{1,0:T(8,128)(2,1)}, u32[]{:S(2)}, u32[]{:S(2)}) collective-permute-start(bf16[592,1024]{1,0:T(8,128)(2,1)} %pack.5.refs_1_), channel_id=1, source_target_pairs={{0,192},{8,200},{16,208},{24,216},{32,224},{40,232},{48,240},{56,2... | collective-permute-start | bytes 3637256 | tf_op jit(solution)/shard_map/ppermute | solution.py:495
  36.2 27.9 %collective-permute-start.7 = (bf16[4,1152,128]{2,1,0:T(8,128)(2,1)}, bf16[4,1152,128]{2,1,0:T(8,128)(2,1)}, u32[]{:S(2)}, u32[]{:S(2)}) collective-permute-start(bf16[4,1152,128]{2,1,0:T(8,128)(2,1)} %collective-permute-done.refs_5_.refs_1_), channel_id=1, source_target_pairs={{0,8},{8,16},{16,24},{24,32},{32,40},{40,48},{48,56},{56,0},{64,72... | collective-permute-start | bytes 3538952 | tf_op jit(solution)/shard_map/ppermute | solution.py:490
  39.5 28.0 %collective-permute-start.8 = (bf16[4,1152,128]{2,1,0:T(8,128)(2,1)}, bf16[4,1152,128]{2,1,0:T(8,128)(2,1)}, u32[]{:S(2)}, u32[]{:S(2)}) collective-permute-start(bf16[4,1152,128]{2,1,0:T(8,128)(2,1)} %collective-permute-done.1.refs_6_.refs_2_), channel_id=1, source_target_pairs={{0,56},{8,0},{16,8},{24,16},{32,24},{40,32},{48,40},{56,48},{64,12... | collective-permute-start | bytes 3538952 | tf_op jit(solution)/shard_map/ppermute | solution.py:490
  39.5 62.4 %all-to-all-start = ((bf16[4,1536,256]{2,1,0:T(8,128)(2,1)}), bf16[4,1536,256]{2,1,0:T(8,128)(2,1)}, u32[]{:S(2)}, u32[]{:S(2)}) async-start(bf16[4,1536,256]{2,1,0:T(8,128)(2,1)} %base.1), calls=%async_computation | async-start | bytes 6291456 | tf_op jit(solution)/shard_map/all_to_all | solution.py:535
  64.1 29.7 %collective-permute-start.11 = (bf16[4,1152,128]{2,1,0:T(8,128)(2,1)}, bf16[4,1152,128]{2,1,0:T(8,128)(2,1)S(1)}, u32[]{:S(2)}, u32[]{:S(2)}) collective-permute-start(bf16[4,1152,128]{2,1,0:T(8,128)(2,1)} %collective-permute-done.7.refs_7_.refs_3_), channel_id=1, source_target_pairs={{0,8},{8,16},{16,24},{24,32},{32,40},{40,48},{48,56},{56,0},{64,72... | collective-permute-start | bytes 3538952 | tf_op jit(solution)/shard_map/ppermute | solution.py:490
  67.5 30.3 %collective-permute-start.12 = (bf16[4,1152,128]{2,1,0:T(8,128)(2,1)}, bf16[4,1152,128]{2,1,0:T(8,128)(2,1)S(1)}, u32[]{:S(2)}, u32[]{:S(2)}) collective-permute-start(bf16[4,1152,128]{2,1,0:T(8,128)(2,1)} %collective-permute-done.8.refs_8_.refs_4_), channel_id=1, source_target_pairs={{0,56},{8,0},{16,8},{24,16},{32,24},{40,32},{48,40},{56,48},{64,12... | collective-permute-start | bytes 3538952 | tf_op jit(solution)/shard_map/ppermute | solution.py:490
  82.0 6.9 %collective-permute-start.10 = (bf16[2,368,128]{2,1,0:T(8,128)(2,1)S(1)}, bf16[2,368,128]{2,1,0:T(8,128)(2,1)S(1)}, u32[]{:S(2)}, u32[]{:S(2)}) collective-permute-start(bf16[2,368,128]{2,1,0:T(8,128)(2,1)S(1)} %add_convert_fusion.4), channel_id=1, source_target_pairs={{0,2},{1,3},{2,0},{3,1},{4,6},{5,7},{6,4},{7,5},{8,10},{9,11},{10,... | collective-permute-start | bytes 565256 | tf_op jit(solution)/shard_map/ppermute | solution.py:503
  83.6 23.7 %collective-permute-start.18 = (bf16[2,80,1024]{2,1,0:T(8,128)(2,1)S(1)}, bf16[2,80,1024]{2,1,0:T(8,128)(2,1)S(1)}, u32[]{:S(2)}, u32[]{:S(2)}) collective-permute-start(bf16[2,80,1024]{2,1,0:T(8,128)(2,1)S(1)} %get-tuple-element.30.refs_9_), channel_id=1, source_target_pairs={{0,8},{8,16},{16,24},{24,32},{32,40},{40,48},{48,56},{56,0},{64,72... | collective-permute-start | bytes 983048 | tf_op jit(solution)/shard_map/ppermute | solution.py:490
  86.8 20.6 %collective-permute-start.19 = (bf16[2,80,1024]{2,1,0:T(8,128)(2,1)S(1)}, bf16[2,80,1024]{2,1,0:T(8,128)(2,1)S(1)}, u32[]{:S(2)}, u32[]{:S(2)}) collective-permute-start(bf16[2,80,1024]{2,1,0:T(8,128)(2,1)S(1)} %get-tuple-element.40), channel_id=1, source_target_pairs={{0,56},{8,0},{16,8},{24,16},{32,24},{40,32},{48,40},{56,48},{64,12... | collective-permute-start | bytes 983048 | tf_op jit(solution)/shard_map/ppermute | solution.py:490
  114.5 7.7 %collective-permute-start.21 = (bf16[4,224,128]{2,1,0:T(8,128)(2,1)S(1)}, bf16[4,224,128]{2,1,0:T(8,128)(2,1)S(1)}, u32[]{:S(2)}, u32[]{:S(2)}) collective-permute-start(bf16[4,224,128]{2,1,0:T(8,128)(2,1)S(1)} %add_convert_fusion.1), channel_id=1, source_target_pairs={{0,2},{1,3},{2,0},{3,1},{4,6},{5,7},{6,4},{7,5},{8,10},{9,11},{10,... | collective-permute-start | bytes 688136 | tf_op jit(solution)/shard_map/ppermute | solution.py:503
  115.0 10.5 %collective-permute-start.14 = (bf16[2,368,128]{2,1,0:T(8,128)(2,1)S(1)}, bf16[2,368,128]{2,1,0:T(8,128)(2,1)S(1)}, u32[]{:S(2)}, u32[]{:S(2)}) collective-permute-start(bf16[2,368,128]{2,1,0:T(8,128)(2,1)S(1)} %copy-done.13), channel_id=1, source_target_pairs={{0,1},{1,0},{2,3},{3,2},{4,5},{5,4},{6,7},{7,6},{8,9},{9,8},{10,11... | collective-permute-start | bytes 565256 | tf_op jit(solution)/shard_map/ppermute | solution.py:499
  122.3 18.1 %collective-permute-start.22 = (bf16[4,224,128]{2,1,0:T(8,128)(2,1)S(1)}, bf16[4,224,128]{2,1,0:T(8,128)(2,1)S(1)}, u32[]{:S(2)}, u32[]{:S(2)}) collective-permute-start(bf16[4,224,128]{2,1,0:T(8,128)(2,1)S(1)} %add_convert_fusion.mine_ref), channel_id=1, source_target_pairs={{0,6},{1,7},{2,4},{3,5},{4,2},{5,3},{6,0},{7,1},{8,14},{9,15},{10,... | collective-permute-start | bytes 688136 | tf_op jit(solution)/shard_map/ppermute | solution.py:508
  128.9 7.9 %collective-permute-start.15 = (bf16[368,256]{1,0:T(8,128)(2,1)}, bf16[368,256]{1,0:T(8,128)(2,1)S(1)}, u32[]{:S(2)}, u32[]{:S(2)}) collective-permute-start(bf16[368,256]{1,0:T(8,128)(2,1)} %get-tuple-element.35), channel_id=1, source_target_pairs={{0,192},{8,200},{16,208},{24,216},{32,224},{40,232},{48,240},{56,2... | collective-permute-start | bytes 565256 | tf_op jit(solution)/shard_map/ppermute | solution.py:495
  129.2 9.2 %collective-permute-start.16 = (bf16[368,256]{1,0:T(8,128)(2,1)}, bf16[368,256]{1,0:T(8,128)(2,1)S(1)}, u32[]{:S(2)}, u32[]{:S(2)}) collective-permute-start(bf16[368,256]{1,0:T(8,128)(2,1)} %get-tuple-element.36), channel_id=1, source_target_pairs={{0,128},{8,136},{16,144},{24,152},{32,160},{40,168},{48,176},{56,1... | collective-permute-start | bytes 565256 | tf_op jit(solution)/shard_map/ppermute | solution.py:495
  131.6 8.8 %collective-permute-start.17 = (bf16[368,256]{1,0:T(8,128)(2,1)}, bf16[368,256]{1,0:T(8,128)(2,1)S(1)}, u32[]{:S(2)}, u32[]{:S(2)}) collective-permute-start(bf16[368,256]{1,0:T(8,128)(2,1)} %get-tuple-element.37), channel_id=1, source_target_pairs={{0,64},{8,72},{16,80},{24,88},{32,96},{40,104},{48,112},{56,120},{... | collective-permute-start | bytes 565256 | tf_op jit(solution)/shard_map/ppermute | solution.py:495
  145.4 8.0 %collective-permute-start.24 = (bf16[224,256]{1,0:T(8,128)(2,1)}, bf16[224,256]{1,0:T(8,128)(2,1)S(1)}, u32[]{:S(2)}, u32[]{:S(2)}) collective-permute-start(bf16[224,256]{1,0:T(8,128)(2,1)} %get-tuple-element.43), channel_id=1, source_target_pairs={{0,128},{8,136},{16,144},{24,152},{32,160},{40,168},{48,176},{56,1... | collective-permute-start | bytes 344072 | tf_op jit(solution)/shard_map/ppermute | solution.py:495
  149.8 12.1 %collective-permute-start.26 = (bf16[2,80,256]{2,1,0:T(8,128)(2,1)S(1)}, bf16[2,80,256]{2,1,0:T(8,128)(2,1)S(1)}, u32[]{:S(2)}, u32[]{:S(2)}) collective-permute-start(bf16[2,80,256]{2,1,0:T(8,128)(2,1)S(1)} %pad_maximum_fusion.1), channel_id=1, source_target_pairs={{0,56},{8,0},{16,8},{24,16},{32,24},{40,32},{48,40},{56,48},{64,12... | collective-permute-start | bytes 245768 | tf_op jit(solution)/shard_map/ppermute | solution.py:490
  153.4 8.5 %collective-permute-start.27 = (bf16[2,80,256]{2,1,0:T(8,128)(2,1)S(1)}, bf16[2,80,256]{2,1,0:T(8,128)(2,1)S(1)}, u32[]{:S(2)}, u32[]{:S(2)}) collective-permute-start(bf16[2,80,256]{2,1,0:T(8,128)(2,1)S(1)} %pad_maximum_fusion.2), channel_id=1, source_target_pairs={{0,8},{8,16},{16,24},{24,32},{32,40},{40,48},{48,56},{56,0},{64,72... | collective-permute-start | bytes 245768 | tf_op jit(solution)/shard_map/ppermute | solution.py:490
  (28 other events, 155.9 us)

commit v6 on v5

--- a/solution.py
+++ b/solution.py
@@ -260,7 +260,7 @@
         + [pl.BlockSpec(memory_space=pl.ANY)] * len(earlier),
         out_specs=pl.BlockSpec((NX, FAR_ROWS, 128), lambda i: (0, 0, 0)),
         scratch_shapes=[pltpu.VMEM((NX, FAR_ROWS, 128), F32)],
-        compiler_params=params("arbitrary"),
+        compiler_params=params("arbitrary", limit=16 * MIB),
         cost_estimate=cost(COST["shrink_far"]),
         name="shrink_far",
     )(*xs, *panels, *earlier)
@@ -284,7 +284,7 @@
         + [pl.BlockSpec((LOCAL, width, 128), lambda i: (0, 0, 0)) for w in panels]
         + [pl.BlockSpec(memory_space=pl.ANY)],
         out_specs=pl.BlockSpec((NX, LATE_ROWS, 128), lambda i: (0, 0, 0)),
-        compiler_params=params("arbitrary"),
+        compiler_params=params("arbitrary", limit=16 * MIB),
         cost_estimate=cost(COST["shrink_late"]),
         name="shrink_late",
     )(far, *guests, *panels, earlier)
@@ -341,7 +341,7 @@
             pltpu.VMEM((NX, NEAR_ROWS, 256), F32),
             pltpu.VMEM((NX, NEAR_ROWS, 128), BF16),
         ],
-        compiler_params=params("arbitrary"),
+        compiler_params=params("arbitrary", limit=24 * MIB),
         cost_estimate=cost(COST["expand_near"]),
         name="expand_near",
     )(place, mine, other, *panels)
@@ -384,7 +384,7 @@
             pltpu.VMEM((LOCAL * 128, 256), BF16),
             pltpu.VMEM((NX, LATE_ROWS, 256), F32),
         ],
-        compiler_params=params("arbitrary"),
+        compiler_params=params("arbitrary", limit=24 * MIB),
         cost_estimate=cost(COST["expand_late"]),
         name="expand_late",
     )(mine, other, *panels, *earlier)
@@ -543,12 +543,11 @@
     keep, send = shrink_near(place, xs, held, upward)
     near_chip = add(keep, with_core(send))
     near_pair = add(near_chip, with_even(near_chip))
-    near_pair, cw3, ccw3 = lax.optimization_barrier((near_pair, cw3, ccw3))
     near_sum = add(near_pair, with_odd(near_pair))
     near = home(expand_near(place, near_sum, with_core(near_sum), held))
 
-    late = shrink_far(xs, [cw3, ccw3], near_pair, parts)
-    late = shrink_late(late, guests, [cw3, ccw3], near_sum)
+    late = shrink_far(xs, [cw3, ccw3], near_chip, parts)
+    late = shrink_late(late, guests, [cw3, ccw3], near_pair)
     late = add(late, with_core(late))
     late = add(late, with_even(late))
     total = gather(col, parts, near)

time: 166 us -> 153 us (0.922)
  local copies, waits for them, and re-layouts: 10.4 us -> 5.33 us
  other arithmetic: 5.92 us -> 2.25 us
  Pallas kernels: 51.4 us -> 49 us
  starting transfers between devices: 39.8 us -> 37.9 us
    ppermute x2, waiting for transfers between devices: 9.24 us -> 4.41 us  [with_even(): return lax.ppermute(array, 'tp', [(i, i ^ 2) for i in range(2 * NY)])]
    ppermute x2, waiting for transfers between devices: 0.35 us -> 4.91 us  [with_odd(): return lax.ppermute(array, 'tp', pairs)]
    unnamed x46 -> x34, local copies, waits for them, and re-layouts: 9.63 us -> 5.31 us
    convert_element_type x5, other arithmetic: 2.84 us -> 0.28 us  [add(): return (a.astype(F32) + b.astype(F32)).astype(BF16)]
    ppermute x5, waiting for transfers between devices: 3.12 us -> 1.43 us  [with_core(): return lax.ppermute(array, 'tp', [(i, i ^ 1) for i in range(2 * NY)])]
  transfers between devices with their start and end apart: 29 -> 29, of which waited for: 16 -> 16; matrix products, arithmetic and copies ran while one was open for 3% -> 1% of each run, Pallas kernels for 26% -> 28%
where the time goes in v6:
time: 153 us; the launch traced here: 152 us
  waiting for transfers between devices  57.5 us (38%)
  Pallas kernels  49 us (32%)
  starting transfers between devices  37.9 us (25%)
  local copies, waits for them, and re-layouts  5.33 us (3%)
  other arithmetic  2.25 us (1%)
    ppermute x10, waiting for transfers between devices, along_z(): return lax.ppermute(array, 'ad', pairs)  24.1 us
    ppermute x9, waiting for transfers between devices, along_x(): return lax.ppermute(array, 'ad', pairs)  22.7 us
    ppermute x10, starting transfers between devices, along_z(): return lax.ppermute(array, 'ad', pairs)  14.5 us
    pallas_call x1, Pallas kernels, base(): pl.pallas_call(base_kernel, grid_spec=pltpu.PrefetchScalarGridSpec(num_sc...  12.1 us
    ppermute x9, starting transfers between devices, along_x(): return lax.ppermute(array, 'ad', pairs)  11.3 us
    pallas_call x4, Pallas kernels, pack(): pl.pallas_call(functools.partial(pack_kernel, e), out_shape=jax.ShapeDtyp...  11.3 us
    unnamed x34, local copies, waits for them, and re-layouts  5.31 us
    pallas_call x1, Pallas kernels, gather(): pl.pallas_call(gather_kernel, grid=(count // step,), out_shape=jax.ShapeD...  5.23 us
  transfers between devices with their start and end apart: 29, of which 16 were waited for; matrix products, arithmetic and copies ran while one was open for 1% of the time, Pallas kernels for 28%

profile of v6, /device:TPU:64, one launch (start us, length us, event | category | flops | bytes accessed | tf_op | source)
XLA Modules:
  0.0 152.4 jit_solution(9464750931120622711)
XLA Ops:
  4.6 2.8 %route.1 = (s32[1,1536]{1,0:T(1,128)}, s32[1536,128]{1,0:T(8,128)}) custom-call(s32[3]{0:T(128)} %pad_add_fusion.place_ref, s32[1,1536]{1,0:T(1,128)} %bitcast.16, s32[1,128]{1,0:T(1,128)} %bitcast.17), custom_call_target="tpu_custom_call" | custom-call | flops 3300000000 | bytes 1000 | tf_op jit(solution)/shard_map/route/pallas_call | solution.py:95
  8.1 3.1 %pack.4.refs_0_ = bf16[592,1024]{1,0:T(8,128)(2,1)} custom-call(s32[1,1536]{1,0:T(1,128)S(1)} %copy-done.15, bf16[1536,1024]{1,0:T(8,128)(2,1)S(1)} %copy-done.7), custom_call_target="tpu_custom_call" | custom-call | flops 3300000000 | bytes 1000 | tf_op jit(solution)/shard_map/pack/pallas_call | solution.py:118
  12.6 3.1 %pack.5.refs_1_ = bf16[592,1024]{1,0:T(8,128)(2,1)} custom-call(s32[1,1536]{1,0:T(1,128)S(1)} %copy-done.15, bf16[1536,1024]{1,0:T(8,128)(2,1)S(1)} %copy-done.7), custom_call_target="tpu_custom_call" | custom-call | flops 3300000000 | bytes 1000 | tf_op jit(solution)/shard_map/pack/pallas_call | solution.py:118
  15.7 3.1 %pack.6.refs_2_ = bf16[592,1024]{1,0:T(8,128)(2,1)} custom-call(s32[1,1536]{1,0:T(1,128)S(1)} %copy-done.15, bf16[1536,1024]{1,0:T(8,128)(2,1)S(1)} %copy-done.7), custom_call_target="tpu_custom_call" | custom-call | flops 3300000000 | bytes 1000 | tf_op jit(solution)/shard_map/pack/pallas_call | solution.py:118
  18.8 2.7 %collective-permute-start.5 = (bf16[592,1024]{1,0:T(8,128)(2,1)}, bf16[592,1024]{1,0:T(8,128)(2,1)}, u32[]{:S(2)}, u32[]{:S(2)}) collective-permute-start(bf16[592,1024]{1,0:T(8,128)(2,1)} %pack.6.refs_2_), channel_id=1, source_target_pairs={{0,128},{8,136},{16,144},{24,152},{32,160},{40,168},{48,176},{56,1... | collective-permute-start | bytes 3637256 | tf_op jit(solution)/shard_map/ppermute | solution.py:495
  23.0 12.1 %base.1 = bf16[4,1536,256]{2,1,0:T(8,128)(2,1)} custom-call(s32[3]{0:T(128)} %pad_add_fusion.place_ref, bf16[1536,1024]{1,0:T(8,128)(2,1)} %tok_ref.9, bf16[2,1024,1024]{2,1,0:T(8,128)(2,1)} %w_ref.1, bf16[1536,1024]{1,0:T(8,128)(2,1)} %collective-permute-done.2.other_tok_ref, bf16[2,1024,1024]{2,1,0:T(8,128)(2,1)} %collective-permute-done.3.other_w_ref, ...), custom_call_target="tpu_custom_call" | custom-call | flops 12099999744 | bytes 1000 | tf_op jit(solution)/shard_map/base/pallas_call | solution.py:141
  35.1 3.1 %collective-permute-start.7 = (bf16[4,1152,128]{2,1,0:T(8,128)(2,1)}, bf16[4,1152,128]{2,1,0:T(8,128)(2,1)}, u32[]{:S(2)}, u32[]{:S(2)}) collective-permute-start(bf16[4,1152,128]{2,1,0:T(8,128)(2,1)} %collective-permute-done.refs_5_.refs_1_), channel_id=1, source_target_pairs={{0,8},{8,16},{16,24},{24,32},{32,40},{40,48},{48,56},{56,0},{64,72... | collective-permute-start | bytes 3538952 | tf_op jit(solution)/shard_map/ppermute | solution.py:490
  38.2 4.5 %all-to-all-start = ((bf16[4,1536,256]{2,1,0:T(8,128)(2,1)}), bf16[4,1536,256]{2,1,0:T(8,128)(2,1)S(1)}, u32[]{:S(2)}, u32[]{:S(2)}) async-start(bf16[4,1536,256]{2,1,0:T(8,128)(2,1)} %base.1), calls=%async_computation | async-start | bytes 6291456 | tf_op jit(solution)/shard_map/all_to_all | solution.py:535
  46.7 16.2 %collective-permute-done.7.refs_7_.refs_3_ = bf16[4,1152,128]{2,1,0:T(8,128)(2,1)} collective-permute-done((bf16[4,1152,128]{2,1,0:T(8,128)(2,1)}, bf16[4,1152,128]{2,1,0:T(8,128)(2,1)}, u32[]{:S(2)}, u32[]{:S(2)}) %collective-permute-start.7) | collective-permute-done | bytes 1179680 | tf_op jit(solution)/shard_map/ppermute | solution.py:490
  62.8 3.0 %collective-permute-start.16 = (bf16[4,1152,128]{2,1,0:T(8,128)(2,1)}, bf16[4,1152,128]{2,1,0:T(8,128)(2,1)}, u32[]{:S(2)}, u32[]{:S(2)}) collective-permute-start(bf16[4,1152,128]{2,1,0:T(8,128)(2,1)} %collective-permute-done.7.refs_7_.refs_3_), channel_id=1, source_target_pairs={{0,8},{8,16},{16,24},{24,32},{32,40},{40,48},{48,56},{56,0},{64,72... | collective-permute-start | bytes 3538952 | tf_op jit(solution)/shard_map/ppermute | solution.py:490
  67.8 5.8 %collective-permute-done.6.refs_3_ = bf16[592,1024]{1,0:T(8,128)(2,1)} collective-permute-done((bf16[592,1024]{1,0:T(8,128)(2,1)}, bf16[592,1024]{1,0:T(8,128)(2,1)}, u32[]{:S(2)}, u32[]{:S(2)}) %collective-permute-start.6) | collective-permute-done | bytes 1212448 | tf_op jit(solution)/shard_map/ppermute | solution.py:495
  75.6 4.8 %shrink_near.1 = (bf16[2,368,128]{2,1,0:T(8,128)(2,1)S(1)}, bf16[2,368,128]{2,1,0:T(8,128)(2,1)S(1)}) custom-call(s32[3]{0:T(128)S(1)} %copy-done.6, bf16[592,1024]{1,0:T(8,128)(2,1)S(1)} %pack.7.refs_0_, bf16[592,1024]{1,0:T(8,128)(2,1)} %collective-permute-done.4.refs_1_, bf16[592,1024]{1,0:T(8,128)(2,1)} %collective-permute-done.5.refs_2_, ...), custom_call_target="tpu_custom_call" | custom-call | flops 3300000000 | bytes 1000 | tf_op jit(solution)/shard_map/shrink_near/pallas_call | solution.py:203
  83.6 3.1 %collective-permute-start.18 = (bf16[2,80,1024]{2,1,0:T(8,128)(2,1)}, bf16[2,80,1024]{2,1,0:T(8,128)(2,1)}, u32[]{:S(2)}, u32[]{:S(2)}) collective-permute-start(bf16[2,80,1024]{2,1,0:T(8,128)(2,1)} %get-tuple-element.27.refs_9_), channel_id=1, source_target_pairs={{0,8},{8,16},{16,24},{24,32},{32,40},{40,48},{48,56},{56,0},{64,72... | collective-permute-start | bytes 983048 | tf_op jit(solution)/shard_map/ppermute | solution.py:490
  88.9 3.2 %collective-permute-done.16.refs_4_.low_ref.refs_0_ = bf16[4,1152,128]{2,1,0:T(8,128)(2,1)} collective-permute-done((bf16[4,1152,128]{2,1,0:T(8,128)(2,1)}, bf16[4,1152,128]{2,1,0:T(8,128)(2,1)}, u32[]{:S(2)}, u32[]{:S(2)}) %collective-permute-start.16) | collective-permute-done | bytes 1179680 | tf_op jit(solution)/shard_map/ppermute | solution.py:490
  92.1 4.1 %collective-permute-done.17.refs_5_.high_ref.refs_1_ = bf16[4,1152,128]{2,1,0:T(8,128)(2,1)} collective-permute-done((bf16[4,1152,128]{2,1,0:T(8,128)(2,1)}, bf16[4,1152,128]{2,1,0:T(8,128)(2,1)}, u32[]{:S(2)}, u32[]{:S(2)}) %collective-permute-start.17) | collective-permute-done | bytes 1179680 | tf_op jit(solution)/shard_map/ppermute | solution.py:490
  97.4 2.7 %shrink_far.1.far_ref = bf16[4,144,128]{2,1,0:T(8,128)(2,1)S(1)} custom-call(bf16[592,1024]{1,0:T(8,128)(2,1)S(1)} %copy-done.2, bf16[592,1024]{1,0:T(8,128)(2,1)} %collective-permute-done.4.refs_1_, bf16[592,1024]{1,0:T(8,128)(2,1)} %collective-permute-done.5.refs_2_, bf16[592,1024]{1,0:T(8,128)(2,1)} %collective-permute-done.6.refs_3_, ...), custom_call_target="tpu_custom_call" | custom-call | flops 109999996928 | bytes 1000 | tf_op jit(solution)/shard_map/shrink_far/pallas_call | solution.py:251
  102.7 3.6 %collective-permute-start.11 = (bf16[2,368,128]{2,1,0:T(8,128)(2,1)S(1)}, bf16[2,368,128]{2,1,0:T(8,128)(2,1)S(1)}, u32[]{:S(2)}, u32[]{:S(2)}) collective-permute-start(bf16[2,368,128]{2,1,0:T(8,128)(2,1)S(1)} %add_convert_fusion.3._), channel_id=1, source_target_pairs={{0,6},{1,7},{2,4},{3,5},{4,2},{5,3},{6,0},{7,1},{8,14},{9,15},{10,... | collective-permute-start | bytes 565256 | tf_op jit(solution)/shard_map/ppermute | solution.py:508
  106.5 4.9 %collective-permute-done.11 = bf16[2,368,128]{2,1,0:T(8,128)(2,1)S(1)} collective-permute-done((bf16[2,368,128]{2,1,0:T(8,128)(2,1)S(1)}, bf16[2,368,128]{2,1,0:T(8,128)(2,1)S(1)}, u32[]{:S(2)}, u32[]{:S(2)}) %collective-permute-start.11) | collective-permute-done | bytes 188448 | tf_op jit(solution)/shard_map/ppermute | solution.py:508
  119.7 5.3 %collective-permute-done.13.refs_1_.refs_2_ = bf16[368,256]{1,0:T(8,128)(2,1)S(1)} collective-permute-done((bf16[368,256]{1,0:T(8,128)(2,1)S(1)}, bf16[368,256]{1,0:T(8,128)(2,1)S(1)}, u32[]{:S(2)}, u32[]{:S(2)}) %collective-permute-start.13) | collective-permute-done | bytes 188448 | tf_op jit(solution)/shard_map/ppermute | solution.py:495
  134.0 2.6 %collective-permute-done.23.refs_1_ = bf16[224,256]{1,0:T(8,128)(2,1)S(1)} collective-permute-done((bf16[224,256]{1,0:T(8,128)(2,1)S(1)}, bf16[224,256]{1,0:T(8,128)(2,1)S(1)}, u32[]{:S(2)}, u32[]{:S(2)}) %collective-permute-start.23) | collective-permute-done | bytes 114720 | tf_op jit(solution)/shard_map/ppermute | solution.py:495
  136.6 3.4 %collective-permute-done.25.refs_3_ = bf16[224,256]{1,0:T(8,128)(2,1)S(1)} collective-permute-done((bf16[224,256]{1,0:T(8,128)(2,1)S(1)}, bf16[224,256]{1,0:T(8,128)(2,1)S(1)}, u32[]{:S(2)}, u32[]{:S(2)}) %collective-permute-start.25) | collective-permute-done | bytes 114720 | tf_op jit(solution)/shard_map/ppermute | solution.py:495
  140.0 3.1 %collective-permute-start.27 = (bf16[2,80,256]{2,1,0:T(8,128)(2,1)S(1)}, bf16[2,80,256]{2,1,0:T(8,128)(2,1)S(1)}, u32[]{:S(2)}, u32[]{:S(2)}) collective-permute-start(bf16[2,80,256]{2,1,0:T(8,128)(2,1)S(1)} %pad_maximum_fusion.2), channel_id=1, source_target_pairs={{0,8},{8,16},{16,24},{24,32},{32,40},{40,48},{48,56},{56,0},{64,72... | collective-permute-start | bytes 245768 | tf_op jit(solution)/shard_map/ppermute | solution.py:490
  143.1 5.2 %gather.1.total_ref = f32[1536,256]{1,0:T(8,128)} custom-call(s32[1536,128]{1,0:T(8,128)} %get-tuple-element.22.col_ref, bf16[4,1536,256]{2,1,0:T(8,128)(2,1)} %copy-done, bf16[368,256]{1,0:T(8,128)(2,1)} %copy-done.13, bf16[368,256]{1,0:T(8,128)(2,1)} %copy-done.9, bf16[368,256]{1,0:T(8,128)(2,1)} %copy-done.10, bf16[368,256]{1,0:T(8,128)(2,1)} %copy-done.11), custom_call_target="tpu_custom_call" | custom-call | flops 5500000256 | bytes 1000 | tf_op jit(solution)/shard_map/gather/pallas_call | solution.py:420
  149.8 2.6 %finish.1 = bf16[3072,128]{1,0:T(8,128)(2,1)} custom-call(s32[1536,128]{1,0:T(8,128)S(1)} %copy-done.14, f32[1536,256]{1,0:T(8,128)S(1)} %copy-done.12, bf16[224,256]{1,0:T(8,128)(2,1)S(1)} %get-tuple-element.35.refs_0_, bf16[224,256]{1,0:T(8,128)(2,1)S(1)} %collective-permute-done.23.refs_1_, bf16[224,256]{1,0:T(8,128)(2,1)S(1)} %collective-permute-done.24.refs_2_, ...), custom_call_target="tpu_custom_call" | custom-call | flops 5500000256 | bytes 1000 | tf_op jit(solution)/shard_map/finish/pallas_call | solution.py:467
  (95 shorter events, 44.2 us)
Async XLA Ops:
  0.0 21.5 %collective-permute-start.3 = (bf16[2,1024,1024]{2,1,0:T(8,128)(2,1)}, bf16[2,1024,1024]{2,1,0:T(8,128)(2,1)}, u32[]{:S(2)}, u32[]{:S(2)}) collective-permute-start(bf16[2,1024,1024]{2,1,0:T(8,128)(2,1)} %w_ref.1), channel_id=1, source_target_pairs={{0,1},{1,0},{2,3},{3,2},{4,5},{5,4},{6,7},{7,6},{8,9},{9,8},{10,11... | collective-permute-start | bytes 12582920 | tf_op jit(solution)/shard_map/ppermute | solution.py:499
  0.0 18.8 %collective-permute-start.2 = (bf16[1536,1024]{1,0:T(8,128)(2,1)}, bf16[1536,1024]{1,0:T(8,128)(2,1)}, u32[]{:S(2)}, u32[]{:S(2)}) collective-permute-start(bf16[1536,1024]{1,0:T(8,128)(2,1)} %tok_ref.9), channel_id=1, source_target_pairs={{0,1},{1,0},{2,3},{3,2},{4,5},{5,4},{6,7},{7,6},{8,9},{9,8},{10,11... | collective-permute-start | bytes 9437192 | tf_op jit(solution)/shard_map/ppermute | solution.py:499
  1.9 33.2 %collective-permute-start = (bf16[4,1152,128]{2,1,0:T(8,128)(2,1)S(1)}, bf16[4,1152,128]{2,1,0:T(8,128)(2,1)}, u32[]{:S(2)}, u32[]{:S(2)}) collective-permute-start(bf16[4,1152,128]{2,1,0:T(8,128)(2,1)S(1)} %pad_maximum_fusion.refs_4_.refs_0_), channel_id=1, source_target_pairs={{0,8},{8,16},{16,24},{24,32},{32,40},{40,48},{48,56},{56,0},{64,72... | collective-permute-start | bytes 3538952 | tf_op jit(solution)/shard_map/ppermute | solution.py:490
  3.9 31.2 %collective-permute-start.1 = (bf16[4,1152,128]{2,1,0:T(8,128)(2,1)S(1)}, bf16[4,1152,128]{2,1,0:T(8,128)(2,1)}, u32[]{:S(2)}, u32[]{:S(2)}) collective-permute-start(bf16[4,1152,128]{2,1,0:T(8,128)(2,1)S(1)} %pad_maximum_fusion.refs_4_.refs_0_), channel_id=1, source_target_pairs={{0,56},{8,0},{16,8},{24,16},{32,24},{40,32},{48,40},{56,48},{64,12... | collective-permute-start | bytes 3538952 | tf_op jit(solution)/shard_map/ppermute | solution.py:490
  11.1 55.1 %collective-permute-start.4 = (bf16[592,1024]{1,0:T(8,128)(2,1)}, bf16[592,1024]{1,0:T(8,128)(2,1)}, u32[]{:S(2)}, u32[]{:S(2)}) collective-permute-start(bf16[592,1024]{1,0:T(8,128)(2,1)} %pack.4.refs_0_), channel_id=1, source_target_pairs={{0,64},{8,72},{16,80},{24,88},{32,96},{40,104},{48,112},{56,120},{... | collective-permute-start | bytes 3637256 | tf_op jit(solution)/shard_map/ppermute | solution.py:495
  18.8 49.0 %collective-permute-start.5 = (bf16[592,1024]{1,0:T(8,128)(2,1)}, bf16[592,1024]{1,0:T(8,128)(2,1)}, u32[]{:S(2)}, u32[]{:S(2)}) collective-permute-start(bf16[592,1024]{1,0:T(8,128)(2,1)} %pack.6.refs_2_), channel_id=1, source_target_pairs={{0,128},{8,136},{16,144},{24,152},{32,160},{40,168},{48,176},{56,1... | collective-permute-start | bytes 3637256 | tf_op jit(solution)/shard_map/ppermute | solution.py:495
  21.5 52.1 %collective-permute-start.6 = (bf16[592,1024]{1,0:T(8,128)(2,1)}, bf16[592,1024]{1,0:T(8,128)(2,1)}, u32[]{:S(2)}, u32[]{:S(2)}) collective-permute-start(bf16[592,1024]{1,0:T(8,128)(2,1)} %pack.5.refs_1_), channel_id=1, source_target_pairs={{0,192},{8,200},{16,208},{24,216},{32,224},{40,232},{48,240},{56,2... | collective-permute-start | bytes 3637256 | tf_op jit(solution)/shard_map/ppermute | solution.py:495
  35.1 27.7 %collective-permute-start.7 = (bf16[4,1152,128]{2,1,0:T(8,128)(2,1)}, bf16[4,1152,128]{2,1,0:T(8,128)(2,1)}, u32[]{:S(2)}, u32[]{:S(2)}) collective-permute-start(bf16[4,1152,128]{2,1,0:T(8,128)(2,1)} %collective-permute-done.refs_5_.refs_1_), channel_id=1, source_target_pairs={{0,8},{8,16},{16,24},{24,32},{32,40},{40,48},{48,56},{56,0},{64,72... | collective-permute-start | bytes 3538952 | tf_op jit(solution)/shard_map/ppermute | solution.py:490
  38.2 28.0 %collective-permute-start.8 = (bf16[4,1152,128]{2,1,0:T(8,128)(2,1)}, bf16[4,1152,128]{2,1,0:T(8,128)(2,1)}, u32[]{:S(2)}, u32[]{:S(2)}) collective-permute-start(bf16[4,1152,128]{2,1,0:T(8,128)(2,1)} %collective-permute-done.1.refs_6_.refs_2_), channel_id=1, source_target_pairs={{0,56},{8,0},{16,8},{24,16},{32,24},{40,32},{48,40},{56,48},{64,12... | collective-permute-start | bytes 3538952 | tf_op jit(solution)/shard_map/ppermute | solution.py:490
  38.2 50.6 %all-to-all-start = ((bf16[4,1536,256]{2,1,0:T(8,128)(2,1)}), bf16[4,1536,256]{2,1,0:T(8,128)(2,1)S(1)}, u32[]{:S(2)}, u32[]{:S(2)}) async-start(bf16[4,1536,256]{2,1,0:T(8,128)(2,1)} %base.1), calls=%async_computation | async-start | bytes 6291456 | tf_op jit(solution)/shard_map/all_to_all | solution.py:535
  62.8 29.2 %collective-permute-start.16 = (bf16[4,1152,128]{2,1,0:T(8,128)(2,1)}, bf16[4,1152,128]{2,1,0:T(8,128)(2,1)}, u32[]{:S(2)}, u32[]{:S(2)}) collective-permute-start(bf16[4,1152,128]{2,1,0:T(8,128)(2,1)} %collective-permute-done.7.refs_7_.refs_3_), channel_id=1, source_target_pairs={{0,8},{8,16},{16,24},{24,32},{32,40},{40,48},{48,56},{56,0},{64,72... | collective-permute-start | bytes 3538952 | tf_op jit(solution)/shard_map/ppermute | solution.py:490
  66.2 29.9 %collective-permute-start.17 = (bf16[4,1152,128]{2,1,0:T(8,128)(2,1)}, bf16[4,1152,128]{2,1,0:T(8,128)(2,1)}, u32[]{:S(2)}, u32[]{:S(2)}) collective-permute-start(bf16[4,1152,128]{2,1,0:T(8,128)(2,1)} %collective-permute-done.8.refs_8_.refs_4_), channel_id=1, source_target_pairs={{0,56},{8,0},{16,8},{24,16},{32,24},{40,32},{48,40},{56,48},{64,12... | collective-permute-start | bytes 3538952 | tf_op jit(solution)/shard_map/ppermute | solution.py:490
  82.0 6.9 %collective-permute-start.10 = (bf16[2,368,128]{2,1,0:T(8,128)(2,1)S(1)}, bf16[2,368,128]{2,1,0:T(8,128)(2,1)S(1)}, u32[]{:S(2)}, u32[]{:S(2)}) collective-permute-start(bf16[2,368,128]{2,1,0:T(8,128)(2,1)S(1)} %add_convert_fusion.4.refs_6_), channel_id=1, source_target_pairs={{0,2},{1,3},{2,0},{3,1},{4,6},{5,7},{6,4},{7,5},{8,10},{9,11},{10,... | collective-permute-start | bytes 565256 | tf_op jit(solution)/shard_map/ppermute | solution.py:503
  83.6 16.4 %collective-permute-start.18 = (bf16[2,80,1024]{2,1,0:T(8,128)(2,1)}, bf16[2,80,1024]{2,1,0:T(8,128)(2,1)}, u32[]{:S(2)}, u32[]{:S(2)}) collective-permute-start(bf16[2,80,1024]{2,1,0:T(8,128)(2,1)} %get-tuple-element.27.refs_9_), channel_id=1, source_target_pairs={{0,8},{8,16},{16,24},{24,32},{32,40},{40,48},{48,56},{56,0},{64,72... | collective-permute-start | bytes 983048 | tf_op jit(solution)/shard_map/ppermute | solution.py:490
  86.8 13.6 %collective-permute-start.19 = (bf16[2,80,1024]{2,1,0:T(8,128)(2,1)}, bf16[2,80,1024]{2,1,0:T(8,128)(2,1)}, u32[]{:S(2)}, u32[]{:S(2)}) collective-permute-start(bf16[2,80,1024]{2,1,0:T(8,128)(2,1)} %get-tuple-element.34), channel_id=1, source_target_pairs={{0,56},{8,0},{16,8},{24,16},{32,24},{40,32},{48,40},{56,48},{64,12... | collective-permute-start | bytes 983048 | tf_op jit(solution)/shard_map/ppermute | solution.py:490
  102.7 8.7 %collective-permute-start.11 = (bf16[2,368,128]{2,1,0:T(8,128)(2,1)S(1)}, bf16[2,368,128]{2,1,0:T(8,128)(2,1)S(1)}, u32[]{:S(2)}, u32[]{:S(2)}) collective-permute-start(bf16[2,368,128]{2,1,0:T(8,128)(2,1)S(1)} %add_convert_fusion.3._), channel_id=1, source_target_pairs={{0,6},{1,7},{2,4},{3,5},{4,2},{5,3},{6,0},{7,1},{8,14},{9,15},{10,... | collective-permute-start | bytes 565256 | tf_op jit(solution)/shard_map/ppermute | solution.py:508
  106.4 7.5 %collective-permute-start.21 = (bf16[4,224,128]{2,1,0:T(8,128)(2,1)S(1)}, bf16[4,224,128]{2,1,0:T(8,128)(2,1)S(1)}, u32[]{:S(2)}, u32[]{:S(2)}) collective-permute-start(bf16[4,224,128]{2,1,0:T(8,128)(2,1)S(1)} %add_convert_fusion.1), channel_id=1, source_target_pairs={{0,2},{1,3},{2,0},{3,1},{4,6},{5,7},{6,4},{7,5},{8,10},{9,11},{10,... | collective-permute-start | bytes 688136 | tf_op jit(solution)/shard_map/ppermute | solution.py:503
  114.0 15.1 %collective-permute-start.22 = (bf16[4,224,128]{2,1,0:T(8,128)(2,1)S(1)}, bf16[4,224,128]{2,1,0:T(8,128)(2,1)S(1)}, u32[]{:S(2)}, u32[]{:S(2)}) collective-permute-start(bf16[4,224,128]{2,1,0:T(8,128)(2,1)S(1)} %add_convert_fusion.mine_ref), channel_id=1, source_target_pairs={{0,6},{1,7},{2,4},{3,5},{4,2},{5,3},{6,0},{7,1},{8,14},{9,15},{10,... | collective-permute-start | bytes 688136 | tf_op jit(solution)/shard_map/ppermute | solution.py:508
  117.3 7.7 %collective-permute-start.13 = (bf16[368,256]{1,0:T(8,128)(2,1)S(1)}, bf16[368,256]{1,0:T(8,128)(2,1)S(1)}, u32[]{:S(2)}, u32[]{:S(2)}) collective-permute-start(bf16[368,256]{1,0:T(8,128)(2,1)S(1)} %get-tuple-element.31), channel_id=1, source_target_pairs={{0,192},{8,200},{16,208},{24,216},{32,224},{40,232},{48,240},{56,2... | collective-permute-start | bytes 565256 | tf_op jit(solution)/shard_map/ppermute | solution.py:495
  117.6 9.2 %collective-permute-start.14 = (bf16[368,256]{1,0:T(8,128)(2,1)S(1)}, bf16[368,256]{1,0:T(8,128)(2,1)S(1)}, u32[]{:S(2)}, u32[]{:S(2)}) collective-permute-start(bf16[368,256]{1,0:T(8,128)(2,1)S(1)} %get-tuple-element.32), channel_id=1, source_target_pairs={{0,128},{8,136},{16,144},{24,152},{32,160},{40,168},{48,176},{56,1... | collective-permute-start | bytes 565256 | tf_op jit(solution)/shard_map/ppermute | solution.py:495
  119.7 9.4 %collective-permute-start.15 = (bf16[368,256]{1,0:T(8,128)(2,1)S(1)}, bf16[368,256]{1,0:T(8,128)(2,1)S(1)}, u32[]{:S(2)}, u32[]{:S(2)}) collective-permute-start(bf16[368,256]{1,0:T(8,128)(2,1)S(1)} %get-tuple-element.33), channel_id=1, source_target_pairs={{0,64},{8,72},{16,80},{24,88},{32,96},{40,104},{48,112},{56,120},{... | collective-permute-start | bytes 565256 | tf_op jit(solution)/shard_map/ppermute | solution.py:495
  131.9 8.1 %collective-permute-start.24 = (bf16[224,256]{1,0:T(8,128)(2,1)S(1)}, bf16[224,256]{1,0:T(8,128)(2,1)S(1)}, u32[]{:S(2)}, u32[]{:S(2)}) collective-permute-start(bf16[224,256]{1,0:T(8,128)(2,1)S(1)} %get-tuple-element.37), channel_id=1, source_target_pairs={{0,128},{8,136},{16,144},{24,152},{32,160},{40,168},{48,176},{56,1... | collective-permute-start | bytes 344072 | tf_op jit(solution)/shard_map/ppermute | solution.py:495
  136.5 11.8 %collective-permute-start.26 = (bf16[2,80,256]{2,1,0:T(8,128)(2,1)S(1)}, bf16[2,80,256]{2,1,0:T(8,128)(2,1)S(1)}, u32[]{:S(2)}, u32[]{:S(2)}) collective-permute-start(bf16[2,80,256]{2,1,0:T(8,128)(2,1)S(1)} %pad_maximum_fusion.1), channel_id=1, source_target_pairs={{0,56},{8,0},{16,8},{24,16},{32,24},{40,32},{48,40},{56,48},{64,12... | collective-permute-start | bytes 245768 | tf_op jit(solution)/shard_map/ppermute | solution.py:490
  140.0 8.3 %collective-permute-start.27 = (bf16[2,80,256]{2,1,0:T(8,128)(2,1)S(1)}, bf16[2,80,256]{2,1,0:T(8,128)(2,1)S(1)}, u32[]{:S(2)}, u32[]{:S(2)}) collective-permute-start(bf16[2,80,256]{2,1,0:T(8,128)(2,1)S(1)} %pad_maximum_fusion.2), channel_id=1, source_target_pairs={{0,8},{8,16},{16,24},{24,32},{32,40},{40,48},{48,56},{56,0},{64,72... | collective-permute-start | bytes 245768 | tf_op jit(solution)/shard_map/ppermute | solution.py:490
  (22 other events, 183.4 us)
